TPU v7x, 512 devices: a whole 4x4x16 slice. The times are simulated.
512 devices in a mesh: space: 128 (over y, z, core), replicas: 4 (over x).
Axes of the slice: x: 4, y: 4, z: 16, core: 2. Of those that a mesh axis runs over, the one named last changes fastest.
Arguments:
- latents: bfloat16 [4, 32768, 128], P('replicas', 'space'), may hold values from -6 to 6
- pairs: int32 [4, 2, 131072], P('replicas', None, 'space'), may hold values from 0 to 319, as said below
- geometry: bfloat16 [4, 4, 131072], P('replicas', None, 'space'), may hold values from -6 to 6
- pair_count: int32 [4, 128], P('replicas', 'space'), may hold values from 256 to 1024, as said below
- cotangent: bfloat16 [4, 32768, 128], P('replicas', 'space'), may hold values from -6 to 6
- leaving: int32 [4, 256, 16], P('replicas', 'space'), may hold values from 0 to 255, as said below
- edge_in: bfloat16 [2, 260, 128], replicated, may hold values from -0.375 to 0.375
- edge_bias: float32 [2, 128], replicated, may hold values from -3 to 3
- edge_out: bfloat16 [2, 128, 128], replicated, may hold values from -0.5 to 0.5
- node_in: bfloat16 [2, 256, 128], replicated, may hold values from -0.375 to 0.375
- node_bias: float32 [2, 128], replicated, may hold values from -3 to 3
- node_out: bfloat16 [2, 128, 128], replicated, may hold values from -0.5 to 0.5
- gain: float32 [2, 128], replicated, may hold values from 0.1 to 1.9
Outputs:
- final_latents: bfloat16 [4, 32768, 128], P('replicas', 'space')
- grad_latents: float32 [4, 32768, 128], P('replicas', 'space')
- arrivals: bfloat16 [4, 256, 16, 128], P('replicas', 'space')
- grad_edge_in: float32 [2, 260, 128], replicated
- grad_edge_bias: float32 [2, 128], replicated
- grad_edge_out: float32 [2, 128, 128], replicated
- grad_node_in: float32 [2, 256, 128], replicated
- grad_node_bias: float32 [2, 128], replicated
- grad_node_out: float32 [2, 128, 128], replicated
- grad_gain: float32 [2, 128], replicated
Inputs may be any that keep to these rules, and one draw needn't show every extreme that they name: `pairs`: in each domain's slots, the first row holds an owned particle, 32 to 287, and the second row a partner within 32 rows of it, never itself. `pair_count`: at least 256 in every domain; in each replica some domain has all 1024 slots live. `leaving`: the entries of a row are distinct; particles moving down lie among the first 32 rows of their domain, those moving up among the last 32.
All inputs are finite; a program needn't handle non-finite values.
Results may differ from a plain program's by a relative error of at most 0.02.
Values may be sent and summed in bfloat16 or wider, within the bound.
No kernel may reach another device: no remote copies, remote signals or barrier semaphores. Data moves between devices by JAX's collectives and lax.ppermute only.
A program may use at most 64 MiB of HBM per device.

v0:
```python
import jax
import jax.numpy as jnp
from jax import lax
from jax.sharding import PartitionSpec as P

PAIR_BLOCK = 512
STEPS = 2
HALO = 32
EMAX = 1024


eps = 1e-05


def passed_along(array, axis, by):
    peers = lax.axis_size(axis)
    return lax.ppermute(array, axis, [(i, (i + by) % peers) for i in range(peers)])


def extended_2(array, sides, width):
    for axis, dim in sides:
        peers, length = (lax.axis_size(axis), array.shape[dim])
        up = [(i, (i + 1) % peers) for i in range(peers)]
        down = [(j, i) for i, j in up]
        last = lax.slice_in_dim(array, length - width, length, axis=dim)
        leading = lax.slice_in_dim(array, 0, width, axis=dim)
        before = lax.ppermute(last, axis, up)
        after = lax.ppermute(leading, axis, down)
        array = jnp.concatenate([before, array, after], axis=dim)
    return array


def silu_slope(value):
    sig = jax.nn.sigmoid(value)
    return sig * (1.0 + value * (1.0 - sig))


def edge_forward(
    rows_src, owned_rows, other_rows, features, live_slots, weight_in, bias_in, weight_out
):
    left_rows = jnp.take(rows_src, owned_rows, axis=0)
    right_rows = jnp.take(rows_src, other_rows, axis=0)
    x_fwd = jnp.concatenate([left_rows, right_rows, features], axis=1)
    x_rev = jnp.concatenate([right_rows, left_rows, -features], axis=1)
    pre_fwd = jnp.dot(x_fwd, weight_in, preferred_element_type=jnp.float32) + bias_in
    pre_rev = jnp.dot(x_rev, weight_in, preferred_element_type=jnp.float32) + bias_in
    diff = (jax.nn.silu(pre_fwd) - jax.nn.silu(pre_rev)).astype(jnp.bfloat16)
    message = jnp.dot(diff, weight_out, preferred_element_type=jnp.float32) * live_slots[:, None]
    return (message, (x_fwd, x_rev, pre_fwd, pre_rev, diff))


def edge_backward(dagg, owned_rows, other_rows, live_slots, kept, weight_in, weight_out):
    x_fwd, x_rev, pre_fwd, pre_rev, diff = kept
    width = dagg.shape[1]
    dmessage = (
        (jnp.take(dagg, owned_rows, axis=0) - jnp.take(dagg, other_rows, axis=0))
        * live_slots[:, None]
    ).astype(jnp.bfloat16)
    out_term = jnp.dot(diff.T, dmessage, preferred_element_type=jnp.float32)
    dd = jnp.dot(dmessage, weight_out.T, preferred_element_type=jnp.float32)
    dfwd = (dd * silu_slope(pre_fwd)).astype(jnp.bfloat16)
    drev = (-dd * silu_slope(pre_rev)).astype(jnp.bfloat16)
    in_term = jnp.dot(x_fwd.T, dfwd, preferred_element_type=jnp.float32) + jnp.dot(
        x_rev.T, drev, preferred_element_type=jnp.float32
    )
    bias_term = jnp.sum(dfwd.astype(jnp.float32) + drev.astype(jnp.float32), axis=0)
    leading = weight_in[: 2 * width]
    dx_fwd = jnp.dot(dfwd, leading.T, preferred_element_type=jnp.float32)
    dx_rev = jnp.dot(drev, leading.T, preferred_element_type=jnp.float32)
    d_owned = dx_fwd[:, :width] + dx_rev[:, width:]
    d_other = dx_fwd[:, width:] + dx_rev[:, :width]
    return (d_owned, d_other, (in_term, bias_term, out_term))


def node_forward(latent, agg, weight_in, bias_in, weight_out, gain_row):
    joined = jnp.concatenate([latent, agg.astype(jnp.bfloat16)], axis=1)
    node_pre = jnp.dot(joined, weight_in, preferred_element_type=jnp.float32) + bias_in
    hidden = jax.nn.silu(node_pre).astype(jnp.bfloat16)
    out = jnp.dot(hidden, weight_out, preferred_element_type=jnp.float32)
    centred = out - jnp.mean(out, axis=1, keepdims=True)
    inv_std = lax.rsqrt(jnp.mean(centred * centred, axis=1, keepdims=True) + eps)
    normed = centred * inv_std
    new_latent = (latent.astype(jnp.float32) + normed * gain_row).astype(jnp.bfloat16)
    return (new_latent, (joined, node_pre, hidden, normed, inv_std))


def node_backward(grad, kept, weight_in, weight_out, gain_row):
    joined, node_pre, hidden, normed, inv_std = kept
    width = grad.shape[1]
    gain_term = jnp.sum(grad * normed, axis=0)
    dnorm = grad * gain_row
    dout = (
        (
            dnorm
            - jnp.mean(dnorm, axis=1, keepdims=True)
            - normed * jnp.mean(dnorm * normed, axis=1, keepdims=True)
        )
        * inv_std
    ).astype(jnp.bfloat16)
    out_term = jnp.dot(hidden.T, dout, preferred_element_type=jnp.float32)
    dhidden = jnp.dot(dout, weight_out.T, preferred_element_type=jnp.float32)
    dpre = (dhidden * silu_slope(node_pre)).astype(jnp.bfloat16)
    in_term = jnp.dot(joined.T, dpre, preferred_element_type=jnp.float32)
    bias_term = jnp.sum(dpre.astype(jnp.float32), axis=0)
    dx = jnp.dot(dpre, weight_in.T, preferred_element_type=jnp.float32)
    return (grad + dx[:, :width], dx[:, width:], (in_term, bias_term, out_term, gain_term))


def fold_rims(extended):
    core = extended[HALO:-HALO]
    from_upper = passed_along(extended[:HALO], "space", -1)
    from_lower = passed_along(extended[-HALO:], "space", 1)
    core = core.at[core.shape[0] - HALO :].add(from_upper)
    return core.at[:HALO].add(from_lower)


def on_device(
    latents,
    pairs,
    geometry,
    pair_count,
    cotangent,
    leaving,
    edge_in,
    edge_bias,
    edge_out,
    node_in,
    node_bias,
    node_out,
    gain,
):
    latent = latents[0]
    owned_all = pairs[0, 0]
    other_all = pairs[0, 1]
    feature_all = geometry[0]
    live_count = pair_count[0, 0]
    live_all = (jnp.arange(EMAX, dtype=jnp.int32) < live_count).astype(jnp.float32)
    block_count = EMAX // PAIR_BLOCK

    def cut_block(index):
        start = index * PAIR_BLOCK
        owned_rows = lax.dynamic_slice_in_dim(owned_all, start, PAIR_BLOCK)
        other_rows = lax.dynamic_slice_in_dim(other_all, start, PAIR_BLOCK)
        features = lax.dynamic_slice_in_dim(feature_all, start, PAIR_BLOCK, 1).T
        live_slots = lax.dynamic_slice_in_dim(live_all, start, PAIR_BLOCK)
        return (owned_rows, other_rows, features, live_slots)

    history = []
    for layer in range(STEPS):
        extended = extended_2(latent, (("space", 0),), HALO)

        def sweep(index, agg, layer=layer, extended=extended):
            owned_rows, other_rows, features, live_slots = cut_block(index)
            message, _ = edge_forward(
                extended,
                owned_rows,
                other_rows,
                features,
                live_slots,
                edge_in[layer],
                edge_bias[layer],
                edge_out[layer],
            )
            return agg.at[owned_rows].add(message).at[other_rows].add(-message)

        agg_ext = lax.fori_loop(0, block_count, sweep, jnp.zeros(extended.shape, jnp.float32))
        agg = fold_rims(agg_ext)
        new_latent, kept = node_forward(
            latent, agg, node_in[layer], node_bias[layer], node_out[layer], gain[layer]
        )
        history.append((extended, kept))
        latent = new_latent
    grad = cotangent[0].astype(jnp.float32)
    per_layer = [None] * STEPS
    for layer in reversed(range(STEPS)):
        extended, kept = history[layer]
        dh_node, dagg, node_terms = node_backward(
            grad, kept, node_in[layer], node_out[layer], gain[layer]
        )
        dagg_ext = extended_2(dagg.astype(jnp.bfloat16), (("space", 0),), HALO).astype(dagg.dtype)

        def back(index, carry, layer=layer, extended=extended, dagg_ext=dagg_ext):
            accum, in_acc, bias_acc, out_acc = carry
            owned_rows, other_rows, features, live_slots = cut_block(index)
            _, kept_edge = edge_forward(
                extended,
                owned_rows,
                other_rows,
                features,
                live_slots,
                edge_in[layer],
                edge_bias[layer],
                edge_out[layer],
            )
            d_owned, d_other, terms = edge_backward(
                dagg_ext,
                owned_rows,
                other_rows,
                live_slots,
                kept_edge,
                edge_in[layer],
                edge_out[layer],
            )
            accum = accum.at[owned_rows].add(d_owned).at[other_rows].add(d_other)
            return (accum, in_acc + terms[0], bias_acc + terms[1], out_acc + terms[2])

        start = (
            jnp.zeros(extended.shape, jnp.float32),
            jnp.zeros(edge_in.shape[1:], jnp.float32),
            jnp.zeros(edge_bias.shape[1:], jnp.float32),
            jnp.zeros(edge_out.shape[1:], jnp.float32),
        )
        edge_dh, in_acc, bias_acc, out_acc = lax.fori_loop(0, block_count, back, start)
        grad = dh_node + fold_rims(edge_dh)
        layer_terms = (in_acc, bias_acc, out_acc) + node_terms
        per_layer[layer] = layer_terms
    stacked = tuple((jnp.stack([entry[k] for entry in per_layer]) for k in range(7)))
    stacked = lax.psum(stacked, ("space", "replicas"))
    down_rows = jnp.take(latent, leaving[0, 0], axis=0)
    up_rows = jnp.take(latent, leaving[0, 1], axis=0)
    from_upper = passed_along(down_rows, "space", -1)
    from_lower = passed_along(up_rows, "space", 1)
    arrivals = jnp.stack([from_upper, from_lower], axis=0)
    return (latent[None], grad[None], arrivals[None]) + stacked


def solution(mesh):
    return jax.shard_map(
        on_device,
        mesh=mesh,
        in_specs=(
            P("replicas", "space", None),
            P("replicas", None, "space"),
            P("replicas", None, "space"),
            P("replicas", "space"),
            P("replicas", "space", None),
            P("replicas", "space", None),
            P(),
            P(),
            P(),
            P(),
            P(),
            P(),
            P(),
        ),
        out_specs=(
            P("replicas", "space", None),
            P("replicas", "space", None),
            P("replicas", "space", None, None),
            P(),
            P(),
            P(),
            P(),
            P(),
            P(),
            P(),
        ),
        check_vma=False,
    )
```

profile of v0, /device:TPU:1, one launch (start us, length us, event | category | flops | bytes accessed | tf_op | source)
XLA Modules:
  0.0 691.7 jit_solution(5451467195809416752)
XLA Ops:
  8.0 5.1 collective-permute-start
  13.0 5.8 collective-permute-start.1
  22.2 21.5 %while.74 = (s32[]{:T(128)}, f32[320,128]{1,0:T(8,128)S(1)}, s32[1024]{0:T(1024)S(1)}, bf16[320,128]{1,0:T(8,128)(2,1)S(1)}, s32[1024]{0:T(1024)S(1)}, /*index=5...) while((s32[]{:T(128)}, f32[320,128]{1,0:T(8,128)S(1)}, ...), condition=%wide.region_3.5_spmd, body=%wide.region_0.4_spmd.sunk | while | flops 87726080 | bytes 4051135 | solution.py:166
  22.4 1.3 gather_fusion.1
  26.1 3.4 scatter_fusion
  29.5 3.4 scatter_custom_fusion.34
  33.1 1.3 gather_fusion.1
  36.9 3.4 scatter_fusion
  40.2 3.4 scatter_custom_fusion.34
  43.7 7.9 %collective-permute-start.2 = (f32[32,128]{1,0:T(8,128)S(1)}, f32[32,128]{1,0:T(8,128)S(1)}, u32[]{:S(2)}, u32[]{:S(2)}) collective-permute-start(f32[32,128]{1,0:T(8,128)S(1)} %get-tuple-element.1228), channel_id=1, source_target_pairs={{0,508},{4,0},{8,4},{12,8},{16,12},{20,16},{24,20},{28,24},{32,28}... | collective-permute-start | bytes 49160 | tf_op jit(solution)/shard_map/ppermute | solution.py:17
  51.7 1.9 collective-permute-start.3
  53.6 4.5 collective-permute-done.3
  60.0 1.9 collective-permute-start.4
  61.9 7.9 %collective-permute-start.5 = (bf16[32,128]{1,0:T(8,128)(2,1)S(1)}, bf16[32,128]{1,0:T(8,128)(2,1)S(1)}, u32[]{:S(2)}, u32[]{:S(2)}) collective-permute-start(bf16[32,128]{1,0:T(8,128)(2,1)S(1)} %get-tuple-element.1236), channel_id=1, source_target_pairs={{4,0},{8,4},{12,8},{16,12},{20,16},{24,20},{28,24},{32,28},{36,32}... | collective-permute-start | bytes 24584 | tf_op jit(solution)/shard_map/ppermute | solution.py:28
  70.5 21.5 %while.75 = (s32[]{:T(128)}, f32[320,128]{1,0:T(8,128)S(1)}, s32[1024]{0:T(1024)S(1)}, bf16[320,128]{1,0:T(8,128)(2,1)S(1)}, s32[1024]{0:T(1024)S(1)}, /*index=5...) while((s32[]{:T(128)}, f32[320,128]{1,0:T(8,128)S(1)}, ...), condition=%wide.region_9.11_spmd, body=%wide.region_6.0_spmd.sunk | while | flops 87726080 | bytes 4051135 | solution.py:166
  70.7 1.3 gather_fusion.3
  74.4 3.4 scatter_fusion.1
  77.8 3.4 scatter_custom_fusion.37
  85.2 3.4 scatter_fusion.1
  88.6 3.4 scatter_custom_fusion.37
  92.0 7.5 %collective-permute-start.6 = (f32[32,128]{1,0:T(8,128)S(1)}, f32[32,128]{1,0:T(8,128)S(1)}, u32[]{:S(2)}, u32[]{:S(2)}) collective-permute-start(f32[32,128]{1,0:T(8,128)S(1)} %get-tuple-element.1226), channel_id=1, source_target_pairs={{0,508},{4,0},{8,4},{12,8},{16,12},{20,16},{24,20},{28,24},{32,28}... | collective-permute-start | bytes 49160 | tf_op jit(solution)/shard_map/ppermute | solution.py:17
  99.6 1.9 collective-permute-start.7
  101.5 5.6 collective-permute-done.7
  109.7 1.9 collective-permute-start.8
  111.6 7.7 %collective-permute-start.9 = (bf16[32,128]{1,0:T(8,128)(2,1)S(1)}, bf16[32,128]{1,0:T(8,128)(2,1)S(1)}, u32[]{:S(2)}, u32[]{:S(2)}) collective-permute-start(bf16[32,128]{1,0:T(8,128)(2,1)S(1)} %get-tuple-element.1234), channel_id=1, source_target_pairs={{4,0},{8,4},{12,8},{16,12},{20,16},{24,20},{28,24},{32,28},{36,32}... | collective-permute-start | bytes 24584 | tf_op jit(solution)/shard_map/ppermute | solution.py:28
  120.8 7.2 %collective-permute-start.16 = (bf16[16,128]{1,0:T(8,128)(2,1)S(1)}, bf16[16,128]{1,0:T(8,128)(2,1)S(1)}, u32[]{:S(2)}, u32[]{:S(2)}) collective-permute-start(bf16[16,128]{1,0:T(8,128)(2,1)S(1)} %broadcast_select_fusion.11), channel_id=1, source_target_pairs={{0,508},{4,0},{8,4},{12,8},{16,12},{20,16},{24,20},{28,24},{32,28}... | collective-permute-start | bytes 12296 | tf_op jit(solution)/shard_map/ppermute | solution.py:17
  128.1 29.5 %while.76 = (s32[]{:T(128)}, f32[320,128]{1,0:T(8,128)S(1)}, f32[260,128]{1,0:T(8,128)S(1)}, f32[128]{0:T(128)S(1)}, f32[128,128]{1,0:T(8,128)S(1)}, /*index=5*/...) while((s32[]{:T(128)}, f32[320,128]{1,0:T(8,128)S(1)}, ...), condition=%wide.region_18.21_spmd.clone, body=%wide.region_14.20_spmd.clone.sunk | while | flops 243334784 | bytes 10134771 | solution.py:213
  128.3 1.3 gather_fusion.4
  136.0 3.4 scatter_custom_fusion.40
  139.4 3.4 scatter_custom_fusion.41
  150.7 3.4 scatter_custom_fusion.40
  154.1 3.4 scatter_custom_fusion.41
  157.6 1.9 collective-permute-start.10
  159.6 3.6 collective-permute-start.17
  163.3 1.9 collective-permute-start.11
  168.9 3.4 collective-permute-start.12
  172.3 6.5 collective-permute-start.13
  180.3 29.5 %while.77 = (s32[]{:T(128)}, f32[320,128]{1,0:T(8,128)S(1)}, f32[260,128]{1,0:T(8,128)S(1)}, f32[128]{0:T(128)S(1)}, f32[128,128]{1,0:T(8,128)S(1)}, /*index=5*/...) while((s32[]{:T(128)}, f32[320,128]{1,0:T(8,128)S(1)}, ...), condition=%wide.region_25.28_spmd.clone, body=%wide.region_21.27_spmd.clone.sunk | while | flops 243334784 | bytes 10134771 | solution.py:213
  180.5 1.3 gather_fusion.8
  188.2 3.4 scatter_custom_fusion.44
  191.6 3.4 scatter_custom_fusion.45
  203.0 3.4 scatter_custom_fusion.44
  206.4 3.4 scatter_custom_fusion.45
  209.8 7.0 %collective-permute-start.14 = (f32[32,128]{1,0:T(8,128)S(1)}, f32[32,128]{1,0:T(8,128)S(1)}, u32[]{:S(2)}, u32[]{:S(2)}) collective-permute-start(f32[32,128]{1,0:T(8,128)S(1)} %slice.487), channel_id=1, source_target_pairs={{0,508},{4,0},{8,4},{12,8},{16,12},{20,16},{24,20},{28,24},{32,28}... | collective-permute-start | bytes 49160 | tf_op jit(solution)/shard_map/ppermute | solution.py:17
  218.2 1.9 collective-permute-start.15
  220.2 108.6 %all-reduce = (f32[2,128]{1,0:T(2,128)}, f32[2,128]{1,0:T(2,128)}, f32[2,128]{1,0:T(2,128)}) all-reduce(f32[2,128]{1,0:T(2,128)S(1)} %pad_maximum_fusion.24, f32[2,128]{1,0:T(2,128)S(1)} %pad_maximum_fusion.25, f32[2,128]{1,0:T(2,128)S(1)} %pad_maximum_fusion.26), channel_id=1, replica_groups=mesh['space'=128,'replicas'=4] {'space','replicas'}, use_global_device_ids=true, to_apply=%region_27.31 | all-reduce | flops 768 | bytes 6144 | tf_op jit(solution)/shard_map/psum | solution.py:218
  329.4 350.9 %all-reduce.4.cloned.1.call-done = (f32[2,260,128]{2,1,0:T(8,128)}, f32[2,128,128]{2,1,0:T(8,128)}, f32[2,256,128]{2,1,0:T(8,128)}, f32[2,128,128]{2,1,0:T(8,128)}) async-done(((f32[2,260,128]{2,1,0:T(8,128)}, f32[2,128,128]{2,1,0:T(8,128)}, f32[2,256,128]{2,1,0:T(8,128)}, f32[2,128,128]{2,1,0:T(8,128)}), (f32[2,260,128]{2,1,0:T(8,128)}, f32[2,128,128]{2,1,0:T(8,128)}, f32[2,256,128]{2,1,0:T(8,128)}, ...) | async-done | bytes 790544 | tf_op jit(solution)/shard_map/psum | solution.py:218
  680.3 1.8 copy.31
  (273 shorter events, 59.7 us)
Async XLA Ops:
  7.2 673.2 %all-reduce.4.cloned.1.call-start = ((), (), s32[]{:S(2)}) async-start(), calls=%async_computation | async-start | bytes 1589248 | tf_op jit(solution)/shard_map/psum | solution.py:218
  7.2 12.2 %copy-start.10 = (f32[2,128]{1,0:T(2,128)S(1)}, f32[2,128]{1,0:T(2,128)}, u32[]{:S(2)}) copy-start(f32[2,128]{1,0:T(2,128)} %param.53) | copy-start | bytes 3076
  7.2 12.3 %copy-start.9 = (s32[1,2,16]{2,1,0:T(2,128)S(1)}, s32[1,2,16]{2,1,0:T(2,128)}, u32[]{:S(2)}) copy-start(s32[1,2,16]{2,1,0:T(2,128)} %param.48) | copy-start | bytes 388
  8.0 11.5 %copy-start.8 = (s32[1,2,1024]{2,1,0:T(2,128)S(1)}, s32[1,2,1024]{2,1,0:T(2,128)}, u32[]{:S(2)}) copy-start(s32[1,2,1024]{2,1,0:T(2,128)} %param.44) | copy-start | bytes 24580
  8.0 12.8 %collective-permute-start = (bf16[32,128]{1,0:T(8,128)(2,1)S(1)}, bf16[32,128]{1,0:T(8,128)(2,1)S(1)}, u32[]{:S(2)}, u32[]{:S(2)}) collective-permute-start(bf16[32,128]{1,0:T(8,128)(2,1)S(1)} %get-tuple-element.1237), channel_id=1, source_target_pairs={{0,4},{4,8},{8,12},{12,16},{16,20},{20,24},{24,28},{28,32},{32,36}... | collective-permute-start | bytes 24584 | tf_op jit(solution)/shard_map/ppermute | solution.py:27
  13.0 7.7 %collective-permute-start.1 = (bf16[32,128]{1,0:T(8,128)(2,1)S(1)}, bf16[32,128]{1,0:T(8,128)(2,1)S(1)}, u32[]{:S(2)}, u32[]{:S(2)}) collective-permute-start(bf16[32,128]{1,0:T(8,128)(2,1)S(1)} %get-tuple-element.1238), channel_id=1, source_target_pairs={{4,0},{8,4},{12,8},{16,12},{20,16},{24,20},{28,24},{32,28},{36,32}... | collective-permute-start | bytes 24584 | tf_op jit(solution)/shard_map/ppermute | solution.py:28
  19.5 0.9 copy-start.7
  20.5 0.8 copy-start
  21.4 0.8 copy-start.13
  21.4 0.8 copy-start.14
  43.7 7.9 %copy-start.11 = (f32[2,128]{1,0:T(2,128)S(1)}, f32[2,128]{1,0:T(2,128)}, u32[]{:S(2)}) copy-start(f32[2,128]{1,0:T(2,128)} %param.55) | copy-start | bytes 3076
  43.7 9.9 %collective-permute-start.2 = (f32[32,128]{1,0:T(8,128)S(1)}, f32[32,128]{1,0:T(8,128)S(1)}, u32[]{:S(2)}, u32[]{:S(2)}) collective-permute-start(f32[32,128]{1,0:T(8,128)S(1)} %get-tuple-element.1228), channel_id=1, source_target_pairs={{0,508},{4,0},{8,4},{12,8},{16,12},{20,16},{24,20},{28,24},{32,28}... | collective-permute-start | bytes 49160 | tf_op jit(solution)/shard_map/ppermute | solution.py:17
  51.7 6.4 collective-permute-start.3
  53.6 4.5 copy-start.6
  58.1 0.8 copy-start.12
  59.0 0.7 copy-start.15
  60.0 9.8 %collective-permute-start.4 = (bf16[32,128]{1,0:T(8,128)(2,1)S(1)}, bf16[32,128]{1,0:T(8,128)(2,1)S(1)}, u32[]{:S(2)}, u32[]{:S(2)}) collective-permute-start(bf16[32,128]{1,0:T(8,128)(2,1)S(1)} %get-tuple-element.1235), channel_id=1, source_target_pairs={{0,4},{4,8},{8,12},{12,16},{16,20},{20,24},{24,28},{28,32},{32,36}... | collective-permute-start | bytes 24584 | tf_op jit(solution)/shard_map/ppermute | solution.py:27
  61.9 8.5 %collective-permute-start.5 = (bf16[32,128]{1,0:T(8,128)(2,1)S(1)}, bf16[32,128]{1,0:T(8,128)(2,1)S(1)}, u32[]{:S(2)}, u32[]{:S(2)}) collective-permute-start(bf16[32,128]{1,0:T(8,128)(2,1)S(1)} %get-tuple-element.1236), channel_id=1, source_target_pairs={{4,0},{8,4},{12,8},{16,12},{20,16},{24,20},{28,24},{32,28},{36,32}... | collective-permute-start | bytes 24584 | tf_op jit(solution)/shard_map/ppermute | solution.py:28
  92.0 9.5 %collective-permute-start.6 = (f32[32,128]{1,0:T(8,128)S(1)}, f32[32,128]{1,0:T(8,128)S(1)}, u32[]{:S(2)}, u32[]{:S(2)}) collective-permute-start(f32[32,128]{1,0:T(8,128)S(1)} %get-tuple-element.1226), channel_id=1, source_target_pairs={{0,508},{4,0},{8,4},{12,8},{16,12},{20,16},{24,20},{28,24},{32,28}... | collective-permute-start | bytes 49160 | tf_op jit(solution)/shard_map/ppermute | solution.py:17
  99.6 7.6 %collective-permute-start.7 = (f32[32,128]{1,0:T(8,128)S(1)}, f32[32,128]{1,0:T(8,128)S(1)}, u32[]{:S(2)}, u32[]{:S(2)}) collective-permute-start(f32[32,128]{1,0:T(8,128)S(1)} %get-tuple-element.1225), channel_id=1, source_target_pairs={{0,4},{4,8},{8,12},{12,16},{16,20},{20,24},{24,28},{28,32},{32,36}... | collective-permute-start | bytes 49160 | tf_op jit(solution)/shard_map/ppermute | solution.py:17
  107.7 0.8 copy-start.1
  109.0 11.2 %copy-start.2 = (bf16[256,128]{1,0:T(8,128)(2,1)}, bf16[256,128]{1,0:T(8,128)(2,1)S(1)}, u32[]{:S(2)}) copy-start(bf16[256,128]{1,0:T(8,128)(2,1)S(1)} %get-tuple-element.1230) | copy-start | bytes 196612
  109.7 18.3 %collective-permute-start.8 = (bf16[32,128]{1,0:T(8,128)(2,1)S(1)}, bf16[32,128]{1,0:T(8,128)(2,1)S(1)}, u32[]{:S(2)}, u32[]{:S(2)}) collective-permute-start(bf16[32,128]{1,0:T(8,128)(2,1)S(1)} %get-tuple-element.1233), channel_id=1, source_target_pairs={{0,4},{4,8},{8,12},{12,16},{16,20},{20,24},{24,28},{28,32},{32,36}... | collective-permute-start | bytes 24584 | tf_op jit(solution)/shard_map/ppermute | solution.py:27
  111.6 16.4 %collective-permute-start.9 = (bf16[32,128]{1,0:T(8,128)(2,1)S(1)}, bf16[32,128]{1,0:T(8,128)(2,1)S(1)}, u32[]{:S(2)}, u32[]{:S(2)}) collective-permute-start(bf16[32,128]{1,0:T(8,128)(2,1)S(1)} %get-tuple-element.1234), channel_id=1, source_target_pairs={{4,0},{8,4},{12,8},{16,12},{20,16},{24,20},{28,24},{32,28},{36,32}... | collective-permute-start | bytes 24584 | tf_op jit(solution)/shard_map/ppermute | solution.py:28
  120.8 44.4 %collective-permute-start.16 = (bf16[16,128]{1,0:T(8,128)(2,1)S(1)}, bf16[16,128]{1,0:T(8,128)(2,1)S(1)}, u32[]{:S(2)}, u32[]{:S(2)}) collective-permute-start(bf16[16,128]{1,0:T(8,128)(2,1)S(1)} %broadcast_select_fusion.11), channel_id=1, source_target_pairs={{0,508},{4,0},{8,4},{12,8},{16,12},{20,16},{24,20},{28,24},{32,28}... | collective-permute-start | bytes 12296 | tf_op jit(solution)/shard_map/ppermute | solution.py:17
  157.6 5.7 collective-permute-start.10
  159.6 5.6 collective-permute-start.17
  163.3 3.6 collective-permute-start.11
  167.1 0.9 copy-start.16
  168.9 11.3 %collective-permute-start.12 = (bf16[32,128]{1,0:T(8,128)(2,1)S(1)}, bf16[32,128]{1,0:T(8,128)(2,1)S(1)}, u32[]{:S(2)}, u32[]{:S(2)}) collective-permute-start(bf16[32,128]{1,0:T(8,128)(2,1)S(1)} %get-tuple-element.1231), channel_id=1, source_target_pairs={{0,4},{4,8},{8,12},{12,16},{16,20},{20,24},{24,28},{28,32},{32,36}... | collective-permute-start | bytes 24584 | tf_op jit(solution)/shard_map/ppermute | solution.py:27
  172.3 7.9 %collective-permute-start.13 = (bf16[32,128]{1,0:T(8,128)(2,1)S(1)}, bf16[32,128]{1,0:T(8,128)(2,1)S(1)}, u32[]{:S(2)}, u32[]{:S(2)}) collective-permute-start(bf16[32,128]{1,0:T(8,128)(2,1)S(1)} %get-tuple-element.1232), channel_id=1, source_target_pairs={{4,0},{8,4},{12,8},{16,12},{20,16},{24,20},{28,24},{32,28},{36,32}... | collective-permute-start | bytes 24584 | tf_op jit(solution)/shard_map/ppermute | solution.py:28
  209.8 8.4 %collective-permute-start.14 = (f32[32,128]{1,0:T(8,128)S(1)}, f32[32,128]{1,0:T(8,128)S(1)}, u32[]{:S(2)}, u32[]{:S(2)}) collective-permute-start(f32[32,128]{1,0:T(8,128)S(1)} %slice.487), channel_id=1, source_target_pairs={{0,508},{4,0},{8,4},{12,8},{16,12},{20,16},{24,20},{28,24},{32,28}... | collective-permute-start | bytes 49160 | tf_op jit(solution)/shard_map/ppermute | solution.py:17
  218.2 110.5 %collective-permute-start.15 = (f32[32,128]{1,0:T(8,128)S(1)}, f32[32,128]{1,0:T(8,128)S(1)}, u32[]{:S(2)}, u32[]{:S(2)}) collective-permute-start(f32[32,128]{1,0:T(8,128)S(1)} %get-tuple-element.1221), channel_id=1, source_target_pairs={{0,4},{4,8},{8,12},{12,16},{16,20},{20,24},{24,28},{28,32},{32,36}... | collective-permute-start | bytes 49160 | tf_op jit(solution)/shard_map/ppermute | solution.py:17
  680.3 1.8 copy-start.5
  682.2 1.0 copy-start.3
  683.2 1.0 copy-start.4
Sparse Core Ops, SparseCore 0:
  220.3 459.9 all-reduce.3
where the time goes:
time: 693 us; the launch traced here: 692 us
  waiting for transfers between devices  363 us (52%)
  blocking collectives  109 us (16%)
  starting transfers between devices  83 us (12%)
  other arithmetic  64.6 us (9%)
  local copies, waits for them, and re-layouts  42 us (6%)
  between operations  15.5 us (2%)
  matrix products  14.2 us (2%)
    psum x1, waiting for transfers between devices, on_device(): stacked = lax.psum(stacked, ('space', 'replicas'))  351 us
    psum x1, blocking collectives, on_device(): stacked = lax.psum(stacked, ('space', 'replicas'))  109 us
    ppermute x10, starting transfers between devices, passed_along(): lax.ppermute(array, axis, [(i, (i + by) % peers) for i in range(peers)])  42.8 us
    ppermute x4, starting transfers between devices, extended_2(): after = lax.ppermute(leading, axis, down)  27.9 us
    scatter-add x8, other arithmetic, back(): accum = accum.at[owned_rows].add(d_owned).at[other_rows].add(d_other)  27.3 us
    scatter-add x8, other arithmetic, sweep(): return agg.at[owned_rows].add(message).at[other_rows].add(-message)  27.1 us
  transfers between devices with their start and end apart: 19, of which 5 were waited for; matrix products, arithmetic and copies ran while one was open for 5% of the time, Pallas kernels for 0%

commit v1 on v0

v1 whole, which is shorter than its diff:
```python
import jax
import jax.numpy as jnp
from jax import lax
from jax.experimental import pallas as pl
from jax.experimental.pallas import tpu as pltpu
from jax.sharding import Mesh, PartitionSpec as P


F32 = jnp.float32
BF16 = jnp.bfloat16
L = 128
ROWS = 256
EMAX = 1024
BLK = 256
OWN_BLOCKS = EMAX // BLK
NB_BLOCKS = EMAX // 128
LAT_HALO = 128
COT_HALO = 64
SENT = LAT_HALO + COT_HALO + 64 + 16
D_AT = LAT_HALO + COT_HALO
X_AT = D_AT + 64
MIG = 16
MAIN = 1536
EXTRA = 14
EPS = 1e-05
VMEM_LIMIT = 48 * 1024 * 1024


def dot(a, b):
    return jnp.dot(a, b, preferred_element_type=F32)


def dot_nt(a, b):
    return lax.dot_general(a, b, (((1,), (1,)), ((), ())), preferred_element_type=F32)


def dot_tn(a, b):
    return lax.dot_general(a, b, (((0,), (0,)), ((), ())), preferred_element_type=F32)


def place(row):
    below = row < 0
    above = row >= ROWS
    out = jnp.where(below, -1 - row, row - ROWS)
    block = lax.shift_right_arithmetic(out, 5)
    inner = jnp.where(below, row + 32 * (block + 1), row - ROWS - 32 * block + 32)
    outside = jnp.logical_or(below, above)
    return jnp.where(outside, 64 * block + inner, row), outside


def pack_kernel(count_ref, lat_ref, cot_ref, pairs_ref, geo_ref, leav_ref, up_ref, down_ref):
    count = count_ref[0, 0]
    own = pairs_ref[0, 0:1, :]
    other = pairs_ref[0, 1:2, :]
    slot = lax.broadcasted_iota(jnp.int32, (1, EMAX), 1)
    live = slot < count
    geo = geo_ref[0].astype(F32)
    leav = leav_ref[0].astype(F32)

    def fill(ref, lat, cot, shift, movers, mover_shift):
        ref[0:LAT_HALO, :] = lat
        ref[LAT_HALO:D_AT, :] = cot
        i_row = own + shift
        j_row = other + shift
        inside = jnp.logical_and(
            jnp.logical_and(i_row >= -LAT_HALO, i_row < ROWS + LAT_HALO),
            jnp.logical_and(j_row >= -LAT_HALO, j_row < ROWS + LAT_HALO),
        )
        good = jnp.logical_and(live, inside)
        i_at, _ = place(i_row)
        j_at, j_hi = place(j_row)
        i_at = jnp.where(good, i_at, -1).astype(F32)
        j_at = jnp.where(good, j_at, -1).astype(F32)
        hi = jnp.where(j_hi, 1.0, 0.0).astype(F32)
        rows = jnp.concatenate([i_at, j_at, hi, jnp.ones((1, EMAX), F32), geo], axis=0)
        for t in range(4):
            two = [rows[:, 256 * t : 256 * t + 128], rows[:, 256 * t + 128 : 256 * t + 256]]
            ref[D_AT + 16 * t : D_AT + 16 * t + 16, :] = jnp.concatenate(two, axis=0).astype(BF16)
        tail = jnp.concatenate([movers + mover_shift, jnp.zeros((1, 128 - MIG), F32)], axis=1)
        ref[X_AT:SENT, :] = jnp.broadcast_to(tail, (16, 128)).astype(BF16)

    fill(up_ref, lat_ref[0, ROWS - LAT_HALO :, :], cot_ref[0, ROWS - COT_HALO :, :], -32 - ROWS, leav[1:2, :], -224.0)
    fill(down_ref, lat_ref[0, :LAT_HALO, :], cot_ref[0, :COT_HALO, :], ROWS - 32, leav[0:1, :], 32.0)


def main_kernel(
    chunks,
    count_ref,
    lat_ref,
    cot_ref,
    pairs_ref,
    geo_ref,
    low_ref,
    upp_ref,
    edge_in_ref,
    edge_bias_ref,
    edge_out_ref,
    node_in_ref,
    node_bias_ref,
    node_out_ref,
    gain_ref,
    final_ref,
    grad_ref,
    arr_ref,
    packed_ref,
    ohi,
    ohj,
    ohit,
    ohjt,
    jhi,
    dcol,
    drow,
    slope,
    t_nb,
    q_nb,
):
    lanes = lax.broadcasted_iota(jnp.int32, (BLK, BLK), 1).astype(F32)
    subs = lax.broadcasted_iota(jnp.int32, (BLK, BLK), 0).astype(F32)

    def prepare(block, rows, cols):
        ohi[block] = jnp.where(cols[:, 0:1] == lanes, 1.0, 0.0).astype(BF16)
        ohj[block] = jnp.where(cols[:, 1:2] == lanes, 1.0, 0.0).astype(BF16)
        ohit[block] = jnp.where(rows[0:1, :] == subs, 1.0, 0.0).astype(BF16)
        ohjt[block] = jnp.where(rows[1:2, :] == subs, 1.0, 0.0).astype(BF16)
        jhi[block] = jnp.broadcast_to(cols[:, 2:3], (BLK, L))
        dcol[block] = cols.astype(BF16)

    count = count_ref[0, 0]
    slot = lax.broadcasted_iota(jnp.int32, (1, EMAX), 1)
    live = slot < count
    i_at = pairs_ref[0, 0:1, :] - 32
    j_at, j_out = place(pairs_ref[0, 1:2, :] - 32)
    own_rows = jnp.concatenate(
        [
            jnp.where(live, i_at, -1).astype(F32),
            jnp.where(live, j_at, -1).astype(F32),
            jnp.where(j_out, 1.0, 0.0).astype(F32),
            jnp.ones((1, EMAX), F32),
            geo_ref[0].astype(F32),
        ],
        axis=0,
    )
    for k in range(OWN_BLOCKS):
        rows = own_rows[:, BLK * k : BLK * k + BLK]
        drow[k] = rows.astype(BF16)
        prepare(k, rows, jnp.transpose(rows))

    low_rows = low_ref[D_AT:X_AT, :].astype(F32)
    upp_rows = upp_ref[D_AT:X_AT, :].astype(F32)
    for k in range(NB_BLOCKS):
        rows = jnp.concatenate([low_rows[8 * k : 8 * k + 8], upp_rows[8 * k : 8 * k + 8]], axis=1)
        prepare(OWN_BLOCKS + k, rows, jnp.transpose(rows))

    def around(source_low, source_upp, width, height):
        parts = []
        for b in range(width // 32):
            parts.append(source_low[width - 32 * (b + 1) : width - 32 * b])
            parts.append(source_upp[32 * b : 32 * b + 32])
        if height > 2 * width:
            parts.append(jnp.zeros((height - 2 * width, L), parts[0].dtype))
        return jnp.concatenate(parts, axis=0)

    def halves(cat):
        return cat[:, :L], cat[:, L:]

    def edge_weights(layer):
        top = edge_in_ref[layer, 0:L, :]
        bottom = edge_in_ref[layer, L : 2 * L, :]
        straight = jnp.concatenate([top, bottom], axis=1)
        return straight, jnp.concatenate([bottom, top], axis=1)

    def forward_block(block, i_source, both, weights, geo_weights, bias, layer):
        at_i = dot(ohi[block], i_source).astype(BF16)
        lo, hi = halves(dot(ohj[block], both))
        is_hi = jhi[block] > 0.5
        at_j = jnp.where(is_hi, hi, lo).astype(BF16)
        pre = dot(jnp.concatenate([at_i, at_j], axis=1), weights) + dot(dcol[block], geo_weights) + bias
        sig = 0.5 * jnp.tanh(0.5 * pre) + 0.5
        act = pre * sig
        slope[layer, block] = sig + act * (1.0 - sig)
        diff = act[:, :L] - act[:, L:]
        none = jnp.zeros_like(diff)
        split = jnp.concatenate([jnp.where(is_hi, none, diff), jnp.where(is_hi, diff, none)], axis=1)
        return dot(ohit[block], diff.astype(BF16)), dot(ohjt[block], split.astype(BF16))

    def edge_forward(layer, h_lo, h_hi, nb_blocks):
        straight, crossed = edge_weights(layer)
        weights = jnp.concatenate([straight, crossed], axis=0)
        geo_top = edge_in_ref[layer, 2 * L : 2 * L + 4, :].astype(F32)
        geo_weights = jnp.concatenate(
            [jnp.zeros((4, 2 * L), F32), jnp.concatenate([geo_top, -geo_top], axis=1)], axis=0
        ).astype(BF16)
        bias_row = edge_bias_ref[layer : layer + 1, :]
        bias = jnp.concatenate([bias_row, bias_row], axis=1)
        both = jnp.concatenate([h_lo, h_hi], axis=1)
        t_nb[...] = jnp.zeros_like(t_nb)

        def body(k, carry):
            by_i, by_j = forward_block(OWN_BLOCKS + k, h_hi, both, weights, geo_weights, bias, layer)
            t_nb[:, :L] += -by_j[:, :L]
            t_nb[:, L:] += by_i - by_j[:, L:]
            return carry

        lax.fori_loop(0, nb_blocks, body, 0)
        own_lo = jnp.zeros((ROWS, L), F32)
        own_hi = jnp.zeros((ROWS, L), F32)
        for k in range(OWN_BLOCKS):
            by_i, by_j = forward_block(k, h_lo, both, weights, geo_weights, bias, layer)
            own_lo += by_i - by_j[:, :L]
            own_hi += -by_j[:, L:]
        return own_lo, own_hi

    def node_forward(layer, h, total):
        agg = dot(total.astype(BF16), edge_out_ref[layer]).astype(BF16)
        joined = jnp.concatenate([h, agg], axis=1)
        pre = dot(joined, node_in_ref[layer]) + node_bias_ref[layer : layer + 1, :]
        sig = 0.5 * jnp.tanh(0.5 * pre) + 0.5
        act = pre * sig
        hidden = act.astype(BF16)
        out = dot(hidden, node_out_ref[layer])
        centred = out - jnp.mean(out, axis=1, keepdims=True)
        inv = lax.rsqrt(jnp.mean(centred * centred, axis=1, keepdims=True) + EPS)
        normed = centred * inv
        new = (h.astype(F32) + normed * gain_ref[layer : layer + 1, :]).astype(BF16)
        return new, (joined, sig + act * (1.0 - sig), hidden, normed, inv)

    def node_backward(layer, grad, kept):
        size = grad.shape[0]
        joined, node_slope, hidden, normed, inv = (v[:size] for v in kept)
        gain_term = jnp.sum(grad[:ROWS] * normed[:ROWS], axis=0, keepdims=True)
        dnorm = grad * gain_ref[layer : layer + 1, :]
        mean_a = jnp.mean(dnorm, axis=1, keepdims=True)
        mean_b = jnp.mean(dnorm * normed, axis=1, keepdims=True)
        dout = ((dnorm - mean_a - normed * mean_b) * inv).astype(BF16)
        out_term = dot_tn(hidden[:ROWS], dout[:ROWS])
        dpre = (dot_nt(dout, node_out_ref[layer]) * node_slope).astype(BF16)
        in_term = dot_tn(joined[:ROWS], dpre[:ROWS])
        bias_term = jnp.sum(dpre[:ROWS].astype(F32), axis=0, keepdims=True)
        dx = dot_nt(dpre, node_in_ref[layer])
        return grad + dx[:, :L], dx[:, L:].astype(BF16), (in_term, bias_term, out_term, gain_term)

    def backward_block(block, i_source, both, layer):
        at_i = dot(ohi[block], i_source)
        lo, hi = halves(dot(ohj[block], both))
        is_hi = jhi[block] > 0.5
        dd = at_i - jnp.where(is_hi, hi, lo)
        dfwd = dd * slope[layer, block, :, :L]
        drev = -dd * slope[layer, block, :, L:]
        straight = jnp.concatenate([dfwd, drev], axis=1)
        crossed = jnp.concatenate([drev, dfwd], axis=1)
        wide = jnp.concatenate([is_hi, is_hi], axis=1)
        return straight.astype(BF16), crossed, wide

    def edge_backward(layer, e_lo, e_hi, nb_blocks, with_hi):
        both = jnp.concatenate([e_lo, e_hi], axis=1)
        q_nb[...] = jnp.zeros_like(q_nb)

        def body(k, carry):
            block = OWN_BLOCKS + k
            straight, crossed, is_hi = backward_block(block, e_hi, both, layer)
            none = jnp.zeros_like(crossed)
            q_nb[0:ROWS, :] += dot(ohjt[block], jnp.where(is_hi, none, crossed).astype(BF16))
            if with_hi:
                q_nb[ROWS:, :] += dot(ohjt[block], jnp.where(is_hi, crossed, none).astype(BF16)) + dot(
                    ohit[block], straight
                )
            return carry

        lax.fori_loop(0, nb_blocks, body, 0)
        q_lo = jnp.zeros((ROWS, 2 * L), F32)
        q_hi = jnp.zeros((ROWS, 2 * L), F32)
        geo = jnp.zeros((8, 2 * L), F32)
        for k in range(OWN_BLOCKS):
            straight, crossed, is_hi = backward_block(k, e_lo, both, layer)
            none = jnp.zeros_like(crossed)
            q_lo += dot(ohit[k], straight) + dot(ohjt[k], jnp.where(is_hi, none, crossed).astype(BF16))
            q_hi += dot(ohjt[k], jnp.where(is_hi, crossed, none).astype(BF16))
            geo += dot(drow[k], straight)
        return q_lo, q_hi, geo

    h0_lo = lat_ref[0]
    h0_hi = around(low_ref[0:LAT_HALO, :], upp_ref[0:LAT_HALO, :], LAT_HALO, ROWS)
    t0_lo, t0_hi = edge_forward(0, h0_lo, h0_hi, NB_BLOCKS)
    total0 = jnp.concatenate([t0_lo + t_nb[:, :L], t0_hi + t_nb[:, L:]], axis=0)
    h0 = jnp.concatenate([h0_lo, h0_hi], axis=0)
    h1, kept0 = node_forward(0, h0, total0)
    t1_lo, t1_hi = edge_forward(1, h1[:ROWS], h1[ROWS:], NB_BLOCKS)
    near = ROWS + 2 * COT_HALO
    total1 = jnp.concatenate([t1_lo + t_nb[:, :L], t1_hi[: near - ROWS] + t_nb[: near - ROWS, L:]], axis=0)
    h2, kept1 = node_forward(1, h1[:near], total1)
    final_ref[0] = h2[:ROWS]

    few = lax.broadcasted_iota(jnp.int32, (MIG, 2 * COT_HALO), 1).astype(F32)
    for k, ref in ((0, upp_ref), (1, low_ref)):
        movers = jnp.transpose(ref[X_AT:SENT, :].astype(F32))[0:MIG, 0:1]
        chosen = jnp.where(movers == few, 1.0, 0.0).astype(BF16)
        arr_ref[0, k] = dot(chosen, h2[ROWS:]).astype(BF16)

    def with_zeros(value):
        return jnp.concatenate([value, jnp.zeros((2 * ROWS - value.shape[0],) + value.shape[1:], value.dtype)], axis=0)

    def layer_back(layer, grad, kept, own_total, h, nb_blocks, keep_rows):
        part, dagg, node_terms = node_backward(layer, grad, kept)
        spread = with_zeros(dagg)
        e = with_zeros(dot_nt(dagg, edge_out_ref[layer]).astype(BF16))
        q_lo, q_hi, geo = edge_backward(layer, e[:ROWS], e[ROWS:], nb_blocks, keep_rows > ROWS)
        out_term = dot_tn(own_total.astype(BF16), spread)
        q_own = jnp.concatenate([q_lo, q_hi], axis=0)
        in_term = dot_tn(h, q_own.astype(BF16))
        straight, _ = edge_weights(layer)
        q_all = (q_own[:keep_rows] + q_nb[:keep_rows, :]).astype(BF16)
        new = part[:keep_rows] + dot_nt(q_all, straight)
        return new, (in_term, geo, out_term) + node_terms

    own1 = jnp.concatenate([t1_lo, t1_hi], axis=0)
    own0 = jnp.concatenate([t0_lo, t0_hi], axis=0)
    cot = jnp.concatenate(
        [cot_ref[0], around(low_ref[LAT_HALO:D_AT, :], upp_ref[LAT_HALO:D_AT, :], COT_HALO, 2 * COT_HALO)], axis=0
    ).astype(F32)
    grad1, terms1 = layer_back(1, cot, kept1, own1, h1, NB_BLOCKS, ROWS + 64)
    grad0, terms0 = layer_back(0, grad1, kept0, own0, h0, NB_BLOCKS, ROWS)
    grad_ref[0] = grad0

    size = MAIN // chunks
    per = -(-EXTRA // chunks)
    packed_ref[:, size:, :] = jnp.zeros((chunks, packed_ref.shape[1] - size, L), BF16)
    at = 0
    extra = 0
    for terms in (terms0, terms1):
        in_term, geo, out_term, node_in_term, node_bias_term, node_out_term, gain_term = terms
        for value in (in_term[:, :L], in_term[:, L:], out_term, node_in_term, node_out_term):
            value = value.astype(BF16)
            for r in range(0, value.shape[0], 16):
                packed_ref[at // size, pl.ds(at % size, 16), :] = value[r : r + 16]
                at += 16
        small = [geo[4 + g : 5 + g, :L] - geo[4 + g : 5 + g, L:] for g in range(4)]
        small += [geo[3:4, :L] + geo[3:4, L:], node_bias_term, gain_term]
        for value in small:
            spot = size + extra % per
            packed_ref[extra // per, spot : spot + 1, :] = value.astype(BF16)
            extra += 1


def fold_kernel(copies, in_ref, out_ref):
    total = in_ref[0].astype(F32)
    for k in range(1, in_ref.shape[0]):
        total += in_ref[k].astype(F32)
    total = total.astype(BF16)
    for k in range(copies):
        out_ref[k] = total


def fold(array, copies):
    return pl.pallas_call(
        lambda a, b: fold_kernel(copies, a, b),
        out_shape=jax.ShapeDtypeStruct((copies,) + array.shape[1:], BF16),
        in_specs=[pl.BlockSpec(memory_space=pltpu.VMEM)],
        out_specs=pl.BlockSpec(memory_space=pltpu.VMEM),
        compiler_params=pltpu.CompilerParams(vmem_limit_bytes=VMEM_LIMIT),
        name="fold",
    )(array)


def unpack_kernel(chunks, in_ref, edge_in, edge_bias, edge_out, node_in, node_bias, node_out, gain):
    size = MAIN // chunks
    per = -(-EXTRA // chunks)
    at = 0
    extra = 0
    for layer in range(2):
        for ref, rows in ((edge_in, 2 * L), (edge_out, L), (node_in, 2 * L), (node_out, L)):
            for r in range(0, rows, 16):
                ref[layer, r : r + 16, :] = in_ref[at // size, pl.ds(at % size, 16), :].astype(F32)
                at += 16
        small = []
        for _ in range(7):
            spot = size + extra % per
            small.append(in_ref[extra // per, spot : spot + 1, :].astype(F32))
            extra += 1
        edge_in[layer, 2 * L : 2 * L + 4, :] = jnp.concatenate(small[:4], axis=0)
        edge_bias[layer : layer + 1, :] = small[4]
        node_bias[layer : layer + 1, :] = small[5]
        gain[layer : layer + 1, :] = small[6]


def vmem(count):
    return [pl.BlockSpec(memory_space=pltpu.VMEM)] * count


def solution(mesh):
    n_space = mesh.shape["space"]
    n_x = mesh.shape["replicas"]
    n_c = 2
    n_z = min(16, n_space // n_c)
    n_y = n_space // (n_c * n_z)
    fine = Mesh(mesh.devices.reshape(n_y, n_z, n_c, n_x), ("y", "z", "c", "x"))
    space = ("y", "z", "c")
    group = ("y", "x", "c")
    chunks = n_y * n_x * n_c
    size = MAIN // chunks
    chunk_rows = size + -(-(-(-EXTRA // chunks)) // 8) * 8
    params = pltpu.CompilerParams(vmem_limit_bytes=VMEM_LIMIT)

    def on_device(latents, pairs, geometry, pair_count, cotangent, leaving, *weights):
        smem = pl.BlockSpec(memory_space=pltpu.SMEM)
        sent = jax.ShapeDtypeStruct((SENT, L), BF16)
        up, down = pl.pallas_call(
            pack_kernel,
            out_shape=(sent, sent),
            in_specs=[smem] + vmem(5),
            out_specs=tuple(vmem(2)),
            compiler_params=params,
            name="pack",
        )(pair_count, latents, cotangent, pairs, geometry, leaving)
        ring = range(n_space)
        low = lax.ppermute(up, space, [(i, (i + 1) % n_space) for i in ring])
        upp = lax.ppermute(down, space, [(i, (i - 1) % n_space) for i in ring])
        blocks = OWN_BLOCKS + NB_BLOCKS
        final, grad, arrivals, packed = pl.pallas_call(
            lambda *refs: main_kernel(chunks, *refs),
            out_shape=(
                jax.ShapeDtypeStruct((1, ROWS, L), BF16),
                jax.ShapeDtypeStruct((1, ROWS, L), F32),
                jax.ShapeDtypeStruct((1, 2, MIG, L), BF16),
                jax.ShapeDtypeStruct((chunks, chunk_rows, L), BF16),
            ),
            in_specs=[smem] + vmem(13),
            out_specs=tuple(vmem(4)),
            scratch_shapes=[
                pltpu.VMEM((blocks, BLK, BLK), BF16),
                pltpu.VMEM((blocks, BLK, BLK), BF16),
                pltpu.VMEM((blocks, BLK, BLK), BF16),
                pltpu.VMEM((blocks, BLK, BLK), BF16),
                pltpu.VMEM((blocks, BLK, L), F32),
                pltpu.VMEM((blocks, BLK, 8), BF16),
                pltpu.VMEM((OWN_BLOCKS, 8, BLK), BF16),
                pltpu.VMEM((2, blocks, BLK, 2 * L), F32),
                pltpu.VMEM((ROWS, 2 * L), F32),
                pltpu.VMEM((2 * ROWS, 2 * L), F32),
            ],
            compiler_params=params,
            name="steps",
        )(pair_count, latents, cotangent, pairs, geometry, low, upp, *weights)

        got = lax.all_to_all(packed, group, 0, 0, tiled=True)
        got = lax.all_to_all(fold(got, n_z), "z", 0, 0, tiled=True)
        got = lax.all_to_all(fold(got, chunks), group, 0, 0, tiled=True)

        grads = pl.pallas_call(
            lambda *refs: unpack_kernel(chunks, *refs),
            out_shape=tuple(jax.ShapeDtypeStruct(w.shape, F32) for w in weights),
            in_specs=vmem(1),
            out_specs=tuple(vmem(7)),
            compiler_params=params,
            name="unpack",
        )(got)
        return (final, grad, arrivals) + tuple(grads)

    return jax.shard_map(
        on_device,
        mesh=fine,
        in_specs=(
            P("x", space, None),
            P("x", None, space),
            P("x", None, space),
            P("x", space),
            P("x", space, None),
            P("x", space, None),
        )
        + (P(),) * 7,
        out_specs=(P("x", space, None), P("x", space, None), P("x", space, None, None)) + (P(),) * 7,
        check_vma=False,
    )
```

time: 693 us -> 112 us (0.16)
  waiting for transfers between devices: 363 us -> 0.84 us
  starting transfers between devices: 83 us -> 10.8 us
  other arithmetic: 64.6 us -> 0 us
  blocking collectives: 109 us -> 63.6 us
  local copies, waits for them, and re-layouts: 42 us -> 3.98 us
  Pallas kernels: 0 us -> 31.2 us
  matrix products: 14.2 us -> 0 us
  between operations: 15.5 us -> 1.44 us
    psum x1 -> x0, waiting for transfers between devices: 351 us -> none  [on_device(): stacked = lax.psum(stacked, ('space', 'replicas'))]
    psum x1 -> x0, blocking collectives: 109 us -> none  [on_device(): stacked = lax.psum(stacked, ('space', 'replicas'))]
    ppermute x18 -> x2, starting transfers between devices: 82.9 us -> 10.8 us  [the longest x1 5.9 us: on_device(): upp = lax.ppermute(down, space, [(i, (i - 1) % n_space) for i in ring])]
    all_to_all x0 -> x3, blocking collectives: none -> 63.6 us  [the longest x1 22.4 us: on_device(): got = lax.all_to_all(fold(got, n_z), 'z', 0, 0, tiled=True)]
    scatter-add x22 -> x0, other arithmetic: 54.4 us -> none  [the longest x8 27.3 us: back(): accum = accum.at[owned_rows].add(d_owned).at[other_rows].add(d_other)]
    pallas_call x0 -> x5, Pallas kernels: none -> 31.2 us  [the longest x1 30.2 us: on_device(): pl.pallas_call(lambda *refs: main_kernel(chunks, *refs), out_shape=(jax.S...]
    gather x26 -> x0, local copies, waits for them, and re-layouts: 30.9 us -> none  [the longest x8 10.7 us: edge_forward(): right_rows = jnp.take(rows_src, other_rows, axis=0)]
    dot_general x52 -> x0, matrix products: 14.2 us -> none  [the longest x8 2.13 us: edge_forward(): jnp.dot(x_fwd, weight_in, preferred_element_type=jnp.float32) + bias_in]
  transfers between devices with their start and end apart: 19 -> 2, of which waited for: 5 -> 1; matrix products, arithmetic and copies ran while one was open for 5% -> 0% of each run, Pallas kernels for 0% -> 0%
where the time goes in v1:
time: 112 us
  blocking collectives  63.6 us (57%)
  Pallas kernels  31.2 us (28%)
  starting transfers between devices  10.8 us (10%)
  local copies, waits for them, and re-layouts  3.98 us (4%)
  between operations  1.44 us (1%)
    pallas_call x1, Pallas kernels, on_device(): pl.pallas_call(lambda *refs: main_kernel(chunks, *refs), out_shape=(jax.S...  30.2 us
    all_to_all x1, blocking collectives, on_device(): got = lax.all_to_all(fold(got, n_z), 'z', 0, 0, tiled=True)  22.4 us
    all_to_all x1, blocking collectives, on_device(): got = lax.all_to_all(packed, group, 0, 0, tiled=True)  22.3 us
    all_to_all x1, blocking collectives, on_device(): got = lax.all_to_all(fold(got, chunks), group, 0, 0, tiled=True)  18.9 us
    ppermute x1, starting transfers between devices, on_device(): upp = lax.ppermute(down, space, [(i, (i - 1) % n_space) for i in ring])  5.9 us
    ppermute x1, starting transfers between devices, on_device(): low = lax.ppermute(up, space, [(i, (i + 1) % n_space) for i in ring])  4.94 us
    unnamed x26, local copies, waits for them, and re-layouts  3.98 us
  transfers between devices with their start and end apart: 2, of which 1 were waited for; matrix products, arithmetic and copies ran while one was open for 0% of the time, Pallas kernels for 0%

profile of v1, /device:TPU:1, one launch (start us, length us, event | category | flops | bytes accessed | tf_op | source)
XLA Modules:
  0.0 111.9 jit_solution(12763094984862024049)
XLA Ops:
  0.6 0.0 copy-start.7
  1.3 0.0 copy-done.7
  1.3 0.0 copy-start
  1.3 0.8 copy-done
  2.2 0.0 copy-start.1
  2.2 0.8 copy-done.1
  3.0 0.0 copy-start.5
  3.0 0.7 copy-done.5
  3.7 0.0 copy-start.6
  3.7 0.7 copy-done.6
  4.4 0.0 copy-start.11
  4.4 0.1 pack.1
  4.5 4.9 %collective-permute-start = (bf16[272,128]{1,0:T(8,128)(2,1)S(1)}, bf16[272,128]{1,0:T(8,128)(2,1)S(1)}, u32[]{:S(2)}, u32[]{:S(2)}) collective-permute-start(bf16[272,128]{1,0:T(8,128)(2,1)S(1)} %get-tuple-element.23), channel_id=1, source_target_pairs={{0,4},{4,8},{8,12},{12,16},{16,20},{20,24},{24,28},{28,32},{32,36}... | collective-permute-start | bytes 208904 | tf_op jit(solution)/shard_map/ppermute | solution.py:415
  9.4 0.0 copy-start.2
  9.4 0.0 copy-start.3
  9.4 0.0 copy-start.4
  9.4 0.0 copy-start.8
  9.5 0.0 copy-start.9
  9.5 0.0 copy-start.10
  9.5 5.9 %collective-permute-start.1 = (bf16[272,128]{1,0:T(8,128)(2,1)S(1)}, bf16[272,128]{1,0:T(8,128)(2,1)S(1)}, u32[]{:S(2)}, u32[]{:S(2)}) collective-permute-start(bf16[272,128]{1,0:T(8,128)(2,1)S(1)} %get-tuple-element.24), channel_id=1, source_target_pairs={{0,508},{4,0},{8,4},{12,8},{16,12},{20,16},{24,20},{28,24},{32,28}... | collective-permute-start | bytes 208904 | tf_op jit(solution)/shard_map/ppermute | solution.py:416
  15.4 0.0 copy-done.11
  15.4 0.0 collective-permute-done.refs_5_
  15.4 0.8 collective-permute-done.1.refs_6_
  16.3 0.0 copy-done.2
  16.3 0.0 copy-done.3
  16.3 0.0 copy-done.4
  16.3 0.0 copy-done.8
  16.3 0.0 copy-done.9
  16.3 0.0 copy-done.10
  16.3 30.2 %steps.1 = (bf16[1,256,128]{2,1,0:T(8,128)(2,1)}, f32[1,256,128]{2,1,0:T(8,128)}, bf16[1,2,16,128]{3,2,1,0:T(8,128)(2,1)}, bf16[32,56,128]{2,1,0:T(8,128)(2,1)S(1)}) custom-call(s32[1,1]{1,0:T(1,128)S(6)} %copy.25.count_ref.refs_0_, bf16[1,256,128]{2,1,0:T(8,128)(2,1)S(1)} %copy-done, bf16[1,256,128]{2,1,0:T(8,128)(2,1)S(1)} %copy-done.1, ...), custom_call_target="tpu_custom_call" | custom-call | tf_op jit(solution)/shard_map/steps/pallas_call | solution.py:418
  46.5 22.3 %all_to_all.15.a = bf16[32,56,128]{2,1,0:T(8,128)(2,1)S(1)} all-to-all(bf16[32,56,128]{2,1,0:T(8,128)(2,1)S(1)} %get-tuple-element.28), channel_id=1, replica_groups=mesh['y'=4,'z'=16,'c'=2,'x'=4] {'y','x','c'}, dimensions={0} | all-to-all | bytes 917504 | tf_op jit(solution)/shard_map/all_to_all | solution.py:444
  68.9 0.1 fold.2
  68.9 22.4 %all_to_all.16.a = bf16[16,56,128]{2,1,0:T(8,128)(2,1)S(1)} all-to-all(bf16[16,56,128]{2,1,0:T(8,128)(2,1)S(1)} %fold.2), channel_id=1, replica_groups=mesh['y'=4,'z'=16,'c'=2,'x'=4] {'z'}, dimensions={0} | all-to-all | bytes 458752 | tf_op jit(solution)/shard_map/all_to_all | solution.py:445
  91.4 18.9 %all_to_all.17.refs_0_ = bf16[32,56,128]{2,1,0:T(8,128)(2,1)S(1)} all-to-all(bf16[32,56,128]{2,1,0:T(8,128)(2,1)S(1)} %fold.3), channel_id=1, replica_groups=mesh['y'=4,'z'=16,'c'=2,'x'=4] {'y','x','c'}, dimensions={0} | all-to-all | bytes 917504 | tf_op jit(solution)/shard_map/all_to_all | solution.py:446
  110.3 0.8 unpack.1
  111.1 0.8 copy.24
  (2 shorter events, 0.1 us)
Async XLA Ops:
  0.6 0.7 copy-start.7
  1.3 0.8 copy-start
  2.2 0.8 copy-start.1
  3.0 0.7 copy-start.5
  3.7 0.7 copy-start.6
  4.4 11.0 %copy-start.11 = (bf16[2,260,128]{2,0,1:T(2,128)(2,1)S(1)}, bf16[2,260,128]{2,0,1:T(2,128)(2,1)}, u32[]{:S(2)}) copy-start(bf16[2,260,128]{2,0,1:T(2,128)(2,1)} %param.19) | copy-start | bytes 399364
  4.5 11.0 %collective-permute-start = (bf16[272,128]{1,0:T(8,128)(2,1)S(1)}, bf16[272,128]{1,0:T(8,128)(2,1)S(1)}, u32[]{:S(2)}, u32[]{:S(2)}) collective-permute-start(bf16[272,128]{1,0:T(8,128)(2,1)S(1)} %get-tuple-element.23), channel_id=1, source_target_pairs={{0,4},{4,8},{8,12},{12,16},{16,20},{20,24},{24,28},{28,32},{32,36}... | collective-permute-start | bytes 208904 | tf_op jit(solution)/shard_map/ppermute | solution.py:415
  9.4 6.9 %copy-start.2 = (bf16[2,256,128]{2,1,0:T(8,128)(2,1)S(1)}, bf16[2,256,128]{2,1,0:T(8,128)(2,1)}, u32[]{:S(2)}) copy-start(bf16[2,256,128]{2,1,0:T(8,128)(2,1)} %refs_10_.1) | copy-start | bytes 393220
  9.4 6.9 %copy-start.3 = (bf16[2,128,128]{2,1,0:T(8,128)(2,1)S(1)}, bf16[2,128,128]{2,1,0:T(8,128)(2,1)}, u32[]{:S(2)}) copy-start(bf16[2,128,128]{2,1,0:T(8,128)(2,1)} %refs_9_.1) | copy-start | bytes 196612
  9.4 6.9 %copy-start.4 = (bf16[2,128,128]{2,1,0:T(8,128)(2,1)S(1)}, bf16[2,128,128]{2,1,0:T(8,128)(2,1)}, u32[]{:S(2)}) copy-start(bf16[2,128,128]{2,1,0:T(8,128)(2,1)} %refs_12_.1) | copy-start | bytes 196612
  9.4 6.8 %copy-start.8 = (f32[2,128]{1,0:T(2,128)S(1)}, f32[2,128]{1,0:T(2,128)}, u32[]{:S(2)}) copy-start(f32[2,128]{1,0:T(2,128)} %refs_8_.1) | copy-start | bytes 3076
  9.5 6.8 %copy-start.9 = (f32[2,128]{1,0:T(2,128)S(1)}, f32[2,128]{1,0:T(2,128)}, u32[]{:S(2)}) copy-start(f32[2,128]{1,0:T(2,128)} %refs_11_.1) | copy-start | bytes 3076
  9.5 6.8 %copy-start.10 = (f32[2,128]{1,0:T(2,128)S(1)}, f32[2,128]{1,0:T(2,128)}, u32[]{:S(2)}) copy-start(f32[2,128]{1,0:T(2,128)} %refs_13_.1) | copy-start | bytes 3076
  9.5 6.8 %collective-permute-start.1 = (bf16[272,128]{1,0:T(8,128)(2,1)S(1)}, bf16[272,128]{1,0:T(8,128)(2,1)S(1)}, u32[]{:S(2)}, u32[]{:S(2)}) collective-permute-start(bf16[272,128]{1,0:T(8,128)(2,1)S(1)} %get-tuple-element.24), channel_id=1, source_target_pairs={{0,508},{4,0},{8,4},{12,8},{16,12},{20,16},{24,20},{28,24},{32,28}... | collective-permute-start | bytes 208904 | tf_op jit(solution)/shard_map/ppermute | solution.py:416

commit v2 on v1

v2 whole, which is shorter than its diff:
```python
import jax
import jax.numpy as jnp
from jax import lax
from jax.experimental import pallas as pl
from jax.experimental.pallas import tpu as pltpu
from jax.sharding import Mesh, PartitionSpec as P


F32 = jnp.float32
BF16 = jnp.bfloat16
L = 128
ROWS = 256
EMAX = 1024
BLK = 256
OWN_BLOCKS = EMAX // BLK
SIDE = 256
NB_BLK = 2 * SIDE
NB_BLOCKS = EMAX // SIDE
CHUNK = 64
LAT_HALO = 128
COT_HALO = 64
SENT = LAT_HALO + COT_HALO + 64 + 16
D_AT = LAT_HALO + COT_HALO
X_AT = D_AT + 64
MIG = 16
MAIN = 768
EXTRA = 7
EPS = 1e-05
VMEM_LIMIT = 48 * 1024 * 1024


def dot(a, b):
    return jnp.dot(a, b, preferred_element_type=F32)


def dot_nt(a, b):
    return lax.dot_general(a, b, (((1,), (1,)), ((), ())), preferred_element_type=F32)


def dot_tn(a, b):
    return lax.dot_general(a, b, (((0,), (0,)), ((), ())), preferred_element_type=F32)


def place(row):
    below = row < 0
    above = row >= ROWS
    out = jnp.where(below, -1 - row, row - ROWS)
    block = lax.shift_right_arithmetic(out, 5)
    inner = jnp.where(below, row + 32 * (block + 1), row - ROWS - 32 * block + 32)
    outside = jnp.logical_or(below, above)
    return jnp.where(outside, 64 * block + inner, row), outside


def masked(flag):
    return jnp.where(flag, 1.0, 0.0).astype(BF16)


def pack_kernel(
    count_ref, lat_ref, cot_ref, pairs_ref, geo_ref, leav_ref, a_ref, b_ref, pairs_v, geo_v, leav_v, sems
):
    first = lax.axis_index("c") == 0
    copies = [
        pltpu.make_async_copy(pairs_ref.at[0], pairs_v, sems.at[0]),
        pltpu.make_async_copy(geo_ref.at[0], geo_v, sems.at[1]),
        pltpu.make_async_copy(leav_ref.at[0], leav_v, sems.at[2]),
    ]
    ups = (first, jnp.logical_not(first))
    for k, ref in enumerate((a_ref, b_ref)):
        lat_at = pl.multiple_of(jnp.where(ups[k], ROWS - LAT_HALO, 0), LAT_HALO)
        cot_at = pl.multiple_of(jnp.where(ups[k], ROWS - COT_HALO, 0), COT_HALO)
        lat = lat_ref.at[0, pl.ds(lat_at, LAT_HALO), :]
        cot = cot_ref.at[0, pl.ds(cot_at, COT_HALO), :]
        copies.append(pltpu.make_async_copy(lat, ref.at[pl.ds(0, LAT_HALO), :], sems.at[3 + 2 * k]))
        copies.append(pltpu.make_async_copy(cot, ref.at[pl.ds(LAT_HALO, COT_HALO), :], sems.at[4 + 2 * k]))
    for copy in copies:
        copy.start()
    for copy in copies[:3]:
        copy.wait()

    live = lax.broadcasted_iota(jnp.int32, (1, EMAX), 1) < count_ref[...]
    own = pairs_v[0:1, :]
    other = pairs_v[1:2, :]
    geo = geo_v[...].astype(F32)
    leav = leav_v[...].astype(F32)
    rows, kinds = [], []
    for k in range(2):
        up = ups[k]
        shift = jnp.where(up, -32 - ROWS, ROWS - 32)
        i_row = own + shift
        j_row = other + shift
        far = jnp.where(up, -1 - jnp.maximum(i_row, j_row), jnp.minimum(i_row, j_row) - ROWS)
        kind = jnp.where(far < 0, 0, lax.shift_right_arithmetic(far, 5) + 1)
        kind = jnp.where(jnp.logical_and(live, kind < 4), kind, 4).astype(F32)
        i_at, _ = place(i_row)
        j_at, j_hi = place(j_row)
        keep = kind < 3.5
        i_at = jnp.where(keep, i_at + 1, 0).astype(F32)
        j_at = jnp.where(keep, j_at + 1, 0).astype(F32)
        hi = jnp.where(j_hi, 1.0, 0.0).astype(F32)
        rows.append(jnp.concatenate([i_at, j_at, hi, jnp.ones((1, EMAX), F32), geo], axis=0).astype(BF16))
        kinds.append(jnp.concatenate([kind[:, 128 * t : 128 * t + 128] for t in range(8)], axis=0))

    flags = [jnp.where(kinds[k] == c, 1.0, 0.0).astype(F32) for k in range(2) for c in range(4)]
    marks = jnp.concatenate(flags, axis=0).astype(BF16)
    row_i = lax.broadcasted_iota(jnp.int32, (128, 128), 0)
    col_i = lax.broadcasted_iota(jnp.int32, (128, 128), 1)
    inside = dot(marks, masked(row_i < col_i))
    sums = dot(marks, jnp.ones((128, 128), BF16))
    row_b = lax.broadcasted_iota(jnp.int32, (64, 64), 0)
    col_b = lax.broadcasted_iota(jnp.int32, (64, 64), 1)
    same = lax.shift_right_logical(row_b, 5) == lax.shift_right_logical(col_b, 5)
    before = dot(masked(jnp.logical_and(same, col_b < row_b)), sums.astype(BF16))
    at = inside + before
    lane = lax.broadcasted_iota(jnp.int32, (1, 128), 1)
    col_w = lax.broadcasted_iota(jnp.int32, (128, BLK), 1).astype(F32)
    for k, ref in enumerate((a_ref, b_ref)):
        up = ups[k]
        rank = jnp.full((8, 128), -1.0, F32)
        for c in range(4):
            here = 32 * k + 8 * c
            rank = jnp.where(kinds[k] == c, at[here : here + 8, :], rank)
        by_slot = jnp.transpose(rank)
        ends = [before[32 * k + 8 * c + 7, 0] + sums[32 * k + 8 * c + 7, 0] for c in range(4)]
        trips = lax.shift_right_logical(ends[3].astype(jnp.int32) + (BLK - 1), 8)
        ref[D_AT:X_AT, :] = jnp.zeros((X_AT - D_AT, L), BF16)

        def body(t, carry, ref=ref, by_slot=by_slot, source=rows[k]):
            wanted = col_w + (t * BLK).astype(F32)
            picks = [masked(by_slot[:, q : q + 1] == wanted) for q in range(8)]
            moved = dot(source, jnp.concatenate(picks, axis=0))
            spot = pl.multiple_of(D_AT + 16 * t, 16)
            ref[pl.ds(spot, 16), :] = jnp.concatenate([moved[:, :128], moved[:, 128:]], axis=0).astype(BF16)
            return carry

        lax.fori_loop(0, trips, body, 0)
        movers = jnp.where(up, leav[1:2, :] - 224.0, leav[0:1, :] + 32.0)
        tail = jnp.concatenate([movers, jnp.zeros((1, 128 - MIG), F32)], axis=1)
        for c in range(4):
            blocks = ((ends[c].astype(jnp.int32) + (SIDE - 1)) // SIDE).astype(F32)
            tail = jnp.where(lane == MIG + c, blocks, tail)
        ref[X_AT:SENT, :] = jnp.broadcast_to(tail, (16, 128)).astype(BF16)
    for copy in copies[3:]:
        copy.wait()


def main_kernel(
    chunks,
    count_ref,
    lat_ref,
    cot_ref,
    pairs_ref,
    geo_ref,
    a_ref,
    b_ref,
    edge_in_ref,
    edge_bias_ref,
    edge_out_ref,
    node_in_ref,
    node_bias_ref,
    node_out_ref,
    gain_ref,
    final_ref,
    grad_ref,
    arr_ref,
    keep_ref,
    send_ref,
    low_ref,
    upp_ref,
    own_oh,
    own_oht,
    own_hi,
    own_col,
    own_row,
    own_slope,
    nb_rows,
    nb_oh,
    nb_oht,
    nb_hi,
    nb_col,
    nb_slope,
    work_x,
    work_p,
    work_d,
    work_e,
    t_nb,
    q_nb,
    stage,
):
    first = lax.axis_index("c") == 0

    @pl.when(first)
    def _():
        low_ref[...] = b_ref[...]
        upp_ref[...] = a_ref[...]

    @pl.when(jnp.logical_not(first))
    def _():
        low_ref[...] = a_ref[...]
        upp_ref[...] = b_ref[...]

    def one_hots(rows, cols, size):
        lanes = lax.broadcasted_iota(jnp.int32, (size, BLK), 1).astype(F32) + 1.0
        subs = lax.broadcasted_iota(jnp.int32, (BLK, size), 0).astype(F32) + 1.0
        straight = [masked(cols[:, k : k + 1] == lanes) for k in range(2)]
        turned = [masked(rows[k : k + 1, :] == subs) for k in range(2)]
        return straight, turned

    live = lax.broadcasted_iota(jnp.int32, (1, EMAX), 1) < count_ref[...]
    i_at = pairs_ref[0, 0:1, :] - 32
    j_at, j_out = place(pairs_ref[0, 1:2, :] - 32)
    own_rows = jnp.concatenate(
        [
            jnp.where(live, i_at + 1, 0).astype(F32),
            jnp.where(live, j_at + 1, 0).astype(F32),
            jnp.where(j_out, 1.0, 0.0).astype(F32),
            jnp.ones((1, EMAX), F32),
            geo_ref[0].astype(F32),
        ],
        axis=0,
    )
    own_row[...] = own_rows.astype(BF16)
    for k in range(OWN_BLOCKS):
        here = slice(BLK * k, BLK * k + BLK)
        rows = own_rows[:, here]
        cols = jnp.transpose(rows)
        straight, turned = one_hots(rows, cols, BLK)
        for e in range(2):
            own_oh[e, here, :] = straight[e]
            own_oht[e, :, here] = turned[e]
        own_hi[here, :] = jnp.broadcast_to(cols[:, 2:3], (BLK, L))
        own_col[here, :] = cols.astype(BF16)

    info = jnp.maximum(low_ref[X_AT:SENT, :].astype(F32), upp_ref[X_AT:SENT, :].astype(F32))[0:1, :]
    lane = lax.broadcasted_iota(jnp.int32, (1, L), 1)
    reach = [jnp.sum(jnp.where(lane == MIG + c, info, 0.0)).astype(jnp.int32) for c in range(4)]
    low_rows = low_ref[D_AT:X_AT, :].astype(F32)
    upp_rows = upp_ref[D_AT:X_AT, :].astype(F32)
    for k in range(NB_BLOCKS):
        pieces = [v[r : r + 8] for v in (low_rows, upp_rows) for r in range(SIDE // 16 * k, SIDE // 16 * (k + 1), 8)]
        nb_rows[k] = jnp.concatenate(pieces, axis=1)

    def prepare(k, carry):
        rows = nb_rows[k]
        cols = jnp.transpose(rows)
        straight, turned = one_hots(rows, cols, NB_BLK)
        for e in range(2):
            nb_oh[e, k] = straight[e]
            nb_oht[e, k] = turned[e]
        nb_hi[k] = jnp.broadcast_to(cols[:, 2:3], (NB_BLK, L))
        nb_col[k] = cols.astype(BF16)
        return carry

    lax.fori_loop(0, reach[3], prepare, 0)

    def around(source_low, source_upp, width, height):
        parts = []
        for b in range(width // 32):
            parts.append(source_low[width - 32 * (b + 1) : width - 32 * b])
            parts.append(source_upp[32 * b : 32 * b + 32])
        if height > 2 * width:
            parts.append(jnp.zeros((height - 2 * width, L), parts[0].dtype))
        return jnp.concatenate(parts, axis=0)

    def edge_weights(layer):
        top = edge_in_ref[layer, 0:L, :]
        bottom = edge_in_ref[layer, L : 2 * L, :]
        straight = jnp.concatenate([top, bottom], axis=1)
        return straight, jnp.concatenate([bottom, top], axis=1)

    def forward_block(size, oh_i, oh_j, hi, col, slope, i_source, both, weights, geo_weights, bias):
        work_x[0:size, :L] = dot(oh_i, i_source).astype(BF16)
        work_p[0:size, :] = dot(oh_j, both)
        for r in range(0, size, CHUNK):
            here = slice(r, r + CHUNK)
            is_hi = hi[here, :] > 0.5
            work_x[here, L:] = jnp.where(is_hi, work_p[here, L:], work_p[here, :L]).astype(BF16)
        work_p[0:size, :] = dot(work_x[0:size, :], weights) + dot(col, geo_weights)
        for r in range(0, size, CHUNK):
            here = slice(r, r + CHUNK)
            pre = work_p[here, :] + bias
            sig = 0.5 * jnp.tanh(0.5 * pre) + 0.5
            act = pre * sig
            slope[here, :] = sig + act * (1.0 - sig)
            diff = act[:, :L] - act[:, L:]
            is_hi = hi[here, :] > 0.5
            none = jnp.zeros_like(diff)
            work_d[here, :L] = diff.astype(BF16)
            work_e[here, :L] = jnp.where(is_hi, none, diff).astype(BF16)
            work_e[here, L:] = jnp.where(is_hi, diff, none).astype(BF16)

    def edge_forward(layer, h_lo, h_hi, nb_blocks):
        straight, crossed = edge_weights(layer)
        weights = jnp.concatenate([straight, crossed], axis=0)
        geo_top = edge_in_ref[layer, 2 * L : 2 * L + 4, :].astype(F32)
        geo_weights = jnp.concatenate(
            [jnp.zeros((4, 2 * L), F32), jnp.concatenate([geo_top, -geo_top], axis=1)], axis=0
        ).astype(BF16)
        bias_row = edge_bias_ref[layer : layer + 1, :]
        bias = jnp.concatenate([bias_row, bias_row], axis=1)
        both = jnp.concatenate([h_lo, h_hi], axis=1)
        t_nb[...] = jnp.zeros_like(t_nb)

        def body(k, carry):
            forward_block(
                NB_BLK, nb_oh[0, k], nb_oh[1, k], nb_hi.at[k], nb_col[k], nb_slope.at[layer, k],
                h_hi, both, weights, geo_weights, bias,
            )
            by_j = dot(nb_oht[1, k], work_e[0:NB_BLK, :])
            t_nb[:, :L] += -by_j[:, :L]
            t_nb[:, L:] += dot(nb_oht[0, k], work_d[0:NB_BLK, :L]) - by_j[:, L:]
            return carry

        lax.fori_loop(0, nb_blocks, body, 0)
        forward_block(
            EMAX, own_oh[0], own_oh[1], own_hi, own_col[...], own_slope.at[layer],
            h_lo, both, weights, geo_weights, bias,
        )
        by_j = dot(own_oht[1], work_e[...])
        return dot(own_oht[0], work_d[:, :L]) - by_j[:, :L], -by_j[:, L:]

    def node_forward(layer, h, total):
        agg = dot(total.astype(BF16), edge_out_ref[layer]).astype(BF16)
        joined = jnp.concatenate([h, agg], axis=1)
        pre = dot(joined, node_in_ref[layer]) + node_bias_ref[layer : layer + 1, :]
        sig = 0.5 * jnp.tanh(0.5 * pre) + 0.5
        act = pre * sig
        hidden = act.astype(BF16)
        out = dot(hidden, node_out_ref[layer])
        centred = out - jnp.mean(out, axis=1, keepdims=True)
        inv = lax.rsqrt(jnp.mean(centred * centred, axis=1, keepdims=True) + EPS)
        normed = centred * inv
        new = (h.astype(F32) + normed * gain_ref[layer : layer + 1, :]).astype(BF16)
        return new, (joined, sig + act * (1.0 - sig), hidden, normed, inv)

    def node_backward(layer, grad, kept):
        size = grad.shape[0]
        joined, node_slope, hidden, normed, inv = (v[:size] for v in kept)
        gain_term = jnp.sum(grad[:ROWS] * normed[:ROWS], axis=0, keepdims=True)
        dnorm = grad * gain_ref[layer : layer + 1, :]
        mean_a = jnp.mean(dnorm, axis=1, keepdims=True)
        mean_b = jnp.mean(dnorm * normed, axis=1, keepdims=True)
        dout = ((dnorm - mean_a - normed * mean_b) * inv).astype(BF16)
        out_term = dot_tn(hidden[:ROWS], dout[:ROWS])
        dpre = (dot_nt(dout, node_out_ref[layer]) * node_slope).astype(BF16)
        in_term = dot_tn(joined[:ROWS], dpre[:ROWS])
        bias_term = jnp.sum(dpre[:ROWS].astype(F32), axis=0, keepdims=True)
        dx = dot_nt(dpre, node_in_ref[layer])
        return grad + dx[:, :L], dx[:, L:].astype(BF16), (in_term, bias_term, out_term, gain_term)

    def backward_block(size, oh_i, oh_j, hi, slope, i_source, both):
        work_p[0:size, :] = dot(oh_j, both)
        at_i = dot(oh_i, i_source)
        for r in range(0, size, CHUNK):
            here = slice(r, r + CHUNK)
            is_hi = hi[here, :] > 0.5
            dd = at_i[here, :] - jnp.where(is_hi, work_p[here, L:], work_p[here, :L])
            dfwd = dd * slope[here, :L]
            drev = -dd * slope[here, L:]
            none = jnp.zeros_like(dfwd)
            work_d[here, :L] = dfwd.astype(BF16)
            work_d[here, L:] = drev.astype(BF16)
            work_x[here, :L] = jnp.where(is_hi, none, drev).astype(BF16)
            work_x[here, L:] = jnp.where(is_hi, none, dfwd).astype(BF16)
            work_e[here, :L] = jnp.where(is_hi, drev, none).astype(BF16)
            work_e[here, L:] = jnp.where(is_hi, dfwd, none).astype(BF16)

    def edge_backward(layer, e_lo, e_hi, nb_blocks, with_hi):
        both = jnp.concatenate([e_lo, e_hi], axis=1)
        q_nb[...] = jnp.zeros_like(q_nb)

        def body(k, carry):
            backward_block(NB_BLK, nb_oh[0, k], nb_oh[1, k], nb_hi.at[k], nb_slope.at[layer, k], e_hi, both)
            q_nb[0:ROWS, :] += dot(nb_oht[1, k], work_x[0:NB_BLK, :])
            if with_hi:
                q_nb[ROWS:, :] += dot(nb_oht[1, k], work_e[0:NB_BLK, :]) + dot(nb_oht[0, k], work_d[0:NB_BLK, :])
            return carry

        lax.fori_loop(0, nb_blocks, body, 0)
        backward_block(EMAX, own_oh[0], own_oh[1], own_hi, own_slope.at[layer], e_lo, both)
        q_lo = dot(own_oht[0], work_d[...]) + dot(own_oht[1], work_x[...])
        q_hi = dot(own_oht[1], work_e[...])
        return q_lo, q_hi, dot(own_row[...], work_d[...])

    h0_lo = lat_ref[0]
    h0_hi = around(low_ref[0:LAT_HALO, :], upp_ref[0:LAT_HALO, :], LAT_HALO, ROWS)
    t0_lo, t0_hi = edge_forward(0, h0_lo, h0_hi, reach[3])
    total0 = jnp.concatenate([t0_lo + t_nb[:, :L], t0_hi + t_nb[:, L:]], axis=0)
    h0 = jnp.concatenate([h0_lo, h0_hi], axis=0)
    h1, kept0 = node_forward(0, h0, total0)
    t1_lo, t1_hi = edge_forward(1, h1[:ROWS], h1[ROWS:], reach[2])
    near = ROWS + 2 * COT_HALO
    total1 = jnp.concatenate([t1_lo + t_nb[:, :L], t1_hi[: near - ROWS] + t_nb[: near - ROWS, L:]], axis=0)
    h2, kept1 = node_forward(1, h1[:near], total1)
    final_ref[0] = h2[:ROWS]

    few = lax.broadcasted_iota(jnp.int32, (MIG, 2 * COT_HALO), 1).astype(F32)
    for k, ref in ((0, upp_ref), (1, low_ref)):
        movers = jnp.transpose(ref[X_AT:SENT, :].astype(F32))[0:MIG, 0:1]
        arr_ref[0, k] = dot(masked(movers == few), h2[ROWS:]).astype(BF16)

    def with_zeros(value):
        return jnp.concatenate([value, jnp.zeros((2 * ROWS - value.shape[0],) + value.shape[1:], value.dtype)], axis=0)

    def layer_back(layer, grad, kept, own_total, h, nb_blocks, keep_rows):
        part, dagg, node_terms = node_backward(layer, grad, kept)
        spread = with_zeros(dagg)
        e = with_zeros(dot_nt(dagg, edge_out_ref[layer]).astype(BF16))
        q_lo, q_hi, geo = edge_backward(layer, e[:ROWS], e[ROWS:], nb_blocks, keep_rows > ROWS)
        out_term = dot_tn(own_total.astype(BF16), spread)
        q_own = jnp.concatenate([q_lo, q_hi], axis=0)
        in_term = dot_tn(h, q_own.astype(BF16))
        straight, _ = edge_weights(layer)
        q_all = (q_own[:keep_rows] + q_nb[:keep_rows, :]).astype(BF16)
        new = part[:keep_rows] + dot_nt(q_all, straight)
        return new, (in_term, geo, out_term) + node_terms

    own1 = jnp.concatenate([t1_lo, t1_hi], axis=0)
    own0 = jnp.concatenate([t0_lo, t0_hi], axis=0)
    cot = jnp.concatenate(
        [cot_ref[0], around(low_ref[LAT_HALO:D_AT, :], upp_ref[LAT_HALO:D_AT, :], COT_HALO, 2 * COT_HALO)], axis=0
    ).astype(F32)
    grad1, terms1 = layer_back(1, cot, kept1, own1, h1, reach[1], ROWS + 64)
    grad0, terms0 = layer_back(0, grad1, kept0, own0, h0, reach[0], ROWS)
    grad_ref[0] = grad0

    size = MAIN // chunks
    per = -(-EXTRA // chunks)
    for layer, terms in enumerate((terms0, terms1)):
        in_term, geo, out_term, node_in_term, node_bias_term, node_out_term, gain_term = terms
        stage[layer, :, size:, :] = jnp.zeros((chunks, stage.shape[2] - size, L), BF16)
        at = 0
        for value in (in_term[:, :L], in_term[:, L:], out_term, node_in_term, node_out_term):
            value = value.astype(BF16)
            while value.shape[0]:
                take = min(value.shape[0], size - at % size)
                stage[layer, at // size, at % size : at % size + take, :] = value[:take]
                value = value[take:]
                at += take
        small = [geo[4 + g : 5 + g, :L] - geo[4 + g : 5 + g, L:] for g in range(4)]
        small += [geo[3:4, :L] + geo[3:4, L:], node_bias_term, gain_term]
        for extra, value in enumerate(small):
            spot = size + extra % per
            stage[layer, extra // per, spot : spot + 1, :] = value.astype(BF16)

    @pl.when(first)
    def _():
        keep_ref[...] = stage[0]
        send_ref[...] = stage[1]

    @pl.when(jnp.logical_not(first))
    def _():
        keep_ref[...] = stage[1]
        send_ref[...] = stage[0]


def fold_kernel(copies, in_ref, out_ref):
    total = in_ref[0].astype(F32)
    for k in range(1, in_ref.shape[0]):
        total += in_ref[k].astype(F32)
    total = total.astype(BF16)
    for k in range(copies):
        out_ref[k] = total


def fold(array, copies):
    return pl.pallas_call(
        lambda a, b: fold_kernel(copies, a, b),
        out_shape=jax.ShapeDtypeStruct((copies,) + array.shape[1:], BF16),
        in_specs=[pl.BlockSpec(memory_space=pltpu.VMEM)],
        out_specs=pl.BlockSpec(memory_space=pltpu.VMEM),
        compiler_params=pltpu.CompilerParams(vmem_limit_bytes=VMEM_LIMIT),
        name="fold",
    )(array)


def add_kernel(a_ref, b_ref, out_ref):
    out_ref[...] = (a_ref[...].astype(F32) + b_ref[...].astype(F32)).astype(BF16)


def add(a, b):
    return pl.pallas_call(
        add_kernel,
        out_shape=jax.ShapeDtypeStruct(a.shape, BF16),
        in_specs=vmem(2),
        out_specs=pl.BlockSpec(memory_space=pltpu.VMEM),
        compiler_params=pltpu.CompilerParams(vmem_limit_bytes=VMEM_LIMIT),
        name="add",
    )(a, b)


def unpack_kernel(chunks, mine_ref, other_ref, *outs):
    def write(layer, ref):
        edge_in, edge_bias, edge_out, node_in, node_bias, node_out, gain = outs
        size = MAIN // chunks
        per = -(-EXTRA // chunks)
        at = 0
        for out, rows in ((edge_in, 2 * L), (edge_out, L), (node_in, 2 * L), (node_out, L)):
            r = 0
            while r < rows:
                take = min(rows - r, size - at % size)
                out[layer, r : r + take, :] = ref[at // size, at % size : at % size + take, :].astype(F32)
                r += take
                at += take
        small = []
        for extra in range(EXTRA):
            spot = size + extra % per
            small.append(ref[extra // per, spot : spot + 1, :].astype(F32))
        edge_in[layer, 2 * L : 2 * L + 4, :] = jnp.concatenate(small[:4], axis=0)
        edge_bias[layer : layer + 1, :] = small[4]
        node_bias[layer : layer + 1, :] = small[5]
        gain[layer : layer + 1, :] = small[6]

    first = lax.axis_index("c") == 0

    @pl.when(first)
    def _():
        write(0, mine_ref)
        write(1, other_ref)

    @pl.when(jnp.logical_not(first))
    def _():
        write(1, mine_ref)
        write(0, other_ref)


def vmem(count):
    return [pl.BlockSpec(memory_space=pltpu.VMEM)] * count


def solution(mesh):
    n_space = mesh.shape["space"]
    n_x = mesh.shape["replicas"]
    n_c = 2
    n_z = min(16, n_space // n_c)
    n_y = n_space // (n_c * n_z)
    n_l = 2 if n_z > 4 else 1
    n_h = n_z // n_l
    fine = Mesh(mesh.devices.reshape(n_y, n_h, n_l, n_c, n_x), ("y", "zh", "zl", "c", "x"))
    space = ("y", "zh", "zl", "c")
    group = ("y", "zl", "x")
    chunks = n_y * n_l * n_x
    size = MAIN // chunks
    chunk_rows = size + -(-(-(-EXTRA // chunks)) // 8) * 8
    params = pltpu.CompilerParams(vmem_limit_bytes=VMEM_LIMIT)

    def on_device(latents, pairs, geometry, pair_count, cotangent, leaving, *weights):
        sent = jax.ShapeDtypeStruct((SENT, L), BF16)
        to_a, to_b = pl.pallas_call(
            pack_kernel,
            out_shape=(sent, sent),
            in_specs=vmem(1) + [pl.BlockSpec(memory_space=pl.ANY)] * 5,
            out_specs=tuple(vmem(2)),
            scratch_shapes=[
                pltpu.VMEM((2, EMAX), jnp.int32),
                pltpu.VMEM((4, EMAX), BF16),
                pltpu.VMEM((2, MIG), jnp.int32),
                pltpu.SemaphoreType.DMA((7,)),
            ],
            compiler_params=pltpu.CompilerParams(vmem_limit_bytes=60 * 1024 * 1024),
            name="pack",
        )(pair_count, latents, cotangent, pairs, geometry, leaving)
        half = range(n_space // 2)
        near = [(2 * i, 2 * i + 1) for i in half]
        cross = [(2 * i + 1, (2 * i + 2) % n_space) for i in half]
        from_a = lax.ppermute(to_a, space, near + [(j, i) for i, j in near])
        from_b = lax.ppermute(to_b, space, cross + [(j, i) for i, j in cross])
        final, grad, arrivals, keep, send = pl.pallas_call(
            lambda *refs: main_kernel(chunks, *refs),
            out_shape=(
                jax.ShapeDtypeStruct((1, ROWS, L), BF16),
                jax.ShapeDtypeStruct((1, ROWS, L), F32),
                jax.ShapeDtypeStruct((1, 2, MIG, L), BF16),
                jax.ShapeDtypeStruct((chunks, chunk_rows, L), BF16),
                jax.ShapeDtypeStruct((chunks, chunk_rows, L), BF16),
            ),
            in_specs=vmem(14),
            out_specs=tuple(vmem(5)),
            scratch_shapes=[
                pltpu.VMEM((SENT, L), BF16),
                pltpu.VMEM((SENT, L), BF16),
                pltpu.VMEM((2, EMAX, ROWS), BF16),
                pltpu.VMEM((2, ROWS, EMAX), BF16),
                pltpu.VMEM((EMAX, L), F32),
                pltpu.VMEM((EMAX, 8), BF16),
                pltpu.VMEM((8, EMAX), BF16),
                pltpu.VMEM((2, EMAX, 2 * L), F32),
                pltpu.VMEM((NB_BLOCKS, 8, NB_BLK), F32),
                pltpu.VMEM((2, NB_BLOCKS, NB_BLK, ROWS), BF16),
                pltpu.VMEM((2, NB_BLOCKS, ROWS, NB_BLK), BF16),
                pltpu.VMEM((NB_BLOCKS, NB_BLK, L), F32),
                pltpu.VMEM((NB_BLOCKS, NB_BLK, 8), BF16),
                pltpu.VMEM((2, NB_BLOCKS, NB_BLK, 2 * L), F32),
                pltpu.VMEM((EMAX, 2 * L), BF16),
                pltpu.VMEM((EMAX, 2 * L), F32),
                pltpu.VMEM((EMAX, 2 * L), BF16),
                pltpu.VMEM((EMAX, 2 * L), BF16),
                pltpu.VMEM((ROWS, 2 * L), F32),
                pltpu.VMEM((2 * ROWS, 2 * L), F32),
                pltpu.VMEM((2, chunks, chunk_rows, L), BF16),
            ],
            compiler_params=params,
            name="steps",
        )(pair_count, latents, cotangent, pairs, geometry, from_a, from_b, *weights)

        swap = [(0, 1), (1, 0)]
        got = add(keep, lax.ppermute(send, "c", swap))
        got = lax.all_to_all(got, group, 0, 0, tiled=True)
        got = lax.all_to_all(fold(got, n_h), "zh", 0, 0, tiled=True)
        got = lax.all_to_all(fold(got, chunks), group, 0, 0, tiled=True)

        grads = pl.pallas_call(
            lambda *refs: unpack_kernel(chunks, *refs),
            out_shape=tuple(jax.ShapeDtypeStruct(w.shape, F32) for w in weights),
            in_specs=vmem(2),
            out_specs=tuple(vmem(7)),
            compiler_params=params,
            name="unpack",
        )(got, lax.ppermute(got, "c", swap))
        return (final, grad, arrivals) + tuple(grads)

    return jax.shard_map(
        on_device,
        mesh=fine,
        in_specs=(
            P("x", space, None),
            P("x", None, space),
            P("x", None, space),
            P("x", space),
            P("x", space, None),
            P("x", space, None),
        )
        + (P(),) * 7,
        out_specs=(P("x", space, None), P("x", space, None), P("x", space, None, None)) + (P(),) * 7,
        check_vma=False,
    )
```

time: 112 us -> 97.8 us (0.87)
  blocking collectives: 63.6 us -> 46.4 us
  starting transfers between devices: 10.8 us -> 24.3 us
  Pallas kernels: 31.2 us -> 18.1 us
  waiting for transfers between devices: 0.84 us -> 5.25 us
  local copies, waits for them, and re-layouts: 3.98 us -> 1.82 us
    pallas_call x1, Pallas kernels: 30.2 us -> 14.3 us  [on_device(): pl.pallas_call(lambda *refs: main_kernel(chunks, *refs), out_shape=(jax.S...]
    ppermute x2 -> x4, starting transfers between devices: 10.8 us -> 24.3 us  [the longest x1 8.79 us: on_device(): from_a = lax.ppermute(to_a, space, near + [(j, i) for i, j in near])]
    all_to_all x2, blocking collectives: 44.7 us -> 34 us  [the longest x1 19.9 us: on_device(): got = lax.all_to_all(fold(got, n_h), 'zh', 0, 0, tiled=True)]
    all_to_all x1, blocking collectives: 18.9 us -> 12.4 us  [on_device(): got = lax.all_to_all(fold(got, chunks), group, 0, 0, tiled=True)]
    ppermute x2 -> x4, waiting for transfers between devices: 0.84 us -> 5.25 us  [the longest x1 2.97 us: on_device(): from_b = lax.ppermute(to_b, space, cross + [(j, i) for i, j in cross])]
    pallas_call x1 -> x2, Pallas kernels: 0.06 us -> 2.87 us  [the longest x1 2.8 us: on_device(): pl.pallas_call(pack_kernel, out_shape=(sent, sent), in_specs=vmem(1) + [p...]
    unnamed x26 -> x22, local copies, waits for them, and re-layouts: 3.98 us -> 1.82 us
  transfers between devices with their start and end apart: 2 -> 4, of which waited for: 1 -> 3; matrix products, arithmetic and copies ran while one was open for 0% -> 1% of each run, Pallas kernels for 0% -> 0%
where the time goes in v2:
time: 97.8 us; the launch traced here: 97.3 us
  blocking collectives  46.4 us (47%)
  starting transfers between devices  24.3 us (25%)
  Pallas kernels  18.1 us (19%)
  waiting for transfers between devices  5.25 us (5%)
  local copies, waits for them, and re-layouts  1.82 us (2%)
  between operations  1.49 us (2%)
    all_to_all x1, blocking collectives, on_device(): got = lax.all_to_all(fold(got, n_h), 'zh', 0, 0, tiled=True)  19.9 us
    pallas_call x1, Pallas kernels, on_device(): pl.pallas_call(lambda *refs: main_kernel(chunks, *refs), out_shape=(jax.S...  14.3 us
    all_to_all x1, blocking collectives, on_device(): got = lax.all_to_all(got, group, 0, 0, tiled=True)  14.1 us
    all_to_all x1, blocking collectives, on_device(): got = lax.all_to_all(fold(got, chunks), group, 0, 0, tiled=True)  12.4 us
    ppermute x1, starting transfers between devices, on_device(): from_a = lax.ppermute(to_a, space, near + [(j, i) for i, j in near])  8.79 us
    ppermute x1, starting transfers between devices, on_device(): got = add(keep, lax.ppermute(send, 'c', swap))  7.6 us
    ppermute x1, starting transfers between devices, on_device(): lax.ppermute(got, 'c', swap)  5.87 us
    ppermute x1, waiting for transfers between devices, on_device(): from_b = lax.ppermute(to_b, space, cross + [(j, i) for i, j in cross])  2.97 us
  transfers between devices with their start and end apart: 4, of which 3 were waited for; matrix products, arithmetic and copies ran while one was open for 1% of the time, Pallas kernels for 0%

profile of v2, /device:TPU:1, one launch (start us, length us, event | category | flops | bytes accessed | tf_op | source)
XLA Modules:
  0.0 97.3 jit_solution(16298347935567451632)
XLA Ops:
  1.3 0.0 copy-start.3
  1.3 0.0 copy-start.4
  1.3 0.0 copy-start.5
  1.3 0.0 copy-start.6
  1.3 2.8 %pack.1 = (bf16[272,128]{1,0:T(8,128)(2,1)}, bf16[272,128]{1,0:T(8,128)(2,1)}) custom-call(s32[1,1]{1,0:T(1,128)S(6)} %copy.25.count_ref.refs_0_, bf16[1,256,128]{2,1,0:T(8,128)(2,1)} %refs_1_.1, bf16[1,256,128]{2,1,0:T(8,128)(2,1)} %refs_2_.1, s32[1,2,1024]{2,1,0:T(2,128)} %refs_3_.1, bf16[1,4,1024]{2,1,0:T(4,128)(2,1)} %refs_4_.1, s32[1,2,16]{2,1,0:T(2,128)} %leav_ref.1), custom_call_target="tpu_custom_call" | custom-call | tf_op jit(solution)/shard_map/pack/pallas_call | solution.py:548
  4.1 8.8 %collective-permute-start = (bf16[272,128]{1,0:T(8,128)(2,1)}, bf16[272,128]{1,0:T(8,128)(2,1)S(1)}, u32[]{:S(2)}, u32[]{:S(2)}) collective-permute-start(bf16[272,128]{1,0:T(8,128)(2,1)} %get-tuple-element.24), channel_id=1, source_target_pairs={{0,4},{8,12},{16,20},{24,28},{32,36},{40,44},{48,52},{56,60},{64,6... | collective-permute-start | bytes 208904 | tf_op jit(solution)/shard_map/ppermute | solution.py:565
  12.9 0.0 copy-start
  12.9 0.0 copy-start.1
  13.0 0.0 copy-start.2
  13.0 0.0 copy-start.7
  13.0 0.0 copy-start.8
  13.0 0.0 copy-start.9
  13.0 2.1 %collective-permute-start.1 = (bf16[272,128]{1,0:T(8,128)(2,1)}, bf16[272,128]{1,0:T(8,128)(2,1)S(1)}, u32[]{:S(2)}, u32[]{:S(2)}) collective-permute-start(bf16[272,128]{1,0:T(8,128)(2,1)} %get-tuple-element.25), channel_id=1, source_target_pairs={{4,8},{12,16},{20,24},{28,32},{36,40},{44,48},{52,56},{60,64},{68,... | collective-permute-start | bytes 208904 | tf_op jit(solution)/shard_map/ppermute | solution.py:566
  15.1 0.9 copy.23.refs_7_
  16.0 0.0 collective-permute-done.refs_5_
  16.0 3.0 %collective-permute-done.1.refs_6_ = bf16[272,128]{1,0:T(8,128)(2,1)S(1)} collective-permute-done((bf16[272,128]{1,0:T(8,128)(2,1)}, bf16[272,128]{1,0:T(8,128)(2,1)S(1)}, u32[]{:S(2)}, u32[]{:S(2)}) %collective-permute-start.1) | collective-permute-done | bytes 69664 | tf_op jit(solution)/shard_map/ppermute | solution.py:566
  19.0 0.0 copy-done.3
  19.0 0.0 copy-done.4
  19.0 0.0 copy-done.5
  19.0 0.0 copy-done.6
  19.0 0.0 copy-done
  19.0 0.0 copy-done.1
  19.0 0.0 copy-done.2
  19.0 0.0 copy-done.7
  19.0 0.0 copy-done.8
  19.0 0.0 copy-done.9
  19.1 14.3 %steps.1 = (bf16[1,256,128]{2,1,0:T(8,128)(2,1)}, f32[1,256,128]{2,1,0:T(8,128)}, bf16[1,2,16,128]{3,2,1,0:T(8,128)(2,1)}, bf16[32,32,128]{2,1,0:T(8,128)(2,1)S(1)}, bf16[32,32,128]{2,1,0:T(8,128)(2,1)S(1)}) custom-call(s32[1,1]{1,0:T(1,128)S(6)} %copy.25.count_ref.refs_0_, bf16[1,256,128]{2,1,0:T(8,128)(2,1)S(1)} %copy-done, ...), custom_call_target="tpu_custom_call" | custom-call | tf_op jit(solution)/shard_map/steps/pallas_call | solution.py:567
  33.3 7.6 %collective-permute-start.2 = (bf16[32,32,128]{2,1,0:T(8,128)(2,1)S(1)}, bf16[32,32,128]{2,1,0:T(8,128)(2,1)S(1)}, u32[]{:S(2)}, u32[]{:S(2)}) collective-permute-start(bf16[32,32,128]{2,1,0:T(8,128)(2,1)S(1)} %get-tuple-element.30), channel_id=1, source_target_pairs={{0,4},{4,0},{1,5},{5,1},{2,6},{6,2},{3,7},{7,3},{8,12},{12,8},{9,1... | collective-permute-start | bytes 786440 | tf_op jit(solution)/shard_map/ppermute | solution.py:606
  40.9 1.1 %collective-permute-done.2.b_ref = bf16[32,32,128]{2,1,0:T(8,128)(2,1)S(1)} collective-permute-done((bf16[32,32,128]{2,1,0:T(8,128)(2,1)S(1)}, bf16[32,32,128]{2,1,0:T(8,128)(2,1)S(1)}, u32[]{:S(2)}, u32[]{:S(2)}) %collective-permute-start.2) | collective-permute-done | bytes 262176 | tf_op jit(solution)/shard_map/ppermute | solution.py:606
  42.1 0.1 add.1
  42.2 14.1 %all_to_all.15.a = bf16[32,32,128]{2,1,0:T(8,128)(2,1)S(1)} all-to-all(bf16[32,32,128]{2,1,0:T(8,128)(2,1)S(1)} %add.1), channel_id=1, replica_groups=mesh['y'=4,'zh'=8,'zl'=2,'c'=2,'x'=4] {'y','zl','x'}, dimensions={0} | all-to-all | bytes 524288 | tf_op jit(solution)/shard_map/all_to_all | solution.py:607
  56.3 19.9 %all_to_all.16.a = bf16[8,32,128]{2,1,0:T(8,128)(2,1)S(1)} all-to-all(bf16[8,32,128]{2,1,0:T(8,128)(2,1)S(1)} %fold.2), channel_id=1, replica_groups=mesh['y'=4,'zh'=8,'zl'=2,'c'=2,'x'=4] {'zh'}, dimensions={0} | all-to-all | bytes 131072 | tf_op jit(solution)/shard_map/all_to_all | solution.py:608
  76.2 12.4 %all_to_all.17.refs_0_ = bf16[32,32,128]{2,1,0:T(8,128)(2,1)S(1)} all-to-all(bf16[32,32,128]{2,1,0:T(8,128)(2,1)S(1)} %fold.3), channel_id=1, replica_groups=mesh['y'=4,'zh'=8,'zl'=2,'c'=2,'x'=4] {'y','zl','x'}, dimensions={0} | all-to-all | bytes 524288 | tf_op jit(solution)/shard_map/all_to_all | solution.py:609
  88.6 5.9 %collective-permute-start.3 = (bf16[32,32,128]{2,1,0:T(8,128)(2,1)S(1)}, bf16[32,32,128]{2,1,0:T(8,128)(2,1)S(1)}, u32[]{:S(2)}, u32[]{:S(2)}) collective-permute-start(bf16[32,32,128]{2,1,0:T(8,128)(2,1)S(1)} %all_to_all.17.refs_0_), channel_id=1, source_target_pairs={{0,4},{4,0},{1,5},{5,1},{2,6},{6,2},{3,7},{7,3},{8,12},{12,8},{9,1... | collective-permute-start | bytes 786440 | tf_op jit(solution)/shard_map/ppermute | solution.py:618
  94.5 1.1 %collective-permute-done.3.refs_1_ = bf16[32,32,128]{2,1,0:T(8,128)(2,1)S(1)} collective-permute-done((bf16[32,32,128]{2,1,0:T(8,128)(2,1)S(1)}, bf16[32,32,128]{2,1,0:T(8,128)(2,1)S(1)}, u32[]{:S(2)}, u32[]{:S(2)}) %collective-permute-start.3) | collective-permute-done | bytes 262176 | tf_op jit(solution)/shard_map/ppermute | solution.py:618
  95.7 0.8 unpack.1
  96.5 0.8 copy.24
  (2 shorter events, 0.1 us)
Async XLA Ops:
  1.3 17.7 %copy-start.3 = (bf16[2,128,128]{2,1,0:T(8,128)(2,1)S(1)}, bf16[2,128,128]{2,1,0:T(8,128)(2,1)}, u32[]{:S(2)}) copy-start(bf16[2,128,128]{2,1,0:T(8,128)(2,1)} %refs_9_.1) | copy-start | bytes 196612
  1.3 17.7 %copy-start.4 = (bf16[2,128,128]{2,1,0:T(8,128)(2,1)S(1)}, bf16[2,128,128]{2,1,0:T(8,128)(2,1)}, u32[]{:S(2)}) copy-start(bf16[2,128,128]{2,1,0:T(8,128)(2,1)} %refs_12_.1) | copy-start | bytes 196612
  1.3 17.7 %copy-start.5 = (s32[1,2,1024]{2,1,0:T(2,128)S(1)}, s32[1,2,1024]{2,1,0:T(2,128)}, u32[]{:S(2)}) copy-start(s32[1,2,1024]{2,1,0:T(2,128)} %refs_3_.1) | copy-start | bytes 24580
  1.3 17.7 %copy-start.6 = (bf16[1,4,1024]{2,1,0:T(4,128)(2,1)S(1)}, bf16[1,4,1024]{2,1,0:T(4,128)(2,1)}, u32[]{:S(2)}) copy-start(bf16[1,4,1024]{2,1,0:T(4,128)(2,1)} %refs_4_.1) | copy-start | bytes 24580
  4.1 11.9 %collective-permute-start = (bf16[272,128]{1,0:T(8,128)(2,1)}, bf16[272,128]{1,0:T(8,128)(2,1)S(1)}, u32[]{:S(2)}, u32[]{:S(2)}) collective-permute-start(bf16[272,128]{1,0:T(8,128)(2,1)} %get-tuple-element.24), channel_id=1, source_target_pairs={{0,4},{8,12},{16,20},{24,28},{32,36},{40,44},{48,52},{56,60},{64,6... | collective-permute-start | bytes 208904 | tf_op jit(solution)/shard_map/ppermute | solution.py:565
  12.9 6.1 %copy-start = (bf16[1,256,128]{2,1,0:T(8,128)(2,1)S(1)}, bf16[1,256,128]{2,1,0:T(8,128)(2,1)}, u32[]{:S(2)}) copy-start(bf16[1,256,128]{2,1,0:T(8,128)(2,1)} %refs_1_.1) | copy-start | bytes 196612
  12.9 6.1 %copy-start.1 = (bf16[1,256,128]{2,1,0:T(8,128)(2,1)S(1)}, bf16[1,256,128]{2,1,0:T(8,128)(2,1)}, u32[]{:S(2)}) copy-start(bf16[1,256,128]{2,1,0:T(8,128)(2,1)} %refs_2_.1) | copy-start | bytes 196612
  13.0 6.1 %copy-start.2 = (bf16[2,256,128]{2,1,0:T(8,128)(2,1)S(1)}, bf16[2,256,128]{2,1,0:T(8,128)(2,1)}, u32[]{:S(2)}) copy-start(bf16[2,256,128]{2,1,0:T(8,128)(2,1)} %refs_10_.1) | copy-start | bytes 393220
  13.0 6.1 %copy-start.7 = (f32[2,128]{1,0:T(2,128)S(1)}, f32[2,128]{1,0:T(2,128)}, u32[]{:S(2)}) copy-start(f32[2,128]{1,0:T(2,128)} %refs_8_.1) | copy-start | bytes 3076
  13.0 6.1 %copy-start.8 = (f32[2,128]{1,0:T(2,128)S(1)}, f32[2,128]{1,0:T(2,128)}, u32[]{:S(2)}) copy-start(f32[2,128]{1,0:T(2,128)} %refs_11_.1) | copy-start | bytes 3076
  13.0 6.1 %copy-start.9 = (f32[2,128]{1,0:T(2,128)S(1)}, f32[2,128]{1,0:T(2,128)}, u32[]{:S(2)}) copy-start(f32[2,128]{1,0:T(2,128)} %refs_13_.1) | copy-start | bytes 3076
  13.0 6.0 %collective-permute-start.1 = (bf16[272,128]{1,0:T(8,128)(2,1)}, bf16[272,128]{1,0:T(8,128)(2,1)S(1)}, u32[]{:S(2)}, u32[]{:S(2)}) collective-permute-start(bf16[272,128]{1,0:T(8,128)(2,1)} %get-tuple-element.25), channel_id=1, source_target_pairs={{4,8},{12,16},{20,24},{28,32},{36,40},{44,48},{52,56},{60,64},{68,... | collective-permute-start | bytes 208904 | tf_op jit(solution)/shard_map/ppermute | solution.py:566
  33.3 8.7 %collective-permute-start.2 = (bf16[32,32,128]{2,1,0:T(8,128)(2,1)S(1)}, bf16[32,32,128]{2,1,0:T(8,128)(2,1)S(1)}, u32[]{:S(2)}, u32[]{:S(2)}) collective-permute-start(bf16[32,32,128]{2,1,0:T(8,128)(2,1)S(1)} %get-tuple-element.30), channel_id=1, source_target_pairs={{0,4},{4,0},{1,5},{5,1},{2,6},{6,2},{3,7},{7,3},{8,12},{12,8},{9,1... | collective-permute-start | bytes 786440 | tf_op jit(solution)/shard_map/ppermute | solution.py:606
  88.6 7.0 %collective-permute-start.3 = (bf16[32,32,128]{2,1,0:T(8,128)(2,1)S(1)}, bf16[32,32,128]{2,1,0:T(8,128)(2,1)S(1)}, u32[]{:S(2)}, u32[]{:S(2)}) collective-permute-start(bf16[32,32,128]{2,1,0:T(8,128)(2,1)S(1)} %all_to_all.17.refs_0_), channel_id=1, source_target_pairs={{0,4},{4,0},{1,5},{5,1},{2,6},{6,2},{3,7},{7,3},{8,12},{12,8},{9,1... | collective-permute-start | bytes 786440 | tf_op jit(solution)/shard_map/ppermute | solution.py:618

commit v3 on v2

--- a/solution.py
+++ b/solution.py
@@ -13,9 +13,10 @@
 EMAX = 1024
 BLK = 256
 OWN_BLOCKS = EMAX // BLK
-SIDE = 256
-NB_BLK = 2 * SIDE
+SIDE = 128
 NB_BLOCKS = EMAX // SIDE
+ALL_PAIRS = EMAX + 2 * EMAX
+SURE = (1, 2, 3, 4)
 CHUNK = 64
 LAT_HALO = 128
 COT_HALO = 64
@@ -166,22 +167,18 @@
     send_ref,
     low_ref,
     upp_ref,
-    own_oh,
-    own_oht,
-    own_hi,
-    own_col,
+    oh,
+    oht,
+    hi,
+    col,
     own_row,
-    own_slope,
+    slope,
     nb_rows,
-    nb_oh,
-    nb_oht,
-    nb_hi,
-    nb_col,
-    nb_slope,
     work_x,
     work_p,
     work_d,
     work_e,
+    work_s,
     t_nb,
     q_nb,
     stage,
@@ -198,12 +195,8 @@
         low_ref[...] = a_ref[...]
         upp_ref[...] = b_ref[...]
 
-    def one_hots(rows, cols, size):
-        lanes = lax.broadcasted_iota(jnp.int32, (size, BLK), 1).astype(F32) + 1.0
-        subs = lax.broadcasted_iota(jnp.int32, (BLK, size), 0).astype(F32) + 1.0
-        straight = [masked(cols[:, k : k + 1] == lanes) for k in range(2)]
-        turned = [masked(rows[k : k + 1, :] == subs) for k in range(2)]
-        return straight, turned
+    lanes = lax.broadcasted_iota(jnp.int32, (BLK, ROWS), 1).astype(F32) + 1.0
+    subs = lax.broadcasted_iota(jnp.int32, (ROWS, BLK), 0).astype(F32) + 1.0
 
     live = lax.broadcasted_iota(jnp.int32, (1, EMAX), 1) < count_ref[...]
     i_at = pairs_ref[0, 0:1, :] - 32
@@ -219,16 +212,18 @@
         axis=0,
     )
     own_row[...] = own_rows.astype(BF16)
+
+    def prepare(at, rows):
+        here = pl.ds(at, BLK)
+        cols = jnp.transpose(rows)
+        for e in range(2):
+            oh[e, here, :] = masked(cols[:, e : e + 1] == lanes)
+            oht[e, :, here] = masked(rows[e : e + 1, :] == subs)
+        hi[here, :] = jnp.broadcast_to(cols[:, 2:3], (BLK, L))
+        col[here, :] = cols.astype(BF16)
+
     for k in range(OWN_BLOCKS):
-        here = slice(BLK * k, BLK * k + BLK)
-        rows = own_rows[:, here]
-        cols = jnp.transpose(rows)
-        straight, turned = one_hots(rows, cols, BLK)
-        for e in range(2):
-            own_oh[e, here, :] = straight[e]
-            own_oht[e, :, here] = turned[e]
-        own_hi[here, :] = jnp.broadcast_to(cols[:, 2:3], (BLK, L))
-        own_col[here, :] = cols.astype(BF16)
+        prepare(BLK * k, own_rows[:, BLK * k : BLK * k + BLK])
 
     info = jnp.maximum(low_ref[X_AT:SENT, :].astype(F32), upp_ref[X_AT:SENT, :].astype(F32))[0:1, :]
     lane = lax.broadcasted_iota(jnp.int32, (1, L), 1)
@@ -236,21 +231,18 @@
     low_rows = low_ref[D_AT:X_AT, :].astype(F32)
     upp_rows = upp_ref[D_AT:X_AT, :].astype(F32)
     for k in range(NB_BLOCKS):
-        pieces = [v[r : r + 8] for v in (low_rows, upp_rows) for r in range(SIDE // 16 * k, SIDE // 16 * (k + 1), 8)]
-        nb_rows[k] = jnp.concatenate(pieces, axis=1)
-
-    def prepare(k, carry):
-        rows = nb_rows[k]
-        cols = jnp.transpose(rows)
-        straight, turned = one_hots(rows, cols, NB_BLK)
-        for e in range(2):
-            nb_oh[e, k] = straight[e]
-            nb_oht[e, k] = turned[e]
-        nb_hi[k] = jnp.broadcast_to(cols[:, 2:3], (NB_BLK, L))
-        nb_col[k] = cols.astype(BF16)
-        return carry
-
-    lax.fori_loop(0, reach[3], prepare, 0)
+        nb_rows[k] = jnp.concatenate([low_rows[8 * k : 8 * k + 8], upp_rows[8 * k : 8 * k + 8]], axis=1)
+    for k in range(SURE[3]):
+        prepare(EMAX + BLK * k, nb_rows[k])
+
+    def further(last, body):
+        def step(k, carry):
+            body(pl.multiple_of(EMAX + BLK * k, BLK))
+            return carry
+
+        lax.fori_loop(SURE[last], reach[last], step, 0)
+
+    further(3, lambda at: prepare(at, nb_rows[(at - EMAX) // BLK]))
 
     def around(source_low, source_upp, width, height):
         parts = []
@@ -267,20 +259,25 @@
         straight = jnp.concatenate([top, bottom], axis=1)
         return straight, jnp.concatenate([bottom, top], axis=1)
 
-    def forward_block(size, oh_i, oh_j, hi, col, slope, i_source, both, weights, geo_weights, bias):
-        work_x[0:size, :L] = dot(oh_i, i_source).astype(BF16)
-        work_p[0:size, :] = dot(oh_j, both)
-        for r in range(0, size, CHUNK):
-            here = slice(r, r + CHUNK)
+    def chunks_of(at, size):
+        return [pl.ds(at + r, CHUNK) for r in range(0, size, CHUNK)]
+
+    def forward_rows(layer, parts, both, weights, geo_weights, bias):
+        for at, size, source in parts:
+            work_x[pl.ds(at, size), :L] = dot(oh[0, pl.ds(at, size), :], source).astype(BF16)
+        at = parts[0][0]
+        size = sum(part[1] for part in parts)
+        rows = pl.ds(at, size)
+        work_p[rows, :] = dot(oh[1, rows, :], both)
+        for here in chunks_of(at, size):
             is_hi = hi[here, :] > 0.5
             work_x[here, L:] = jnp.where(is_hi, work_p[here, L:], work_p[here, :L]).astype(BF16)
-        work_p[0:size, :] = dot(work_x[0:size, :], weights) + dot(col, geo_weights)
-        for r in range(0, size, CHUNK):
-            here = slice(r, r + CHUNK)
+        work_p[rows, :] = dot(work_x[rows, :], weights) + dot(col[rows, :], geo_weights)
+        for here in chunks_of(at, size):
             pre = work_p[here, :] + bias
             sig = 0.5 * jnp.tanh(0.5 * pre) + 0.5
             act = pre * sig
-            slope[here, :] = sig + act * (1.0 - sig)
+            slope[layer, here, :] = sig + act * (1.0 - sig)
             diff = act[:, :L] - act[:, L:]
             is_hi = hi[here, :] > 0.5
             none = jnp.zeros_like(diff)
@@ -288,7 +285,7 @@
             work_e[here, :L] = jnp.where(is_hi, none, diff).astype(BF16)
             work_e[here, L:] = jnp.where(is_hi, diff, none).astype(BF16)
 
-    def edge_forward(layer, h_lo, h_hi, nb_blocks):
+    def edge_forward(layer, h_lo, h_hi, last):
         straight, crossed = edge_weights(layer)
         weights = jnp.concatenate([straight, crossed], axis=0)
         geo_top = edge_in_ref[layer, 2 * L : 2 * L + 4, :].astype(F32)
@@ -300,23 +297,25 @@
         both = jnp.concatenate([h_lo, h_hi], axis=1)
         t_nb[...] = jnp.zeros_like(t_nb)
 
-        def body(k, carry):
-            forward_block(
-                NB_BLK, nb_oh[0, k], nb_oh[1, k], nb_hi.at[k], nb_col[k], nb_slope.at[layer, k],
-                h_hi, both, weights, geo_weights, bias,
-            )
-            by_j = dot(nb_oht[1, k], work_e[0:NB_BLK, :])
+        def collect(at, size):
+            rows = pl.ds(at, size)
+            by_j = dot(oht[1, :, rows], work_e[rows, :])
+            return dot(oht[0, :, rows], work_d[rows, :L]), by_j
+
+        def more(at):
+            forward_rows(layer, [(at, BLK, h_hi)], both, weights, geo_weights, bias)
+            by_i, by_j = collect(at, BLK)
             t_nb[:, :L] += -by_j[:, :L]
-            t_nb[:, L:] += dot(nb_oht[0, k], work_d[0:NB_BLK, :L]) - by_j[:, L:]
-            return carry
-
-        lax.fori_loop(0, nb_blocks, body, 0)
-        forward_block(
-            EMAX, own_oh[0], own_oh[1], own_hi, own_col[...], own_slope.at[layer],
-            h_lo, both, weights, geo_weights, bias,
-        )
-        by_j = dot(own_oht[1], work_e[...])
-        return dot(own_oht[0], work_d[:, :L]) - by_j[:, :L], -by_j[:, L:]
+            t_nb[:, L:] += by_i - by_j[:, L:]
+
+        further(last, more)
+        sure = BLK * SURE[last]
+        forward_rows(layer, [(0, EMAX, h_lo), (EMAX, sure, h_hi)], both, weights, geo_weights, bias)
+        by_i, by_j = collect(0, EMAX)
+        nb_i, nb_j = collect(EMAX, sure)
+        own = (by_i - by_j[:, :L], -by_j[:, L:])
+        total = (own[0] - nb_j[:, :L] + t_nb[:, :L], own[1] + nb_i - nb_j[:, L:] + t_nb[:, L:])
+        return own, total
 
     def node_forward(layer, h, total):
         agg = dot(total.astype(BF16), edge_out_ref[layer]).astype(BF16)
@@ -347,15 +346,18 @@
         dx = dot_nt(dpre, node_in_ref[layer])
         return grad + dx[:, :L], dx[:, L:].astype(BF16), (in_term, bias_term, out_term, gain_term)
 
-    def backward_block(size, oh_i, oh_j, hi, slope, i_source, both):
-        work_p[0:size, :] = dot(oh_j, both)
-        at_i = dot(oh_i, i_source)
-        for r in range(0, size, CHUNK):
-            here = slice(r, r + CHUNK)
+    def backward_rows(layer, parts, both):
+        for at, size, source in parts:
+            work_s[pl.ds(at, size), :] = dot(oh[0, pl.ds(at, size), :], source)
+        at = parts[0][0]
+        size = sum(part[1] for part in parts)
+        rows = pl.ds(at, size)
+        work_p[rows, :] = dot(oh[1, rows, :], both)
+        for here in chunks_of(at, size):
             is_hi = hi[here, :] > 0.5
-            dd = at_i[here, :] - jnp.where(is_hi, work_p[here, L:], work_p[here, :L])
-            dfwd = dd * slope[here, :L]
-            drev = -dd * slope[here, L:]
+            dd = work_s[here, :] - jnp.where(is_hi, work_p[here, L:], work_p[here, :L])
+            dfwd = dd * slope[layer, here, :L]
+            drev = -dd * slope[layer, here, L:]
             none = jnp.zeros_like(dfwd)
             work_d[here, :L] = dfwd.astype(BF16)
             work_d[here, L:] = drev.astype(BF16)
@@ -364,33 +366,46 @@
             work_e[here, :L] = jnp.where(is_hi, drev, none).astype(BF16)
             work_e[here, L:] = jnp.where(is_hi, dfwd, none).astype(BF16)
 
-    def edge_backward(layer, e_lo, e_hi, nb_blocks, with_hi):
+    def edge_backward(layer, e_lo, e_hi, last):
         both = jnp.concatenate([e_lo, e_hi], axis=1)
         q_nb[...] = jnp.zeros_like(q_nb)
 
-        def body(k, carry):
-            backward_block(NB_BLK, nb_oh[0, k], nb_oh[1, k], nb_hi.at[k], nb_slope.at[layer, k], e_hi, both)
-            q_nb[0:ROWS, :] += dot(nb_oht[1, k], work_x[0:NB_BLK, :])
-            if with_hi:
-                q_nb[ROWS:, :] += dot(nb_oht[1, k], work_e[0:NB_BLK, :]) + dot(nb_oht[0, k], work_d[0:NB_BLK, :])
-            return carry
-
-        lax.fori_loop(0, nb_blocks, body, 0)
-        backward_block(EMAX, own_oh[0], own_oh[1], own_hi, own_slope.at[layer], e_lo, both)
-        q_lo = dot(own_oht[0], work_d[...]) + dot(own_oht[1], work_x[...])
-        q_hi = dot(own_oht[1], work_e[...])
-        return q_lo, q_hi, dot(own_row[...], work_d[...])
+        def nb_collect(at, size):
+            rows = pl.ds(at, size)
+            lo = dot(oht[1, :, rows], work_x[rows, :])
+            if last == 0:
+                return lo, None
+            return lo, dot(oht[1, :, rows], work_e[rows, :]) + dot(oht[0, :, rows], work_d[rows, :])
+
+        def more(at):
+            backward_rows(layer, [(at, BLK, e_hi)], both)
+            lo, up = nb_collect(at, BLK)
+            q_nb[0:ROWS, :] += lo
+            if last:
+                q_nb[ROWS:, :] += up
+
+        further(last, more)
+        sure = BLK * SURE[last]
+        backward_rows(layer, [(0, EMAX, e_lo), (EMAX, sure, e_hi)], both)
+        rows = pl.ds(0, EMAX)
+        q_lo = dot(oht[0, :, rows], work_d[rows, :]) + dot(oht[1, :, rows], work_x[rows, :])
+        q_hi = dot(oht[1, :, rows], work_e[rows, :])
+        nb_lo, nb_up = nb_collect(EMAX, sure)
+        own = jnp.concatenate([q_lo, q_hi], axis=0)
+        if last == 0:
+            total = q_lo + nb_lo + q_nb[0:ROWS, :]
+        else:
+            total = own + jnp.concatenate([nb_lo, nb_up], axis=0) + q_nb[...]
+        return own, total, dot(own_row[...], work_d[rows, :])
 
     h0_lo = lat_ref[0]
     h0_hi = around(low_ref[0:LAT_HALO, :], upp_ref[0:LAT_HALO, :], LAT_HALO, ROWS)
-    t0_lo, t0_hi = edge_forward(0, h0_lo, h0_hi, reach[3])
-    total0 = jnp.concatenate([t0_lo + t_nb[:, :L], t0_hi + t_nb[:, L:]], axis=0)
+    own0, total0 = (jnp.concatenate(t, axis=0) for t in edge_forward(0, h0_lo, h0_hi, 3))
     h0 = jnp.concatenate([h0_lo, h0_hi], axis=0)
     h1, kept0 = node_forward(0, h0, total0)
-    t1_lo, t1_hi = edge_forward(1, h1[:ROWS], h1[ROWS:], reach[2])
+    own1, total1 = (jnp.concatenate(t, axis=0) for t in edge_forward(1, h1[:ROWS], h1[ROWS:], 2))
     near = ROWS + 2 * COT_HALO
-    total1 = jnp.concatenate([t1_lo + t_nb[:, :L], t1_hi[: near - ROWS] + t_nb[: near - ROWS, L:]], axis=0)
-    h2, kept1 = node_forward(1, h1[:near], total1)
+    h2, kept1 = node_forward(1, h1[:near], total1[:near])
     final_ref[0] = h2[:ROWS]
 
     few = lax.broadcasted_iota(jnp.int32, (MIG, 2 * COT_HALO), 1).astype(F32)
@@ -401,26 +416,22 @@
     def with_zeros(value):
         return jnp.concatenate([value, jnp.zeros((2 * ROWS - value.shape[0],) + value.shape[1:], value.dtype)], axis=0)
 
-    def layer_back(layer, grad, kept, own_total, h, nb_blocks, keep_rows):
+    def layer_back(layer, grad, kept, own_total, h, last, keep_rows):
         part, dagg, node_terms = node_backward(layer, grad, kept)
         spread = with_zeros(dagg)
         e = with_zeros(dot_nt(dagg, edge_out_ref[layer]).astype(BF16))
-        q_lo, q_hi, geo = edge_backward(layer, e[:ROWS], e[ROWS:], nb_blocks, keep_rows > ROWS)
+        q_own, q_all, geo = edge_backward(layer, e[:ROWS], e[ROWS:], last)
         out_term = dot_tn(own_total.astype(BF16), spread)
-        q_own = jnp.concatenate([q_lo, q_hi], axis=0)
         in_term = dot_tn(h, q_own.astype(BF16))
         straight, _ = edge_weights(layer)
-        q_all = (q_own[:keep_rows] + q_nb[:keep_rows, :]).astype(BF16)
-        new = part[:keep_rows] + dot_nt(q_all, straight)
+        new = part[:keep_rows] + dot_nt(q_all[:keep_rows].astype(BF16), straight)
         return new, (in_term, geo, out_term) + node_terms
 
-    own1 = jnp.concatenate([t1_lo, t1_hi], axis=0)
-    own0 = jnp.concatenate([t0_lo, t0_hi], axis=0)
     cot = jnp.concatenate(
         [cot_ref[0], around(low_ref[LAT_HALO:D_AT, :], upp_ref[LAT_HALO:D_AT, :], COT_HALO, 2 * COT_HALO)], axis=0
     ).astype(F32)
-    grad1, terms1 = layer_back(1, cot, kept1, own1, h1, reach[1], ROWS + 64)
-    grad0, terms0 = layer_back(0, grad1, kept0, own0, h0, reach[0], ROWS)
+    grad1, terms1 = layer_back(1, cot, kept1, own1, h1, 1, ROWS + 64)
+    grad0, terms0 = layer_back(0, grad1, kept0, own0, h0, 0, ROWS)
     grad_ref[0] = grad0
 
     size = MAIN // chunks
@@ -498,14 +509,19 @@
             r = 0
             while r < rows:
                 take = min(rows - r, size - at % size)
-                out[layer, r : r + take, :] = ref[at // size, at % size : at % size + take, :].astype(F32)
+                value = ref[at // size, at % size : at % size + take, :].astype(F32)
+                if out is edge_in:
+                    out[pl.ds(2 * r + layer, take, stride=2), :] = value
+                else:
+                    out[layer, r : r + take, :] = value
                 r += take
                 at += take
         small = []
         for extra in range(EXTRA):
             spot = size + extra % per
             small.append(ref[extra // per, spot : spot + 1, :].astype(F32))
-        edge_in[layer, 2 * L : 2 * L + 4, :] = jnp.concatenate(small[:4], axis=0)
+        for g in range(4):
+            edge_in[4 * L + 2 * g + layer : 4 * L + 2 * g + layer + 1, :] = small[g]
         edge_bias[layer : layer + 1, :] = small[4]
         node_bias[layer : layer + 1, :] = small[5]
         gain[layer : layer + 1, :] = small[6]
@@ -578,22 +594,18 @@
             scratch_shapes=[
                 pltpu.VMEM((SENT, L), BF16),
                 pltpu.VMEM((SENT, L), BF16),
-                pltpu.VMEM((2, EMAX, ROWS), BF16),
-                pltpu.VMEM((2, ROWS, EMAX), BF16),
-                pltpu.VMEM((EMAX, L), F32),
-                pltpu.VMEM((EMAX, 8), BF16),
+                pltpu.VMEM((2, ALL_PAIRS, ROWS), BF16),
+                pltpu.VMEM((2, ROWS, ALL_PAIRS), BF16),
+                pltpu.VMEM((ALL_PAIRS, L), F32),
+                pltpu.VMEM((ALL_PAIRS, 8), BF16),
                 pltpu.VMEM((8, EMAX), BF16),
-                pltpu.VMEM((2, EMAX, 2 * L), F32),
-                pltpu.VMEM((NB_BLOCKS, 8, NB_BLK), F32),
-                pltpu.VMEM((2, NB_BLOCKS, NB_BLK, ROWS), BF16),
-                pltpu.VMEM((2, NB_BLOCKS, ROWS, NB_BLK), BF16),
-                pltpu.VMEM((NB_BLOCKS, NB_BLK, L), F32),
-                pltpu.VMEM((NB_BLOCKS, NB_BLK, 8), BF16),
-                pltpu.VMEM((2, NB_BLOCKS, NB_BLK, 2 * L), F32),
-                pltpu.VMEM((EMAX, 2 * L), BF16),
-                pltpu.VMEM((EMAX, 2 * L), F32),
-                pltpu.VMEM((EMAX, 2 * L), BF16),
-                pltpu.VMEM((EMAX, 2 * L), BF16),
+                pltpu.VMEM((2, ALL_PAIRS, 2 * L), F32),
+                pltpu.VMEM((NB_BLOCKS, 8, BLK), F32),
+                pltpu.VMEM((ALL_PAIRS, 2 * L), BF16),
+                pltpu.VMEM((ALL_PAIRS, 2 * L), F32),
+                pltpu.VMEM((ALL_PAIRS, 2 * L), BF16),
+                pltpu.VMEM((ALL_PAIRS, 2 * L), BF16),
+                pltpu.VMEM((ALL_PAIRS, L), F32),
                 pltpu.VMEM((ROWS, 2 * L), F32),
                 pltpu.VMEM((2 * ROWS, 2 * L), F32),
                 pltpu.VMEM((2, chunks, chunk_rows, L), BF16),
@@ -610,13 +622,15 @@
 
         grads = pl.pallas_call(
             lambda *refs: unpack_kernel(chunks, *refs),
-            out_shape=tuple(jax.ShapeDtypeStruct(w.shape, F32) for w in weights),
+            out_shape=(jax.ShapeDtypeStruct((2 * weights[0].shape[1], L), F32),)
+            + tuple(jax.ShapeDtypeStruct(w.shape, F32) for w in weights[1:]),
             in_specs=vmem(2),
             out_specs=tuple(vmem(7)),
             compiler_params=params,
             name="unpack",
         )(got, lax.ppermute(got, "c", swap))
-        return (final, grad, arrivals) + tuple(grads)
+        edge_in_grad = jnp.transpose(grads[0].reshape(-1, 2, L), (1, 0, 2))
+        return (final, grad, arrivals, edge_in_grad) + tuple(grads[1:])
 
     return jax.shard_map(
         on_device,

time: 97.8 us -> 94.1 us (0.962)
  starting transfers between devices: 24.3 us -> 22.9 us
  blocking collectives: 46.4 us -> 45.4 us
    pallas_call x1, Pallas kernels: 14.3 us -> 13 us  [on_device(): pl.pallas_call(lambda *refs: main_kernel(chunks, *refs), out_shape=(jax.S...]
    all_to_all x1, blocking collectives: 14.1 us -> 12.9 us  [on_device(): got = lax.all_to_all(got, group, 0, 0, tiled=True)]
where the time goes in v3:
time: 94.1 us; the launch traced here: 93.7 us
  blocking collectives  45.4 us (48%)
  starting transfers between devices  22.9 us (24%)
  Pallas kernels  17.6 us (19%)
  waiting for transfers between devices  5.25 us (6%)
  between operations  1.49 us (2%)
  local copies, waits for them, and re-layouts  0.98 us (1%)
    all_to_all x1, blocking collectives, on_device(): got = lax.all_to_all(fold(got, n_h), 'zh', 0, 0, tiled=True)  20.1 us
    pallas_call x1, Pallas kernels, on_device(): pl.pallas_call(lambda *refs: main_kernel(chunks, *refs), out_shape=(jax.S...  13 us
    all_to_all x1, blocking collectives, on_device(): got = lax.all_to_all(got, group, 0, 0, tiled=True)  12.9 us
    all_to_all x1, blocking collectives, on_device(): got = lax.all_to_all(fold(got, chunks), group, 0, 0, tiled=True)  12.4 us
    ppermute x1, starting transfers between devices, on_device(): from_a = lax.ppermute(to_a, space, near + [(j, i) for i, j in near])  8.05 us
    ppermute x1, starting transfers between devices, on_device(): got = add(keep, lax.ppermute(send, 'c', swap))  6.95 us
    ppermute x1, starting transfers between devices, on_device(): lax.ppermute(got, 'c', swap)  5.87 us
    pallas_call x1, Pallas kernels, on_device(): pl.pallas_call(pack_kernel, out_shape=(sent, sent), in_specs=vmem(1) + [p...  3.54 us
  transfers between devices with their start and end apart: 4, of which 3 were waited for; matrix products, arithmetic and copies ran while one was open for 1% of the time, Pallas kernels for 0%

profile of v3, /device:TPU:1, one launch (start us, length us, event | category | flops | bytes accessed | tf_op | source)
XLA Modules:
  0.0 93.7 jit_solution(2349862987044954854)
XLA Ops:
  1.3 0.0 copy-start.3
  1.3 0.0 copy-start.4
  1.3 0.0 copy-start.5
  1.3 0.0 copy-start.6
  1.3 3.5 %pack.1 = (bf16[272,128]{1,0:T(8,128)(2,1)}, bf16[272,128]{1,0:T(8,128)(2,1)}) custom-call(s32[1,1]{1,0:T(1,128)S(6)} %copy.24.count_ref.refs_0_, bf16[1,256,128]{2,1,0:T(8,128)(2,1)} %refs_1_.1, bf16[1,256,128]{2,1,0:T(8,128)(2,1)} %refs_2_.1, s32[1,2,1024]{2,1,0:T(2,128)} %refs_3_.1, bf16[1,4,1024]{2,1,0:T(4,128)(2,1)} %refs_4_.1, s32[1,2,16]{2,1,0:T(2,128)} %leav_ref.1), custom_call_target="tpu_custom_call" | custom-call | tf_op jit(solution)/shard_map/pack/pallas_call | solution.py:564
  4.9 8.1 %collective-permute-start = (bf16[272,128]{1,0:T(8,128)(2,1)}, bf16[272,128]{1,0:T(8,128)(2,1)S(1)}, u32[]{:S(2)}, u32[]{:S(2)}) collective-permute-start(bf16[272,128]{1,0:T(8,128)(2,1)} %get-tuple-element.24), channel_id=1, source_target_pairs={{0,4},{8,12},{16,20},{24,28},{32,36},{40,44},{48,52},{56,60},{64,6... | collective-permute-start | bytes 208904 | tf_op jit(solution)/shard_map/ppermute | solution.py:581
  12.9 0.0 copy-start
  12.9 0.0 copy-start.1
  13.0 0.0 copy-start.2
  13.0 0.0 copy-start.7
  13.0 0.0 copy-start.8
  13.0 0.0 copy-start.9
  13.0 2.1 %collective-permute-start.1 = (bf16[272,128]{1,0:T(8,128)(2,1)}, bf16[272,128]{1,0:T(8,128)(2,1)S(1)}, u32[]{:S(2)}, u32[]{:S(2)}) collective-permute-start(bf16[272,128]{1,0:T(8,128)(2,1)} %get-tuple-element.25), channel_id=1, source_target_pairs={{4,8},{12,16},{20,24},{28,32},{36,40},{44,48},{52,56},{60,64},{68,... | collective-permute-start | bytes 208904 | tf_op jit(solution)/shard_map/ppermute | solution.py:582
  15.1 0.9 copy.23.refs_7_
  16.0 0.0 collective-permute-done.refs_5_
  16.0 3.0 %collective-permute-done.1.refs_6_ = bf16[272,128]{1,0:T(8,128)(2,1)S(1)} collective-permute-done((bf16[272,128]{1,0:T(8,128)(2,1)}, bf16[272,128]{1,0:T(8,128)(2,1)S(1)}, u32[]{:S(2)}, u32[]{:S(2)}) %collective-permute-start.1) | collective-permute-done | bytes 69664 | tf_op jit(solution)/shard_map/ppermute | solution.py:582
  19.0 0.0 copy-done.3
  19.0 0.0 copy-done.4
  19.0 0.0 copy-done.5
  19.0 0.0 copy-done.6
  19.0 0.0 copy-done
  19.0 0.0 copy-done.1
  19.0 0.0 copy-done.2
  19.0 0.0 copy-done.7
  19.0 0.0 copy-done.8
  19.0 0.0 copy-done.9
  19.1 13.0 %steps.1 = (bf16[1,256,128]{2,1,0:T(8,128)(2,1)}, f32[1,256,128]{2,1,0:T(8,128)}, bf16[1,2,16,128]{3,2,1,0:T(8,128)(2,1)}, bf16[32,32,128]{2,1,0:T(8,128)(2,1)S(1)}, bf16[32,32,128]{2,1,0:T(8,128)(2,1)S(1)}) custom-call(s32[1,1]{1,0:T(1,128)S(6)} %copy.24.count_ref.refs_0_, bf16[1,256,128]{2,1,0:T(8,128)(2,1)S(1)} %copy-done, ...), custom_call_target="tpu_custom_call" | custom-call | tf_op jit(solution)/shard_map/steps/pallas_call | solution.py:583
  32.1 6.9 %collective-permute-start.2 = (bf16[32,32,128]{2,1,0:T(8,128)(2,1)S(1)}, bf16[32,32,128]{2,1,0:T(8,128)(2,1)S(1)}, u32[]{:S(2)}, u32[]{:S(2)}) collective-permute-start(bf16[32,32,128]{2,1,0:T(8,128)(2,1)S(1)} %get-tuple-element.30), channel_id=1, source_target_pairs={{0,4},{4,0},{1,5},{5,1},{2,6},{6,2},{3,7},{7,3},{8,12},{12,8},{9,1... | collective-permute-start | bytes 786440 | tf_op jit(solution)/shard_map/ppermute | solution.py:618
  39.1 1.1 %collective-permute-done.2.b_ref = bf16[32,32,128]{2,1,0:T(8,128)(2,1)S(1)} collective-permute-done((bf16[32,32,128]{2,1,0:T(8,128)(2,1)S(1)}, bf16[32,32,128]{2,1,0:T(8,128)(2,1)S(1)}, u32[]{:S(2)}, u32[]{:S(2)}) %collective-permute-start.2) | collective-permute-done | bytes 262176 | tf_op jit(solution)/shard_map/ppermute | solution.py:618
  40.2 0.1 add.1
  40.3 12.9 %all_to_all.15.a = bf16[32,32,128]{2,1,0:T(8,128)(2,1)S(1)} all-to-all(bf16[32,32,128]{2,1,0:T(8,128)(2,1)S(1)} %add.1), channel_id=1, replica_groups=mesh['y'=4,'zh'=8,'zl'=2,'c'=2,'x'=4] {'y','zl','x'}, dimensions={0} | all-to-all | bytes 524288 | tf_op jit(solution)/shard_map/all_to_all | solution.py:619
  53.3 20.1 %all_to_all.16.a = bf16[8,32,128]{2,1,0:T(8,128)(2,1)S(1)} all-to-all(bf16[8,32,128]{2,1,0:T(8,128)(2,1)S(1)} %fold.2), channel_id=1, replica_groups=mesh['y'=4,'zh'=8,'zl'=2,'c'=2,'x'=4] {'zh'}, dimensions={0} | all-to-all | bytes 131072 | tf_op jit(solution)/shard_map/all_to_all | solution.py:620
  73.3 12.4 %all_to_all.17.refs_0_ = bf16[32,32,128]{2,1,0:T(8,128)(2,1)S(1)} all-to-all(bf16[32,32,128]{2,1,0:T(8,128)(2,1)S(1)} %fold.3), channel_id=1, replica_groups=mesh['y'=4,'zh'=8,'zl'=2,'c'=2,'x'=4] {'y','zl','x'}, dimensions={0} | all-to-all | bytes 524288 | tf_op jit(solution)/shard_map/all_to_all | solution.py:621
  85.8 5.9 %collective-permute-start.3 = (bf16[32,32,128]{2,1,0:T(8,128)(2,1)S(1)}, bf16[32,32,128]{2,1,0:T(8,128)(2,1)S(1)}, u32[]{:S(2)}, u32[]{:S(2)}) collective-permute-start(bf16[32,32,128]{2,1,0:T(8,128)(2,1)S(1)} %all_to_all.17.refs_0_), channel_id=1, source_target_pairs={{0,4},{4,0},{1,5},{5,1},{2,6},{6,2},{3,7},{7,3},{8,12},{12,8},{9,1... | collective-permute-start | bytes 786440 | tf_op jit(solution)/shard_map/ppermute | solution.py:631
  91.6 1.1 %collective-permute-done.3.refs_1_ = bf16[32,32,128]{2,1,0:T(8,128)(2,1)S(1)} collective-permute-done((bf16[32,32,128]{2,1,0:T(8,128)(2,1)S(1)}, bf16[32,32,128]{2,1,0:T(8,128)(2,1)S(1)}, u32[]{:S(2)}, u32[]{:S(2)}) %collective-permute-start.3) | collective-permute-done | bytes 262176 | tf_op jit(solution)/shard_map/ppermute | solution.py:631
  92.8 0.9 unpack.1
  (2 shorter events, 0.1 us)
Async XLA Ops:
  1.3 17.7 %copy-start.3 = (bf16[2,128,128]{2,1,0:T(8,128)(2,1)S(1)}, bf16[2,128,128]{2,1,0:T(8,128)(2,1)}, u32[]{:S(2)}) copy-start(bf16[2,128,128]{2,1,0:T(8,128)(2,1)} %refs_9_.1) | copy-start | bytes 196612
  1.3 17.7 %copy-start.4 = (bf16[2,128,128]{2,1,0:T(8,128)(2,1)S(1)}, bf16[2,128,128]{2,1,0:T(8,128)(2,1)}, u32[]{:S(2)}) copy-start(bf16[2,128,128]{2,1,0:T(8,128)(2,1)} %refs_12_.1) | copy-start | bytes 196612
  1.3 17.7 %copy-start.5 = (s32[1,2,1024]{2,1,0:T(2,128)S(1)}, s32[1,2,1024]{2,1,0:T(2,128)}, u32[]{:S(2)}) copy-start(s32[1,2,1024]{2,1,0:T(2,128)} %refs_3_.1) | copy-start | bytes 24580
  1.3 17.7 %copy-start.6 = (bf16[1,4,1024]{2,1,0:T(4,128)(2,1)S(1)}, bf16[1,4,1024]{2,1,0:T(4,128)(2,1)}, u32[]{:S(2)}) copy-start(bf16[1,4,1024]{2,1,0:T(4,128)(2,1)} %refs_4_.1) | copy-start | bytes 24580
  4.9 11.1 %collective-permute-start = (bf16[272,128]{1,0:T(8,128)(2,1)}, bf16[272,128]{1,0:T(8,128)(2,1)S(1)}, u32[]{:S(2)}, u32[]{:S(2)}) collective-permute-start(bf16[272,128]{1,0:T(8,128)(2,1)} %get-tuple-element.24), channel_id=1, source_target_pairs={{0,4},{8,12},{16,20},{24,28},{32,36},{40,44},{48,52},{56,60},{64,6... | collective-permute-start | bytes 208904 | tf_op jit(solution)/shard_map/ppermute | solution.py:581
  12.9 6.1 %copy-start = (bf16[1,256,128]{2,1,0:T(8,128)(2,1)S(1)}, bf16[1,256,128]{2,1,0:T(8,128)(2,1)}, u32[]{:S(2)}) copy-start(bf16[1,256,128]{2,1,0:T(8,128)(2,1)} %refs_1_.1) | copy-start | bytes 196612
  12.9 6.1 %copy-start.1 = (bf16[1,256,128]{2,1,0:T(8,128)(2,1)S(1)}, bf16[1,256,128]{2,1,0:T(8,128)(2,1)}, u32[]{:S(2)}) copy-start(bf16[1,256,128]{2,1,0:T(8,128)(2,1)} %refs_2_.1) | copy-start | bytes 196612
  13.0 6.1 %copy-start.2 = (bf16[2,256,128]{2,1,0:T(8,128)(2,1)S(1)}, bf16[2,256,128]{2,1,0:T(8,128)(2,1)}, u32[]{:S(2)}) copy-start(bf16[2,256,128]{2,1,0:T(8,128)(2,1)} %refs_10_.1) | copy-start | bytes 393220
  13.0 6.1 %copy-start.7 = (f32[2,128]{1,0:T(2,128)S(1)}, f32[2,128]{1,0:T(2,128)}, u32[]{:S(2)}) copy-start(f32[2,128]{1,0:T(2,128)} %refs_8_.1) | copy-start | bytes 3076
  13.0 6.1 %copy-start.8 = (f32[2,128]{1,0:T(2,128)S(1)}, f32[2,128]{1,0:T(2,128)}, u32[]{:S(2)}) copy-start(f32[2,128]{1,0:T(2,128)} %refs_11_.1) | copy-start | bytes 3076
  13.0 6.1 %copy-start.9 = (f32[2,128]{1,0:T(2,128)S(1)}, f32[2,128]{1,0:T(2,128)}, u32[]{:S(2)}) copy-start(f32[2,128]{1,0:T(2,128)} %refs_13_.1) | copy-start | bytes 3076
  13.0 6.0 %collective-permute-start.1 = (bf16[272,128]{1,0:T(8,128)(2,1)}, bf16[272,128]{1,0:T(8,128)(2,1)S(1)}, u32[]{:S(2)}, u32[]{:S(2)}) collective-permute-start(bf16[272,128]{1,0:T(8,128)(2,1)} %get-tuple-element.25), channel_id=1, source_target_pairs={{4,8},{12,16},{20,24},{28,32},{36,40},{44,48},{52,56},{60,64},{68,... | collective-permute-start | bytes 208904 | tf_op jit(solution)/shard_map/ppermute | solution.py:582
  32.1 8.1 %collective-permute-start.2 = (bf16[32,32,128]{2,1,0:T(8,128)(2,1)S(1)}, bf16[32,32,128]{2,1,0:T(8,128)(2,1)S(1)}, u32[]{:S(2)}, u32[]{:S(2)}) collective-permute-start(bf16[32,32,128]{2,1,0:T(8,128)(2,1)S(1)} %get-tuple-element.30), channel_id=1, source_target_pairs={{0,4},{4,0},{1,5},{5,1},{2,6},{6,2},{3,7},{7,3},{8,12},{12,8},{9,1... | collective-permute-start | bytes 786440 | tf_op jit(solution)/shard_map/ppermute | solution.py:618
  85.8 7.0 %collective-permute-start.3 = (bf16[32,32,128]{2,1,0:T(8,128)(2,1)S(1)}, bf16[32,32,128]{2,1,0:T(8,128)(2,1)S(1)}, u32[]{:S(2)}, u32[]{:S(2)}) collective-permute-start(bf16[32,32,128]{2,1,0:T(8,128)(2,1)S(1)} %all_to_all.17.refs_0_), channel_id=1, source_target_pairs={{0,4},{4,0},{1,5},{5,1},{2,6},{6,2},{3,7},{7,3},{8,12},{12,8},{9,1... | collective-permute-start | bytes 786440 | tf_op jit(solution)/shard_map/ppermute | solution.py:631

commit v4 on v3

--- a/solution.py
+++ b/solution.py
@@ -57,13 +57,14 @@
 
 
 def pack_kernel(
-    count_ref, lat_ref, cot_ref, pairs_ref, geo_ref, leav_ref, a_ref, b_ref, pairs_v, geo_v, leav_v, sems
+    count_ref, lat_ref, cot_ref, pairs_ref, geo_ref, leav_ref, a_ref, b_ref, count_v, pairs_v, geo_v, leav_v, sems
 ):
     first = lax.axis_index("c") == 0
     copies = [
         pltpu.make_async_copy(pairs_ref.at[0], pairs_v, sems.at[0]),
         pltpu.make_async_copy(geo_ref.at[0], geo_v, sems.at[1]),
         pltpu.make_async_copy(leav_ref.at[0], leav_v, sems.at[2]),
+        pltpu.make_async_copy(count_ref, count_v, sems.at[7]),
     ]
     ups = (first, jnp.logical_not(first))
     for k, ref in enumerate((a_ref, b_ref)):
@@ -75,10 +76,10 @@
         copies.append(pltpu.make_async_copy(cot, ref.at[pl.ds(LAT_HALO, COT_HALO), :], sems.at[4 + 2 * k]))
     for copy in copies:
         copy.start()
-    for copy in copies[:3]:
+    for copy in copies[:4]:
         copy.wait()
 
-    live = lax.broadcasted_iota(jnp.int32, (1, EMAX), 1) < count_ref[...]
+    live = lax.broadcasted_iota(jnp.int32, (1, EMAX), 1) < count_v[...]
     own = pairs_v[0:1, :]
     other = pairs_v[1:2, :]
     geo = geo_v[...].astype(F32)
@@ -114,43 +115,95 @@
     at = inside + before
     lane = lax.broadcasted_iota(jnp.int32, (1, 128), 1)
     col_w = lax.broadcasted_iota(jnp.int32, (128, BLK), 1).astype(F32)
-    for k, ref in enumerate((a_ref, b_ref)):
-        up = ups[k]
+    places = []
+    for k in range(2):
         rank = jnp.full((8, 128), -1.0, F32)
         for c in range(4):
             here = 32 * k + 8 * c
             rank = jnp.where(kinds[k] == c, at[here : here + 8, :], rank)
-        by_slot = jnp.transpose(rank)
+        places.append(jnp.transpose(rank))
+
+    def move(k, t, shift):
+        picks = [masked(places[k][:, q : q + 1] == col_w + shift) for q in range(8)]
+        moved = dot(rows[k], jnp.concatenate(picks, axis=0))
+        ref = (a_ref, b_ref)[k]
+        spot = D_AT + 16 * t
+        if not isinstance(t, int):
+            spot = pl.multiple_of(spot, 16)
+        ref[pl.ds(spot, 16), :] = jnp.concatenate([moved[:, :128], moved[:, 128:]], axis=0).astype(BF16)
+
+    for t in range(2):
+        for k in range(2):
+            move(k, t, float(BLK * t))
+    for k, ref in enumerate((a_ref, b_ref)):
+        up = ups[k]
         ends = [before[32 * k + 8 * c + 7, 0] + sums[32 * k + 8 * c + 7, 0] for c in range(4)]
         trips = lax.shift_right_logical(ends[3].astype(jnp.int32) + (BLK - 1), 8)
-        ref[D_AT:X_AT, :] = jnp.zeros((X_AT - D_AT, L), BF16)
-
-        def body(t, carry, ref=ref, by_slot=by_slot, source=rows[k]):
-            wanted = col_w + (t * BLK).astype(F32)
-            picks = [masked(by_slot[:, q : q + 1] == wanted) for q in range(8)]
-            moved = dot(source, jnp.concatenate(picks, axis=0))
-            spot = pl.multiple_of(D_AT + 16 * t, 16)
-            ref[pl.ds(spot, 16), :] = jnp.concatenate([moved[:, :128], moved[:, 128:]], axis=0).astype(BF16)
+        ref[D_AT + 32 : X_AT, :] = jnp.zeros((X_AT - D_AT - 32, L), BF16)
+
+        def body(t, carry, k=k):
+            move(k, t, (t * BLK).astype(F32))
             return carry
 
-        lax.fori_loop(0, trips, body, 0)
+        lax.fori_loop(2, trips, body, 0)
         movers = jnp.where(up, leav[1:2, :] - 224.0, leav[0:1, :] + 32.0)
         tail = jnp.concatenate([movers, jnp.zeros((1, 128 - MIG), F32)], axis=1)
         for c in range(4):
             blocks = ((ends[c].astype(jnp.int32) + (SIDE - 1)) // SIDE).astype(F32)
             tail = jnp.where(lane == MIG + c, blocks, tail)
         ref[X_AT:SENT, :] = jnp.broadcast_to(tail, (16, 128)).astype(BF16)
-    for copy in copies[3:]:
+    for copy in copies[4:]:
         copy.wait()
+
+
+def grids():
+    lanes = lax.broadcasted_iota(jnp.int32, (BLK, ROWS), 1).astype(F32) + 1.0
+    subs = lax.broadcasted_iota(jnp.int32, (ROWS, BLK), 0).astype(F32) + 1.0
+    return lanes, subs
+
+
+def set_block(at, rows, lanes, subs, oh, oht, hi, col):
+    here = pl.ds(at, BLK)
+    cols = jnp.transpose(rows)
+    for e in range(2):
+        oh[e, here, :] = masked(cols[:, e : e + 1] == lanes)
+        oht[e, :, here] = masked(rows[e : e + 1, :] == subs)
+    hi[here, :] = jnp.broadcast_to(cols[:, 2:3], (BLK, L))
+    col[here, :] = cols.astype(BF16)
+
+
+def own_kernel(count_ref, pairs_ref, geo_ref, bias_e, bias_n, gain, oh, oht, hi, col, row, bias_e_out, bias_n_out, gain_out):
+    bias_e_out[...] = bias_e[...]
+    bias_n_out[...] = bias_n[...]
+    gain_out[...] = gain[...]
+    live = lax.broadcasted_iota(jnp.int32, (1, EMAX), 1) < count_ref[...]
+    i_at = pairs_ref[0, 0:1, :] - 32
+    j_at, j_out = place(pairs_ref[0, 1:2, :] - 32)
+    rows = jnp.concatenate(
+        [
+            jnp.where(live, i_at + 1, 0).astype(F32),
+            jnp.where(live, j_at + 1, 0).astype(F32),
+            jnp.where(j_out, 1.0, 0.0).astype(F32),
+            jnp.ones((1, EMAX), F32),
+            geo_ref[0].astype(F32),
+        ],
+        axis=0,
+    )
+    row[...] = rows.astype(BF16)
+    lanes, subs = grids()
+    for k in range(OWN_BLOCKS):
+        set_block(BLK * k, rows[:, BLK * k : BLK * k + BLK], lanes, subs, oh, oht, hi, col)
 
 
 def main_kernel(
     chunks,
-    count_ref,
     lat_ref,
     cot_ref,
-    pairs_ref,
-    geo_ref,
+    own_oh,
+    own_oht,
+    own_hi,
+    own_col,
+    own_row,
     a_ref,
     b_ref,
     edge_in_ref,
@@ -167,11 +220,10 @@
     send_ref,
     low_ref,
     upp_ref,
-    oh,
-    oht,
-    hi,
-    col,
-    own_row,
+    nb_oh,
+    nb_oht,
+    nb_hi,
+    nb_col,
     slope,
     nb_rows,
     work_x,
@@ -182,6 +234,10 @@
     t_nb,
     q_nb,
     stage,
+    final_v,
+    arr_v,
+    grad_v,
+    sems,
 ):
     first = lax.axis_index("c") == 0
 
@@ -195,35 +251,13 @@
         low_ref[...] = a_ref[...]
         upp_ref[...] = b_ref[...]
 
-    lanes = lax.broadcasted_iota(jnp.int32, (BLK, ROWS), 1).astype(F32) + 1.0
-    subs = lax.broadcasted_iota(jnp.int32, (ROWS, BLK), 0).astype(F32) + 1.0
-
-    live = lax.broadcasted_iota(jnp.int32, (1, EMAX), 1) < count_ref[...]
-    i_at = pairs_ref[0, 0:1, :] - 32
-    j_at, j_out = place(pairs_ref[0, 1:2, :] - 32)
-    own_rows = jnp.concatenate(
-        [
-            jnp.where(live, i_at + 1, 0).astype(F32),
-            jnp.where(live, j_at + 1, 0).astype(F32),
-            jnp.where(j_out, 1.0, 0.0).astype(F32),
-            jnp.ones((1, EMAX), F32),
-            geo_ref[0].astype(F32),
-        ],
-        axis=0,
-    )
-    own_row[...] = own_rows.astype(BF16)
-
-    def prepare(at, rows):
-        here = pl.ds(at, BLK)
-        cols = jnp.transpose(rows)
-        for e in range(2):
-            oh[e, here, :] = masked(cols[:, e : e + 1] == lanes)
-            oht[e, :, here] = masked(rows[e : e + 1, :] == subs)
-        hi[here, :] = jnp.broadcast_to(cols[:, 2:3], (BLK, L))
-        col[here, :] = cols.astype(BF16)
-
-    for k in range(OWN_BLOCKS):
-        prepare(BLK * k, own_rows[:, BLK * k : BLK * k + BLK])
+    lanes, subs = grids()
+    own_refs = (own_oh, own_oht, own_hi, own_col)
+    nb_refs = (nb_oh, nb_oht, nb_hi, nb_col)
+    own_part = (own_refs, 0, EMAX, 0)
+
+    def nb_part(at, size):
+        return nb_refs, at, size, EMAX + at
 
     info = jnp.maximum(low_ref[X_AT:SENT, :].astype(F32), upp_ref[X_AT:SENT, :].astype(F32))[0:1, :]
     lane = lax.broadcasted_iota(jnp.int32, (1, L), 1)
@@ -233,16 +267,16 @@
     for k in range(NB_BLOCKS):
         nb_rows[k] = jnp.concatenate([low_rows[8 * k : 8 * k + 8], upp_rows[8 * k : 8 * k + 8]], axis=1)
     for k in range(SURE[3]):
-        prepare(EMAX + BLK * k, nb_rows[k])
+        set_block(BLK * k, nb_rows[k], lanes, subs, *nb_refs)
 
     def further(last, body):
         def step(k, carry):
-            body(pl.multiple_of(EMAX + BLK * k, BLK))
+            body(pl.multiple_of(BLK * k, BLK))
             return carry
 
         lax.fori_loop(SURE[last], reach[last], step, 0)
 
-    further(3, lambda at: prepare(at, nb_rows[(at - EMAX) // BLK]))
+    further(3, lambda at: set_block(at, nb_rows[at // BLK], lanes, subs, *nb_refs))
 
     def around(source_low, source_upp, width, height):
         parts = []
@@ -259,27 +293,34 @@
         straight = jnp.concatenate([top, bottom], axis=1)
         return straight, jnp.concatenate([bottom, top], axis=1)
 
-    def chunks_of(at, size):
-        return [pl.ds(at + r, CHUNK) for r in range(0, size, CHUNK)]
-
-    def forward_rows(layer, parts, both, weights, geo_weights, bias):
-        for at, size, source in parts:
-            work_x[pl.ds(at, size), :L] = dot(oh[0, pl.ds(at, size), :], source).astype(BF16)
-        at = parts[0][0]
-        size = sum(part[1] for part in parts)
-        rows = pl.ds(at, size)
-        work_p[rows, :] = dot(oh[1, rows, :], both)
-        for here in chunks_of(at, size):
-            is_hi = hi[here, :] > 0.5
+    def whole(parts):
+        return pl.ds(parts[0][3], sum(part[2] for part in parts))
+
+    def pieces(parts):
+        for refs, at, size, to in parts:
+            for r in range(0, size, CHUNK):
+                yield refs[2].at[pl.ds(at + r, CHUNK), :], pl.ds(to + r, CHUNK)
+
+    def gather(parts, sources, both, by_i):
+        for (refs, at, size, to), source in zip(parts, sources):
+            by_i[pl.ds(to, size), :L] = dot(refs[0][0, pl.ds(at, size), :], source).astype(by_i.dtype)
+            work_p[pl.ds(to, size), :] = dot(refs[0][1, pl.ds(at, size), :], both)
+
+    def forward_rows(layer, parts, sources, both, weights, geo_weights, bias):
+        gather(parts, sources, both, work_x)
+        for hi, here in pieces(parts):
+            is_hi = hi[...] > 0.5
             work_x[here, L:] = jnp.where(is_hi, work_p[here, L:], work_p[here, :L]).astype(BF16)
-        work_p[rows, :] = dot(work_x[rows, :], weights) + dot(col[rows, :], geo_weights)
-        for here in chunks_of(at, size):
+        for refs, at, size, to in parts:
+            rows = pl.ds(to, size)
+            work_p[rows, :] = dot(work_x[rows, :], weights) + dot(refs[3][pl.ds(at, size), :], geo_weights)
+        for hi, here in pieces(parts):
             pre = work_p[here, :] + bias
             sig = 0.5 * jnp.tanh(0.5 * pre) + 0.5
             act = pre * sig
             slope[layer, here, :] = sig + act * (1.0 - sig)
             diff = act[:, :L] - act[:, L:]
-            is_hi = hi[here, :] > 0.5
+            is_hi = hi[...] > 0.5
             none = jnp.zeros_like(diff)
             work_d[here, :L] = diff.astype(BF16)
             work_e[here, :L] = jnp.where(is_hi, none, diff).astype(BF16)
@@ -297,22 +338,24 @@
         both = jnp.concatenate([h_lo, h_hi], axis=1)
         t_nb[...] = jnp.zeros_like(t_nb)
 
-        def collect(at, size):
-            rows = pl.ds(at, size)
-            by_j = dot(oht[1, :, rows], work_e[rows, :])
-            return dot(oht[0, :, rows], work_d[rows, :L]), by_j
+        def collect(part):
+            refs, at, size, to = part
+            rows = pl.ds(to, size)
+            by_j = dot(refs[1][1, :, pl.ds(at, size)], work_e[rows, :])
+            return dot(refs[1][0, :, pl.ds(at, size)], work_d[rows, :L]), by_j
 
         def more(at):
-            forward_rows(layer, [(at, BLK, h_hi)], both, weights, geo_weights, bias)
-            by_i, by_j = collect(at, BLK)
+            part = nb_part(at, BLK)
+            forward_rows(layer, [part], [h_hi], both, weights, geo_weights, bias)
+            by_i, by_j = collect(part)
             t_nb[:, :L] += -by_j[:, :L]
             t_nb[:, L:] += by_i - by_j[:, L:]
 
         further(last, more)
-        sure = BLK * SURE[last]
-        forward_rows(layer, [(0, EMAX, h_lo), (EMAX, sure, h_hi)], both, weights, geo_weights, bias)
-        by_i, by_j = collect(0, EMAX)
-        nb_i, nb_j = collect(EMAX, sure)
+        parts = [own_part, nb_part(0, BLK * SURE[last])]
+        forward_rows(layer, parts, [h_lo, h_hi], both, weights, geo_weights, bias)
+        by_i, by_j = collect(parts[0])
+        nb_i, nb_j = collect(parts[1])
         own = (by_i - by_j[:, :L], -by_j[:, L:])
         total = (own[0] - nb_j[:, :L] + t_nb[:, :L], own[1] + nb_i - nb_j[:, L:] + t_nb[:, L:])
         return own, total
@@ -346,15 +389,10 @@
         dx = dot_nt(dpre, node_in_ref[layer])
         return grad + dx[:, :L], dx[:, L:].astype(BF16), (in_term, bias_term, out_term, gain_term)
 
-    def backward_rows(layer, parts, both):
-        for at, size, source in parts:
-            work_s[pl.ds(at, size), :] = dot(oh[0, pl.ds(at, size), :], source)
-        at = parts[0][0]
-        size = sum(part[1] for part in parts)
-        rows = pl.ds(at, size)
-        work_p[rows, :] = dot(oh[1, rows, :], both)
-        for here in chunks_of(at, size):
-            is_hi = hi[here, :] > 0.5
+    def backward_rows(layer, parts, sources, both):
+        gather(parts, sources, both, work_s)
+        for hi, here in pieces(parts):
+            is_hi = hi[...] > 0.5
             dd = work_s[here, :] - jnp.where(is_hi, work_p[here, L:], work_p[here, :L])
             dfwd = dd * slope[layer, here, :L]
             drev = -dd * slope[layer, here, L:]
@@ -370,27 +408,29 @@
         both = jnp.concatenate([e_lo, e_hi], axis=1)
         q_nb[...] = jnp.zeros_like(q_nb)
 
-        def nb_collect(at, size):
-            rows = pl.ds(at, size)
-            lo = dot(oht[1, :, rows], work_x[rows, :])
+        def nb_collect(part):
+            refs, at, size, to = part
+            rows, cols = pl.ds(to, size), pl.ds(at, size)
+            lo = dot(refs[1][1, :, cols], work_x[rows, :])
             if last == 0:
                 return lo, None
-            return lo, dot(oht[1, :, rows], work_e[rows, :]) + dot(oht[0, :, rows], work_d[rows, :])
+            return lo, dot(refs[1][1, :, cols], work_e[rows, :]) + dot(refs[1][0, :, cols], work_d[rows, :])
 
         def more(at):
-            backward_rows(layer, [(at, BLK, e_hi)], both)
-            lo, up = nb_collect(at, BLK)
+            part = nb_part(at, BLK)
+            backward_rows(layer, [part], [e_hi], both)
+            lo, up = nb_collect(part)
             q_nb[0:ROWS, :] += lo
             if last:
                 q_nb[ROWS:, :] += up
 
         further(last, more)
-        sure = BLK * SURE[last]
-        backward_rows(layer, [(0, EMAX, e_lo), (EMAX, sure, e_hi)], both)
+        parts = [own_part, nb_part(0, BLK * SURE[last])]
+        backward_rows(layer, parts, [e_lo, e_hi], both)
         rows = pl.ds(0, EMAX)
-        q_lo = dot(oht[0, :, rows], work_d[rows, :]) + dot(oht[1, :, rows], work_x[rows, :])
-        q_hi = dot(oht[1, :, rows], work_e[rows, :])
-        nb_lo, nb_up = nb_collect(EMAX, sure)
+        q_lo = dot(own_oht[0], work_d[rows, :]) + dot(own_oht[1], work_x[rows, :])
+        q_hi = dot(own_oht[1], work_e[rows, :])
+        nb_lo, nb_up = nb_collect(parts[1])
         own = jnp.concatenate([q_lo, q_hi], axis=0)
         if last == 0:
             total = q_lo + nb_lo + q_nb[0:ROWS, :]
@@ -406,12 +446,19 @@
     own1, total1 = (jnp.concatenate(t, axis=0) for t in edge_forward(1, h1[:ROWS], h1[ROWS:], 2))
     near = ROWS + 2 * COT_HALO
     h2, kept1 = node_forward(1, h1[:near], total1[:near])
-    final_ref[0] = h2[:ROWS]
+    final_v[...] = h2[:ROWS]
 
     few = lax.broadcasted_iota(jnp.int32, (MIG, 2 * COT_HALO), 1).astype(F32)
     for k, ref in ((0, upp_ref), (1, low_ref)):
         movers = jnp.transpose(ref[X_AT:SENT, :].astype(F32))[0:MIG, 0:1]
-        arr_ref[0, k] = dot(masked(movers == few), h2[ROWS:]).astype(BF16)
+        arr_v[k] = dot(masked(movers == few), h2[ROWS:]).astype(BF16)
+    copies = [
+        pltpu.make_async_copy(final_v, final_ref.at[0], sems.at[0]),
+        pltpu.make_async_copy(arr_v, arr_ref.at[0], sems.at[1]),
+        pltpu.make_async_copy(grad_v, grad_ref.at[0], sems.at[2]),
+    ]
+    copies[0].start()
+    copies[1].start()
 
     def with_zeros(value):
         return jnp.concatenate([value, jnp.zeros((2 * ROWS - value.shape[0],) + value.shape[1:], value.dtype)], axis=0)
@@ -432,7 +479,8 @@
     ).astype(F32)
     grad1, terms1 = layer_back(1, cot, kept1, own1, h1, 1, ROWS + 64)
     grad0, terms0 = layer_back(0, grad1, kept0, own0, h0, 0, ROWS)
-    grad_ref[0] = grad0
+    grad_v[...] = grad0
+    copies[2].start()
 
     size = MAIN // chunks
     per = -(-EXTRA // chunks)
@@ -462,6 +510,9 @@
     def _():
         keep_ref[...] = stage[1]
         send_ref[...] = stage[0]
+
+    for copy in copies:
+        copy.wait()
 
 
 def fold_kernel(copies, in_ref, out_ref):
@@ -553,7 +604,7 @@
     n_h = n_z // n_l
     fine = Mesh(mesh.devices.reshape(n_y, n_h, n_l, n_c, n_x), ("y", "zh", "zl", "c", "x"))
     space = ("y", "zh", "zl", "c")
-    group = ("y", "zl", "x")
+    group = ("zl", "y", "x")
     chunks = n_y * n_l * n_x
     size = MAIN // chunks
     chunk_rows = size + -(-(-(-EXTRA // chunks)) // 8) * 8
@@ -564,13 +615,14 @@
         to_a, to_b = pl.pallas_call(
             pack_kernel,
             out_shape=(sent, sent),
-            in_specs=vmem(1) + [pl.BlockSpec(memory_space=pl.ANY)] * 5,
+            in_specs=[pl.BlockSpec(memory_space=pltpu.HBM)] * 6,
             out_specs=tuple(vmem(2)),
             scratch_shapes=[
+                pltpu.VMEM((1, 1), jnp.int32),
                 pltpu.VMEM((2, EMAX), jnp.int32),
                 pltpu.VMEM((4, EMAX), BF16),
                 pltpu.VMEM((2, MIG), jnp.int32),
-                pltpu.SemaphoreType.DMA((7,)),
+                pltpu.SemaphoreType.DMA((8,)),
             ],
             compiler_params=pltpu.CompilerParams(vmem_limit_bytes=60 * 1024 * 1024),
             name="pack",
@@ -580,6 +632,22 @@
         cross = [(2 * i + 1, (2 * i + 2) % n_space) for i in half]
         from_a = lax.ppermute(to_a, space, near + [(j, i) for i, j in near])
         from_b = lax.ppermute(to_b, space, cross + [(j, i) for i, j in cross])
+        own = pl.pallas_call(
+            own_kernel,
+            out_shape=(
+                jax.ShapeDtypeStruct((2, EMAX, ROWS), BF16),
+                jax.ShapeDtypeStruct((2, ROWS, EMAX), BF16),
+                jax.ShapeDtypeStruct((EMAX, L), F32),
+                jax.ShapeDtypeStruct((EMAX, 8), BF16),
+                jax.ShapeDtypeStruct((8, EMAX), BF16),
+            )
+            + (jax.ShapeDtypeStruct((2, L), F32),) * 3,
+            in_specs=vmem(6),
+            out_specs=tuple(vmem(8)),
+            compiler_params=pltpu.CompilerParams(vmem_limit_bytes=16 * 1024 * 1024),
+            cost_estimate=pl.CostEstimate(flops=2000000, bytes_accessed=8000000, transcendentals=0),
+            name="own",
+        )(pair_count, pairs, geometry, weights[1], weights[4], weights[6])
         final, grad, arrivals, keep, send = pl.pallas_call(
             lambda *refs: main_kernel(chunks, *refs),
             out_shape=(
@@ -589,16 +657,15 @@
                 jax.ShapeDtypeStruct((chunks, chunk_rows, L), BF16),
                 jax.ShapeDtypeStruct((chunks, chunk_rows, L), BF16),
             ),
-            in_specs=vmem(14),
-            out_specs=tuple(vmem(5)),
+            in_specs=vmem(16),
+            out_specs=tuple([pl.BlockSpec(memory_space=pl.ANY)] * 3 + vmem(2)),
             scratch_shapes=[
                 pltpu.VMEM((SENT, L), BF16),
                 pltpu.VMEM((SENT, L), BF16),
-                pltpu.VMEM((2, ALL_PAIRS, ROWS), BF16),
-                pltpu.VMEM((2, ROWS, ALL_PAIRS), BF16),
-                pltpu.VMEM((ALL_PAIRS, L), F32),
-                pltpu.VMEM((ALL_PAIRS, 8), BF16),
-                pltpu.VMEM((8, EMAX), BF16),
+                pltpu.VMEM((2, 2 * EMAX, ROWS), BF16),
+                pltpu.VMEM((2, ROWS, 2 * EMAX), BF16),
+                pltpu.VMEM((2 * EMAX, L), F32),
+                pltpu.VMEM((2 * EMAX, 8), BF16),
                 pltpu.VMEM((2, ALL_PAIRS, 2 * L), F32),
                 pltpu.VMEM((NB_BLOCKS, 8, BLK), F32),
                 pltpu.VMEM((ALL_PAIRS, 2 * L), BF16),
@@ -609,10 +676,17 @@
                 pltpu.VMEM((ROWS, 2 * L), F32),
                 pltpu.VMEM((2 * ROWS, 2 * L), F32),
                 pltpu.VMEM((2, chunks, chunk_rows, L), BF16),
+                pltpu.VMEM((ROWS, L), BF16),
+                pltpu.VMEM((2, MIG, L), BF16),
+                pltpu.VMEM((ROWS, L), F32),
+                pltpu.SemaphoreType.DMA((3,)),
             ],
             compiler_params=params,
             name="steps",
-        )(pair_count, latents, cotangent, pairs, geometry, from_a, from_b, *weights)
+        )(
+            latents, cotangent, *own[:5], from_a, from_b,
+            weights[0], own[5], weights[2], weights[3], own[6], weights[5], own[7],
+        )
 
         swap = [(0, 1), (1, 0)]
         got = add(keep, lax.ppermute(send, "c", swap))

time: 94.1 us -> 92.1 us (0.979)
  starting transfers between devices: 22.9 us -> 24.2 us
  Pallas kernels: 17.6 us -> 16.4 us
  waiting for transfers between devices: 5.25 us -> 4.12 us
    pallas_call x1, Pallas kernels: 13 us -> 11.6 us  [on_device(): pl.pallas_call(lambda *refs: main_kernel(chunks, *refs), out_shape=(jax.S...]
    ppermute x1, waiting for transfers between devices: 2.97 us -> 1.84 us  [on_device(): from_b = lax.ppermute(to_b, space, cross + [(j, i) for i, j in cross])]
    pallas_call x1 -> x2, Pallas kernels: 3.54 us -> 3.71 us  [the longest x1 2.68 us: on_device(): pl.pallas_call(pack_kernel, out_shape=(sent, sent), in_specs=[pl.BlockSpe...]
  transfers between devices with their start and end apart: 4 -> 4, of which waited for: 3 -> 3; matrix products, arithmetic and copies ran while one was open for 1% -> 1% of each run, Pallas kernels for 0% -> 1%
where the time goes in v4:
time: 92.1 us; the launch traced here: 91.7 us
  blocking collectives  44.5 us (48%)
  starting transfers between devices  24.2 us (26%)
  Pallas kernels  16.4 us (18%)
  waiting for transfers between devices  4.12 us (4%)
  between operations  1.49 us (2%)
  local copies, waits for them, and re-layouts  1.02 us (1%)
    all_to_all x1, blocking collectives, on_device(): got = lax.all_to_all(fold(got, n_h), 'zh', 0, 0, tiled=True)  20.3 us
    all_to_all x1, blocking collectives, on_device(): got = lax.all_to_all(got, group, 0, 0, tiled=True)  12.5 us
    all_to_all x1, blocking collectives, on_device(): got = lax.all_to_all(fold(got, chunks), group, 0, 0, tiled=True)  11.7 us
    pallas_call x1, Pallas kernels, on_device(): pl.pallas_call(lambda *refs: main_kernel(chunks, *refs), out_shape=(jax.S...  11.6 us
    ppermute x1, starting transfers between devices, on_device(): from_a = lax.ppermute(to_a, space, near + [(j, i) for i, j in near])  8.79 us
    ppermute x1, starting transfers between devices, on_device(): got = add(keep, lax.ppermute(send, 'c', swap))  6.92 us
    ppermute x1, starting transfers between devices, on_device(): lax.ppermute(got, 'c', swap)  6.45 us
    pallas_call x1, Pallas kernels, on_device(): pl.pallas_call(pack_kernel, out_shape=(sent, sent), in_specs=[pl.BlockSpe...  2.68 us
  transfers between devices with their start and end apart: 4, of which 3 were waited for; matrix products, arithmetic and copies ran while one was open for 1% of the time, Pallas kernels for 1%

profile of v4, /device:TPU:1, one launch (start us, length us, event | category | flops | bytes accessed | tf_op | source)
XLA Modules:
  0.0 91.7 jit_solution(16788244822205782183)
XLA Ops:
  1.3 0.0 copy-start.3
  1.3 0.0 copy-start.4
  1.3 2.7 %pack.1 = (bf16[272,128]{1,0:T(8,128)(2,1)}, bf16[272,128]{1,0:T(8,128)(2,1)}) custom-call(s32[1,1]{1,0:T(1,128)S(6)} %copy.24.count_ref, bf16[1,256,128]{2,1,0:T(8,128)(2,1)} %refs_0_.1, bf16[1,256,128]{2,1,0:T(8,128)(2,1)} %refs_1_.1, s32[1,2,1024]{2,1,0:T(2,128)} %pairs_ref.3, bf16[1,4,1024]{2,1,0:T(4,128)(2,1)} %geo_ref.3, s32[1,2,16]{2,1,0:T(2,128)} %leav_ref.1), custom_call_target="tpu_custom_call" | custom-call | tf_op jit(solution)/shard_map/pack/pallas_call | solution.py:615
  4.0 8.8 %collective-permute-start = (bf16[272,128]{1,0:T(8,128)(2,1)}, bf16[272,128]{1,0:T(8,128)(2,1)S(1)}, u32[]{:S(2)}, u32[]{:S(2)}) collective-permute-start(bf16[272,128]{1,0:T(8,128)(2,1)} %get-tuple-element.37), channel_id=1, source_target_pairs={{0,4},{8,12},{16,20},{24,28},{32,36},{40,44},{48,52},{56,60},{64,6... | collective-permute-start | bytes 208904 | tf_op jit(solution)/shard_map/ppermute | solution.py:633
  12.8 0.0 copy-start.5
  12.8 0.0 copy-start.6
  12.8 0.0 copy-start.7
  12.8 0.0 copy-start.8
  12.8 0.0 copy-start.9
  12.9 0.0 copy-start.2
  12.9 2.1 %collective-permute-start.1 = (bf16[272,128]{1,0:T(8,128)(2,1)}, bf16[272,128]{1,0:T(8,128)(2,1)S(1)}, u32[]{:S(2)}, u32[]{:S(2)}) collective-permute-start(bf16[272,128]{1,0:T(8,128)(2,1)} %get-tuple-element.38), channel_id=1, source_target_pairs={{4,8},{12,16},{20,24},{28,32},{36,40},{44,48},{52,56},{60,64},{68,... | collective-permute-start | bytes 208904 | tf_op jit(solution)/shard_map/ppermute | solution.py:634
  14.9 0.0 copy-start
  14.9 0.0 copy-start.1
  14.9 1.0 %copy.23.refs_9_ = bf16[2,260,128]{2,1,0:T(8,128)(2,1)S(1)} copy(bf16[2,260,128]{2,0,1:T(2,128)(2,1)} %param.19) | data formatting | bytes 266240 | tf_op args[6]
  15.9 0.0 copy-done.5
  15.9 0.0 copy-done.6
  15.9 0.0 copy-done.7
  15.9 0.0 copy-done.8
  16.0 0.0 copy-done.9
  16.0 1.0 %own.1 = (bf16[2,1024,256]{2,1,0:T(8,128)(2,1)S(1)}, bf16[2,256,1024]{2,1,0:T(8,128)(2,1)S(1)}, f32[1024,128]{1,0:T(8,128)S(1)}, bf16[1024,8]{1,0:T(8,128)(2,1)S...) custom-call(s32[1,1]{1,0:T(1,128)S(6)} %copy.24.count_ref, ...), custom_call_target="tpu_custom_call" | custom-call | flops 2000000 | bytes 8000000 | tf_op jit(solution)/shard_map/own/pallas_call | solution.py:635
  17.0 0.0 collective-permute-done.refs_7_
  17.0 1.8 %collective-permute-done.1.refs_8_ = bf16[272,128]{1,0:T(8,128)(2,1)S(1)} collective-permute-done((bf16[272,128]{1,0:T(8,128)(2,1)}, bf16[272,128]{1,0:T(8,128)(2,1)S(1)}, u32[]{:S(2)}, u32[]{:S(2)}) %collective-permute-start.1) | collective-permute-done | bytes 69664 | tf_op jit(solution)/shard_map/ppermute | solution.py:634
  18.8 0.0 copy-done.3
  18.8 0.0 copy-done.4
  18.8 0.0 copy-done.2
  18.8 0.0 copy-done
  18.9 0.0 copy-done.1
  18.9 11.6 %steps.1 = (bf16[1,256,128]{2,1,0:T(8,128)(2,1)}, f32[1,256,128]{2,1,0:T(8,128)}, bf16[1,2,16,128]{3,2,1,0:T(8,128)(2,1)}, bf16[32,32,128]{2,1,0:T(8,128)(2,1)S(1)}, bf16[32,32,128]{2,1,0:T(8,128)(2,1)S(1)}) custom-call(bf16[1,256,128]{2,1,0:T(8,128)(2,1)S(1)} %copy-done, bf16[1,256,128]{2,1,0:T(8,128)(2,1)S(1)} %copy-done.1, ...), custom_call_target="tpu_custom_call" | custom-call | tf_op jit(solution)/shard_map/steps/pallas_call | solution.py:651
  30.5 6.9 %collective-permute-start.2 = (bf16[32,32,128]{2,1,0:T(8,128)(2,1)S(1)}, bf16[32,32,128]{2,1,0:T(8,128)(2,1)S(1)}, u32[]{:S(2)}, u32[]{:S(2)}) collective-permute-start(bf16[32,32,128]{2,1,0:T(8,128)(2,1)S(1)} %get-tuple-element.46), channel_id=1, source_target_pairs={{0,4},{4,0},{1,5},{5,1},{2,6},{6,2},{3,7},{7,3},{8,12},{12,8},{9,1... | collective-permute-start | bytes 786440 | tf_op jit(solution)/shard_map/ppermute | solution.py:692
  37.4 1.1 %collective-permute-done.2.b_ref = bf16[32,32,128]{2,1,0:T(8,128)(2,1)S(1)} collective-permute-done((bf16[32,32,128]{2,1,0:T(8,128)(2,1)S(1)}, bf16[32,32,128]{2,1,0:T(8,128)(2,1)S(1)}, u32[]{:S(2)}, u32[]{:S(2)}) %collective-permute-start.2) | collective-permute-done | bytes 262176 | tf_op jit(solution)/shard_map/ppermute | solution.py:692
  38.5 0.1 add.1
  38.6 12.5 %all_to_all.15.a = bf16[32,32,128]{2,1,0:T(8,128)(2,1)S(1)} all-to-all(bf16[32,32,128]{2,1,0:T(8,128)(2,1)S(1)} %add.1), channel_id=1, replica_groups=mesh['y'=4,'zh'=8,'zl'=2,'c'=2,'x'=4] {'zl','y','x'}, dimensions={0} | all-to-all | bytes 524288 | tf_op jit(solution)/shard_map/all_to_all | solution.py:693
  51.2 20.3 %all_to_all.16.a = bf16[8,32,128]{2,1,0:T(8,128)(2,1)S(1)} all-to-all(bf16[8,32,128]{2,1,0:T(8,128)(2,1)S(1)} %fold.2), channel_id=1, replica_groups=mesh['y'=4,'zh'=8,'zl'=2,'c'=2,'x'=4] {'zh'}, dimensions={0} | all-to-all | bytes 131072 | tf_op jit(solution)/shard_map/all_to_all | solution.py:694
  71.5 11.7 %all_to_all.17.refs_0_ = bf16[32,32,128]{2,1,0:T(8,128)(2,1)S(1)} all-to-all(bf16[32,32,128]{2,1,0:T(8,128)(2,1)S(1)} %fold.3), channel_id=1, replica_groups=mesh['y'=4,'zh'=8,'zl'=2,'c'=2,'x'=4] {'zl','y','x'}, dimensions={0} | all-to-all | bytes 524288 | tf_op jit(solution)/shard_map/all_to_all | solution.py:695
  83.2 6.4 %collective-permute-start.3 = (bf16[32,32,128]{2,1,0:T(8,128)(2,1)S(1)}, bf16[32,32,128]{2,1,0:T(8,128)(2,1)S(1)}, u32[]{:S(2)}, u32[]{:S(2)}) collective-permute-start(bf16[32,32,128]{2,1,0:T(8,128)(2,1)S(1)} %all_to_all.17.refs_0_), channel_id=1, source_target_pairs={{0,4},{4,0},{1,5},{5,1},{2,6},{6,2},{3,7},{7,3},{8,12},{12,8},{9,1... | collective-permute-start | bytes 786440 | tf_op jit(solution)/shard_map/ppermute | solution.py:705
  89.6 1.1 %collective-permute-done.3.refs_1_ = bf16[32,32,128]{2,1,0:T(8,128)(2,1)S(1)} collective-permute-done((bf16[32,32,128]{2,1,0:T(8,128)(2,1)S(1)}, bf16[32,32,128]{2,1,0:T(8,128)(2,1)S(1)}, u32[]{:S(2)}, u32[]{:S(2)}) %collective-permute-start.3) | collective-permute-done | bytes 262176 | tf_op jit(solution)/shard_map/ppermute | solution.py:705
  90.7 0.9 %unpack.1 = (f32[520,128]{1,0:T(8,128)}, f32[2,128]{1,0:T(2,128)}, f32[2,128,128]{2,1,0:T(8,128)}, f32[2,256,128]{2,1,0:T(8,128)}, f32[2,128]{1,0:T(2,128)}, /*index=5*/f32[2,128,128]{2,1,0:T(8,128)}, f32[2,128]{1,0:T(2,128)}) custom-call(bf16[32,32,128]{2,1,0:T(8,128)(2,1)S(1)} %all_to_all.17.refs_0_, bf16[32,32,128]{2,1,0:T(8,128)(2,1)S(1)} %collective-permute-done.3.refs_1_), custom_call_target="tpu_custom_call" | custom-call | tf_op jit(solution)/shard_map/unpack/pallas_call | solution.py:697
  (2 shorter events, 0.1 us)
Async XLA Ops:
  1.3 17.5 %copy-start.3 = (bf16[2,128,128]{2,1,0:T(8,128)(2,1)S(1)}, bf16[2,128,128]{2,1,0:T(8,128)(2,1)}, u32[]{:S(2)}) copy-start(bf16[2,128,128]{2,1,0:T(8,128)(2,1)} %refs_11_.1) | copy-start | bytes 196612
  1.3 17.5 %copy-start.4 = (bf16[2,128,128]{2,1,0:T(8,128)(2,1)S(1)}, bf16[2,128,128]{2,1,0:T(8,128)(2,1)}, u32[]{:S(2)}) copy-start(bf16[2,128,128]{2,1,0:T(8,128)(2,1)} %refs_14_.1) | copy-start | bytes 196612
  4.0 13.0 %collective-permute-start = (bf16[272,128]{1,0:T(8,128)(2,1)}, bf16[272,128]{1,0:T(8,128)(2,1)S(1)}, u32[]{:S(2)}, u32[]{:S(2)}) collective-permute-start(bf16[272,128]{1,0:T(8,128)(2,1)} %get-tuple-element.37), channel_id=1, source_target_pairs={{0,4},{8,12},{16,20},{24,28},{32,36},{40,44},{48,52},{56,60},{64,6... | collective-permute-start | bytes 208904 | tf_op jit(solution)/shard_map/ppermute | solution.py:633
  12.8 3.1 %copy-start.5 = (s32[1,2,1024]{2,1,0:T(2,128)S(1)}, s32[1,2,1024]{2,1,0:T(2,128)}, u32[]{:S(2)}) copy-start(s32[1,2,1024]{2,1,0:T(2,128)} %pairs_ref.3) | copy-start | bytes 24580
  12.8 3.1 %copy-start.6 = (bf16[1,4,1024]{2,1,0:T(4,128)(2,1)S(1)}, bf16[1,4,1024]{2,1,0:T(4,128)(2,1)}, u32[]{:S(2)}) copy-start(bf16[1,4,1024]{2,1,0:T(4,128)(2,1)} %geo_ref.3) | copy-start | bytes 24580
  12.8 3.1 %copy-start.7 = (f32[2,128]{1,0:T(2,128)S(1)}, f32[2,128]{1,0:T(2,128)}, u32[]{:S(2)}) copy-start(f32[2,128]{1,0:T(2,128)} %bias_e.1) | copy-start | bytes 3076
  12.8 3.1 %copy-start.8 = (f32[2,128]{1,0:T(2,128)S(1)}, f32[2,128]{1,0:T(2,128)}, u32[]{:S(2)}) copy-start(f32[2,128]{1,0:T(2,128)} %bias_n.1) | copy-start | bytes 3076
  12.8 3.1 %copy-start.9 = (f32[2,128]{1,0:T(2,128)S(1)}, f32[2,128]{1,0:T(2,128)}, u32[]{:S(2)}) copy-start(f32[2,128]{1,0:T(2,128)} %gain.1) | copy-start | bytes 3076
  12.9 6.0 %copy-start.2 = (bf16[2,256,128]{2,1,0:T(8,128)(2,1)S(1)}, bf16[2,256,128]{2,1,0:T(8,128)(2,1)}, u32[]{:S(2)}) copy-start(bf16[2,256,128]{2,1,0:T(8,128)(2,1)} %refs_12_.1) | copy-start | bytes 393220
  12.9 6.0 %collective-permute-start.1 = (bf16[272,128]{1,0:T(8,128)(2,1)}, bf16[272,128]{1,0:T(8,128)(2,1)S(1)}, u32[]{:S(2)}, u32[]{:S(2)}) collective-permute-start(bf16[272,128]{1,0:T(8,128)(2,1)} %get-tuple-element.38), channel_id=1, source_target_pairs={{4,8},{12,16},{20,24},{28,32},{36,40},{44,48},{52,56},{60,64},{68,... | collective-permute-start | bytes 208904 | tf_op jit(solution)/shard_map/ppermute | solution.py:634
  14.9 3.9 %copy-start = (bf16[1,256,128]{2,1,0:T(8,128)(2,1)S(1)}, bf16[1,256,128]{2,1,0:T(8,128)(2,1)}, u32[]{:S(2)}) copy-start(bf16[1,256,128]{2,1,0:T(8,128)(2,1)} %refs_0_.1) | copy-start | bytes 196612
  14.9 3.9 %copy-start.1 = (bf16[1,256,128]{2,1,0:T(8,128)(2,1)S(1)}, bf16[1,256,128]{2,1,0:T(8,128)(2,1)}, u32[]{:S(2)}) copy-start(bf16[1,256,128]{2,1,0:T(8,128)(2,1)} %refs_1_.1) | copy-start | bytes 196612
  30.5 8.1 %collective-permute-start.2 = (bf16[32,32,128]{2,1,0:T(8,128)(2,1)S(1)}, bf16[32,32,128]{2,1,0:T(8,128)(2,1)S(1)}, u32[]{:S(2)}, u32[]{:S(2)}) collective-permute-start(bf16[32,32,128]{2,1,0:T(8,128)(2,1)S(1)} %get-tuple-element.46), channel_id=1, source_target_pairs={{0,4},{4,0},{1,5},{5,1},{2,6},{6,2},{3,7},{7,3},{8,12},{12,8},{9,1... | collective-permute-start | bytes 786440 | tf_op jit(solution)/shard_map/ppermute | solution.py:692
  83.2 7.6 %collective-permute-start.3 = (bf16[32,32,128]{2,1,0:T(8,128)(2,1)S(1)}, bf16[32,32,128]{2,1,0:T(8,128)(2,1)S(1)}, u32[]{:S(2)}, u32[]{:S(2)}) collective-permute-start(bf16[32,32,128]{2,1,0:T(8,128)(2,1)S(1)} %all_to_all.17.refs_0_), channel_id=1, source_target_pairs={{0,4},{4,0},{1,5},{5,1},{2,6},{6,2},{3,7},{7,3},{8,12},{12,8},{9,1... | collective-permute-start | bytes 786440 | tf_op jit(solution)/shard_map/ppermute | solution.py:705

commit v5 on v4

--- a/solution.py
+++ b/solution.py
@@ -24,8 +24,8 @@
 D_AT = LAT_HALO + COT_HALO
 X_AT = D_AT + 64
 MIG = 16
-MAIN = 768
-EXTRA = 7
+MAIN = 1536
+EXTRA = 14
 EPS = 1e-05
 VMEM_LIMIT = 48 * 1024 * 1024
 
@@ -57,7 +57,7 @@
 
 
 def pack_kernel(
-    count_ref, lat_ref, cot_ref, pairs_ref, geo_ref, leav_ref, a_ref, b_ref, count_v, pairs_v, geo_v, leav_v, sems
+    count_ref, lat_ref, cot_ref, pairs_ref, geo_ref, leav_ref, b_ref, a_ref, count_v, pairs_v, geo_v, leav_v, sems
 ):
     first = lax.axis_index("c") == 0
     copies = [
@@ -204,8 +204,8 @@
     own_hi,
     own_col,
     own_row,
+    b_ref,
     a_ref,
-    b_ref,
     edge_in_ref,
     edge_bias_ref,
     edge_out_ref,
@@ -216,8 +216,7 @@
     final_ref,
     grad_ref,
     arr_ref,
-    keep_ref,
-    send_ref,
+    packed_ref,
     low_ref,
     upp_ref,
     nb_oh,
@@ -233,7 +232,6 @@
     work_s,
     t_nb,
     q_nb,
-    stage,
     final_v,
     arr_v,
     grad_v,
@@ -484,78 +482,61 @@
 
     size = MAIN // chunks
     per = -(-EXTRA // chunks)
-    for layer, terms in enumerate((terms0, terms1)):
+    packed_ref[:, size:, :] = jnp.zeros((chunks, packed_ref.shape[1] - size, L), BF16)
+    at = 0
+    extra = 0
+    for terms in (terms0, terms1):
         in_term, geo, out_term, node_in_term, node_bias_term, node_out_term, gain_term = terms
-        stage[layer, :, size:, :] = jnp.zeros((chunks, stage.shape[2] - size, L), BF16)
-        at = 0
         for value in (in_term[:, :L], in_term[:, L:], out_term, node_in_term, node_out_term):
             value = value.astype(BF16)
             while value.shape[0]:
                 take = min(value.shape[0], size - at % size)
-                stage[layer, at // size, at % size : at % size + take, :] = value[:take]
+                packed_ref[at // size, at % size : at % size + take, :] = value[:take]
                 value = value[take:]
                 at += take
         small = [geo[4 + g : 5 + g, :L] - geo[4 + g : 5 + g, L:] for g in range(4)]
         small += [geo[3:4, :L] + geo[3:4, L:], node_bias_term, gain_term]
-        for extra, value in enumerate(small):
+        for value in small:
             spot = size + extra % per
-            stage[layer, extra // per, spot : spot + 1, :] = value.astype(BF16)
-
-    @pl.when(first)
-    def _():
-        keep_ref[...] = stage[0]
-        send_ref[...] = stage[1]
-
-    @pl.when(jnp.logical_not(first))
-    def _():
-        keep_ref[...] = stage[1]
-        send_ref[...] = stage[0]
+            packed_ref[extra // per, spot : spot + 1, :] = value.astype(BF16)
+            extra += 1
 
     for copy in copies:
         copy.wait()
 
 
-def fold_kernel(copies, in_ref, out_ref):
+def fold_kernel(copies, in_ref, *refs):
     total = in_ref[0].astype(F32)
     for k in range(1, in_ref.shape[0]):
         total += in_ref[k].astype(F32)
+    if len(refs) > 1:
+        total += refs[0][...].astype(F32)
     total = total.astype(BF16)
-    for k in range(copies):
-        out_ref[k] = total
-
-
-def fold(array, copies):
+    if copies is None:
+        refs[-1][...] = total
+    else:
+        for k in range(copies):
+            refs[-1][k] = total
+
+
+def fold(copies, array, *more):
+    shape = array.shape[1:] if copies is None else (copies,) + array.shape[1:]
     return pl.pallas_call(
-        lambda a, b: fold_kernel(copies, a, b),
-        out_shape=jax.ShapeDtypeStruct((copies,) + array.shape[1:], BF16),
-        in_specs=[pl.BlockSpec(memory_space=pltpu.VMEM)],
+        lambda *refs: fold_kernel(copies, *refs),
+        out_shape=jax.ShapeDtypeStruct(shape, BF16),
+        in_specs=vmem(1 + len(more)),
         out_specs=pl.BlockSpec(memory_space=pltpu.VMEM),
         compiler_params=pltpu.CompilerParams(vmem_limit_bytes=VMEM_LIMIT),
         name="fold",
-    )(array)
-
-
-def add_kernel(a_ref, b_ref, out_ref):
-    out_ref[...] = (a_ref[...].astype(F32) + b_ref[...].astype(F32)).astype(BF16)
-
-
-def add(a, b):
-    return pl.pallas_call(
-        add_kernel,
-        out_shape=jax.ShapeDtypeStruct(a.shape, BF16),
-        in_specs=vmem(2),
-        out_specs=pl.BlockSpec(memory_space=pltpu.VMEM),
-        compiler_params=pltpu.CompilerParams(vmem_limit_bytes=VMEM_LIMIT),
-        name="add",
-    )(a, b)
-
-
-def unpack_kernel(chunks, mine_ref, other_ref, *outs):
-    def write(layer, ref):
-        edge_in, edge_bias, edge_out, node_in, node_bias, node_out, gain = outs
-        size = MAIN // chunks
-        per = -(-EXTRA // chunks)
-        at = 0
+    )(array, *more)
+
+
+def unpack_kernel(chunks, ref, edge_in, edge_bias, edge_out, node_in, node_bias, node_out, gain):
+    size = MAIN // chunks
+    per = -(-EXTRA // chunks)
+    at = 0
+    extra = 0
+    for layer in range(2):
         for out, rows in ((edge_in, 2 * L), (edge_out, L), (node_in, 2 * L), (node_out, L)):
             r = 0
             while r < rows:
@@ -568,26 +549,15 @@
                 r += take
                 at += take
         small = []
-        for extra in range(EXTRA):
+        for _ in range(7):
             spot = size + extra % per
             small.append(ref[extra // per, spot : spot + 1, :].astype(F32))
+            extra += 1
         for g in range(4):
             edge_in[4 * L + 2 * g + layer : 4 * L + 2 * g + layer + 1, :] = small[g]
         edge_bias[layer : layer + 1, :] = small[4]
         node_bias[layer : layer + 1, :] = small[5]
         gain[layer : layer + 1, :] = small[6]
-
-    first = lax.axis_index("c") == 0
-
-    @pl.when(first)
-    def _():
-        write(0, mine_ref)
-        write(1, other_ref)
-
-    @pl.when(jnp.logical_not(first))
-    def _():
-        write(1, mine_ref)
-        write(0, other_ref)
 
 
 def vmem(count):
@@ -612,7 +582,7 @@
 
     def on_device(latents, pairs, geometry, pair_count, cotangent, leaving, *weights):
         sent = jax.ShapeDtypeStruct((SENT, L), BF16)
-        to_a, to_b = pl.pallas_call(
+        to_b, to_a = pl.pallas_call(
             pack_kernel,
             out_shape=(sent, sent),
             in_specs=[pl.BlockSpec(memory_space=pltpu.HBM)] * 6,
@@ -630,8 +600,8 @@
         half = range(n_space // 2)
         near = [(2 * i, 2 * i + 1) for i in half]
         cross = [(2 * i + 1, (2 * i + 2) % n_space) for i in half]
+        from_b = lax.ppermute(to_b, space, cross + [(j, i) for i, j in cross])
         from_a = lax.ppermute(to_a, space, near + [(j, i) for i, j in near])
-        from_b = lax.ppermute(to_b, space, cross + [(j, i) for i, j in cross])
         own = pl.pallas_call(
             own_kernel,
             out_shape=(
@@ -648,17 +618,16 @@
             cost_estimate=pl.CostEstimate(flops=2000000, bytes_accessed=8000000, transcendentals=0),
             name="own",
         )(pair_count, pairs, geometry, weights[1], weights[4], weights[6])
-        final, grad, arrivals, keep, send = pl.pallas_call(
+        final, grad, arrivals, packed = pl.pallas_call(
             lambda *refs: main_kernel(chunks, *refs),
             out_shape=(
                 jax.ShapeDtypeStruct((1, ROWS, L), BF16),
                 jax.ShapeDtypeStruct((1, ROWS, L), F32),
                 jax.ShapeDtypeStruct((1, 2, MIG, L), BF16),
                 jax.ShapeDtypeStruct((chunks, chunk_rows, L), BF16),
-                jax.ShapeDtypeStruct((chunks, chunk_rows, L), BF16),
             ),
             in_specs=vmem(16),
-            out_specs=tuple([pl.BlockSpec(memory_space=pl.ANY)] * 3 + vmem(2)),
+            out_specs=tuple([pl.BlockSpec(memory_space=pl.ANY)] * 3 + vmem(1)),
             scratch_shapes=[
                 pltpu.VMEM((SENT, L), BF16),
                 pltpu.VMEM((SENT, L), BF16),
@@ -675,7 +644,6 @@
                 pltpu.VMEM((ALL_PAIRS, L), F32),
                 pltpu.VMEM((ROWS, 2 * L), F32),
                 pltpu.VMEM((2 * ROWS, 2 * L), F32),
-                pltpu.VMEM((2, chunks, chunk_rows, L), BF16),
                 pltpu.VMEM((ROWS, L), BF16),
                 pltpu.VMEM((2, MIG, L), BF16),
                 pltpu.VMEM((ROWS, L), F32),
@@ -684,25 +652,24 @@
             compiler_params=params,
             name="steps",
         )(
-            latents, cotangent, *own[:5], from_a, from_b,
+            latents, cotangent, *own[:5], from_b, from_a,
             weights[0], own[5], weights[2], weights[3], own[6], weights[5], own[7],
         )
 
-        swap = [(0, 1), (1, 0)]
-        got = add(keep, lax.ppermute(send, "c", swap))
-        got = lax.all_to_all(got, group, 0, 0, tiled=True)
-        got = lax.all_to_all(fold(got, n_h), "zh", 0, 0, tiled=True)
-        got = lax.all_to_all(fold(got, chunks), group, 0, 0, tiled=True)
+        got = fold(None, lax.all_to_all(packed, group, 0, 0, tiled=True))
+        got = fold(n_h, got[None], lax.ppermute(got, "c", [(0, 1), (1, 0)]))
+        got = lax.all_to_all(got, "zh", 0, 0, tiled=True)
+        got = lax.all_to_all(fold(chunks, got), group, 0, 0, tiled=True)
 
         grads = pl.pallas_call(
             lambda *refs: unpack_kernel(chunks, *refs),
             out_shape=(jax.ShapeDtypeStruct((2 * weights[0].shape[1], L), F32),)
             + tuple(jax.ShapeDtypeStruct(w.shape, F32) for w in weights[1:]),
-            in_specs=vmem(2),
+            in_specs=vmem(1),
             out_specs=tuple(vmem(7)),
             compiler_params=params,
             name="unpack",
-        )(got, lax.ppermute(got, "c", swap))
+        )(got)
         edge_in_grad = jnp.transpose(grads[0].reshape(-1, 2, L), (1, 0, 2))
         return (final, grad, arrivals, edge_in_grad) + tuple(grads[1:])
 

time: 92.1 us -> 89.7 us (0.974)
  the two profiles are of different devices: /device:TPU:1 before, /device:TPU:2 now
where the time goes in v5:
time: 89.7 us; the launch traced here: 89.3 us
  blocking collectives  52 us (58%)
  starting transfers between devices  17.3 us (19%)
  Pallas kernels  16.4 us (18%)
  between operations  1.51 us (2%)
  waiting for transfers between devices  1.15 us (1%)
  local copies, waits for them, and re-layouts  1.02 us (1%)
    all_to_all x1, blocking collectives, on_device(): got = lax.all_to_all(got, 'zh', 0, 0, tiled=True)  22.5 us
    all_to_all x1, blocking collectives, on_device(): got = fold(None, lax.all_to_all(packed, group, 0, 0, tiled=True))  15.2 us
    all_to_all x1, blocking collectives, on_device(): got = lax.all_to_all(fold(chunks, got), group, 0, 0, tiled=True)  14.3 us
    ppermute x1, starting transfers between devices, on_device(): from_b = lax.ppermute(to_b, space, cross + [(j, i) for i, j in cross])  13.3 us
    pallas_call x1, Pallas kernels, on_device(): pl.pallas_call(lambda *refs: main_kernel(chunks, *refs), out_shape=(jax.S...  11.6 us
    pallas_call x1, Pallas kernels, on_device(): pl.pallas_call(pack_kernel, out_shape=(sent, sent), in_specs=[pl.BlockSpe...  2.68 us
    ppermute x1, starting transfers between devices, on_device(): from_a = lax.ppermute(to_a, space, near + [(j, i) for i, j in near])  2.05 us
    ppermute x1, starting transfers between devices, on_device(): got = fold(n_h, got[None], lax.ppermute(got, 'c', [(0, 1), (1, 0)]))  1.92 us
  transfers between devices with their start and end apart: 3, of which 1 were waited for; matrix products, arithmetic and copies ran while one was open for 1% of the time, Pallas kernels for 1%

profile of v5, /device:TPU:2, one launch (start us, length us, event | category | flops | bytes accessed | tf_op | source)
XLA Modules:
  0.0 89.3 jit_solution(6410670347420139484)
XLA Ops:
  1.3 0.0 copy-start.3
  1.3 0.0 copy-start.4
  1.3 2.7 %pack.1 = (bf16[272,128]{1,0:T(8,128)(2,1)}, bf16[272,128]{1,0:T(8,128)(2,1)}) custom-call(s32[1,1]{1,0:T(1,128)S(6)} %copy.24.count_ref, bf16[1,256,128]{2,1,0:T(8,128)(2,1)} %refs_0_.1, bf16[1,256,128]{2,1,0:T(8,128)(2,1)} %refs_1_.1, s32[1,2,1024]{2,1,0:T(2,128)} %pairs_ref.3, bf16[1,4,1024]{2,1,0:T(4,128)(2,1)} %geo_ref.3, s32[1,2,16]{2,1,0:T(2,128)} %leav_ref.1), custom_call_target="tpu_custom_call" | custom-call | tf_op jit(solution)/shard_map/pack/pallas_call | solution.py:585
  4.0 13.3 %collective-permute-start = (bf16[272,128]{1,0:T(8,128)(2,1)}, bf16[272,128]{1,0:T(8,128)(2,1)S(1)}, u32[]{:S(2)}, u32[]{:S(2)}) collective-permute-start(bf16[272,128]{1,0:T(8,128)(2,1)} %get-tuple-element.36), channel_id=1, source_target_pairs={{4,8},{12,16},{20,24},{28,32},{36,40},{44,48},{52,56},{60,64},{68,... | collective-permute-start | bytes 208904 | tf_op jit(solution)/shard_map/ppermute | solution.py:603
  17.3 0.0 copy-start.5
  17.3 0.0 copy-start.6
  17.3 0.0 copy-start.7
  17.3 0.0 copy-start.8
  17.3 0.0 copy-start.9
  17.4 0.0 copy-start.2
  17.4 2.1 %collective-permute-start.1 = (bf16[272,128]{1,0:T(8,128)(2,1)}, bf16[272,128]{1,0:T(8,128)(2,1)S(1)}, u32[]{:S(2)}, u32[]{:S(2)}) collective-permute-start(bf16[272,128]{1,0:T(8,128)(2,1)} %get-tuple-element.37), channel_id=1, source_target_pairs={{0,4},{8,12},{16,20},{24,28},{32,36},{40,44},{48,52},{56,60},{64,6... | collective-permute-start | bytes 208904 | tf_op jit(solution)/shard_map/ppermute | solution.py:604
  19.4 0.0 copy-start
  19.4 0.0 copy-start.1
  19.5 1.0 %copy.23.refs_9_ = bf16[2,260,128]{2,1,0:T(8,128)(2,1)S(1)} copy(bf16[2,260,128]{2,0,1:T(2,128)(2,1)} %param.19) | data formatting | bytes 266240 | tf_op args[6]
  20.4 0.0 copy-done.5
  20.4 0.0 copy-done.6
  20.4 0.0 copy-done.7
  20.4 0.0 copy-done.8
  20.5 0.0 copy-done.9
  20.5 1.0 %own.1 = (bf16[2,1024,256]{2,1,0:T(8,128)(2,1)S(1)}, bf16[2,256,1024]{2,1,0:T(8,128)(2,1)S(1)}, f32[1024,128]{1,0:T(8,128)S(1)}, bf16[1024,8]{1,0:T(8,128)(2,1)S...) custom-call(s32[1,1]{1,0:T(1,128)S(6)} %copy.24.count_ref, ...), custom_call_target="tpu_custom_call" | custom-call | flops 2000000 | bytes 8000000 | tf_op jit(solution)/shard_map/own/pallas_call | solution.py:605
  21.5 0.0 collective-permute-done.refs_7_
  21.5 0.0 collective-permute-done.1.refs_8_
  21.5 0.0 copy-done.3
  21.5 0.0 copy-done.4
  21.5 0.0 copy-done.2
  21.5 0.0 copy-done
  21.6 0.0 copy-done.1
  21.6 11.6 %steps.1 = (bf16[1,256,128]{2,1,0:T(8,128)(2,1)}, f32[1,256,128]{2,1,0:T(8,128)}, bf16[1,2,16,128]{3,2,1,0:T(8,128)(2,1)}, bf16[32,56,128]{2,1,0:T(8,128)(2,1)S(1)}) custom-call(bf16[1,256,128]{2,1,0:T(8,128)(2,1)S(1)} %copy-done, bf16[1,256,128]{2,1,0:T(8,128)(2,1)S(1)} %copy-done.1, bf16[2,1024,256]{2,1,0:T(8,128)(2,1)S(1)} %get-tuple-element.31.refs_2_, ...), custom_call_target="tpu_custom_call" | custom-call | tf_op jit(solution)/shard_map/steps/pallas_call | solution.py:621
  33.2 15.2 %all_to_all.15.refs_0_ = bf16[32,56,128]{2,1,0:T(8,128)(2,1)S(1)} all-to-all(bf16[32,56,128]{2,1,0:T(8,128)(2,1)S(1)} %get-tuple-element.44), channel_id=1, replica_groups=mesh['y'=4,'zh'=8,'zl'=2,'c'=2,'x'=4] {'zl','y','x'}, dimensions={0} | all-to-all | bytes 917504 | tf_op jit(solution)/shard_map/all_to_all | solution.py:659
  48.4 0.1 fold.3
  48.5 1.9 %collective-permute-start.2 = (bf16[56,128]{1,0:T(8,128)(2,1)S(1)}, bf16[56,128]{1,0:T(8,128)(2,1)S(1)}, u32[]{:S(2)}, u32[]{:S(2)}) collective-permute-start(bf16[56,128]{1,0:T(8,128)(2,1)S(1)} %fold.3), channel_id=1, source_target_pairs={{0,4},{4,0},{1,5},{5,1},{2,6},{6,2},{3,7},{7,3},{8,12},{12,8},{9,1... | collective-permute-start | bytes 43016 | tf_op jit(solution)/shard_map/ppermute | solution.py:660
  50.4 1.1 %collective-permute-done.2.refs_1_ = bf16[56,128]{1,0:T(8,128)(2,1)S(1)} collective-permute-done((bf16[56,128]{1,0:T(8,128)(2,1)S(1)}, bf16[56,128]{1,0:T(8,128)(2,1)S(1)}, u32[]{:S(2)}, u32[]{:S(2)}) %collective-permute-start.2) | collective-permute-done | bytes 14368 | tf_op jit(solution)/shard_map/ppermute | solution.py:660
  51.6 22.5 %all_to_all.16.refs_0_ = bf16[8,56,128]{2,1,0:T(8,128)(2,1)S(1)} all-to-all(bf16[8,56,128]{2,1,0:T(8,128)(2,1)S(1)} %fold.4), channel_id=1, replica_groups=mesh['y'=4,'zh'=8,'zl'=2,'c'=2,'x'=4] {'zh'}, dimensions={0} | all-to-all | bytes 229376 | tf_op jit(solution)/shard_map/all_to_all | solution.py:661
  74.1 14.3 %all_to_all.17.refs_0_ = bf16[32,56,128]{2,1,0:T(8,128)(2,1)S(1)} all-to-all(bf16[32,56,128]{2,1,0:T(8,128)(2,1)S(1)} %fold.5), channel_id=1, replica_groups=mesh['y'=4,'zh'=8,'zl'=2,'c'=2,'x'=4] {'zl','y','x'}, dimensions={0} | all-to-all | bytes 917504 | tf_op jit(solution)/shard_map/all_to_all | solution.py:662
  88.4 0.9 %unpack.1 = (f32[520,128]{1,0:T(8,128)}, f32[2,128]{1,0:T(2,128)}, f32[2,128,128]{2,1,0:T(8,128)}, f32[2,256,128]{2,1,0:T(8,128)}, f32[2,128]{1,0:T(2,128)}, /*index=5*/f32[2,128,128]{2,1,0:T(8,128)}, f32[2,128]{1,0:T(2,128)}) custom-call(bf16[32,56,128]{2,1,0:T(8,128)(2,1)S(1)} %all_to_all.17.refs_0_), custom_call_target="tpu_custom_call" | custom-call | tf_op jit(solution)/shard_map/unpack/pallas_call | solution.py:664
  (2 shorter events, 0.1 us)
Async XLA Ops:
  1.3 20.2 %copy-start.3 = (bf16[2,128,128]{2,1,0:T(8,128)(2,1)S(1)}, bf16[2,128,128]{2,1,0:T(8,128)(2,1)}, u32[]{:S(2)}) copy-start(bf16[2,128,128]{2,1,0:T(8,128)(2,1)} %refs_11_.1) | copy-start | bytes 196612
  1.3 20.2 %copy-start.4 = (bf16[2,128,128]{2,1,0:T(8,128)(2,1)S(1)}, bf16[2,128,128]{2,1,0:T(8,128)(2,1)}, u32[]{:S(2)}) copy-start(bf16[2,128,128]{2,1,0:T(8,128)(2,1)} %refs_14_.1) | copy-start | bytes 196612
  4.0 17.5 %collective-permute-start = (bf16[272,128]{1,0:T(8,128)(2,1)}, bf16[272,128]{1,0:T(8,128)(2,1)S(1)}, u32[]{:S(2)}, u32[]{:S(2)}) collective-permute-start(bf16[272,128]{1,0:T(8,128)(2,1)} %get-tuple-element.36), channel_id=1, source_target_pairs={{4,8},{12,16},{20,24},{28,32},{36,40},{44,48},{52,56},{60,64},{68,... | collective-permute-start | bytes 208904 | tf_op jit(solution)/shard_map/ppermute | solution.py:603
  17.3 3.1 %copy-start.5 = (s32[1,2,1024]{2,1,0:T(2,128)S(1)}, s32[1,2,1024]{2,1,0:T(2,128)}, u32[]{:S(2)}) copy-start(s32[1,2,1024]{2,1,0:T(2,128)} %pairs_ref.3) | copy-start | bytes 24580
  17.3 3.1 %copy-start.6 = (bf16[1,4,1024]{2,1,0:T(4,128)(2,1)S(1)}, bf16[1,4,1024]{2,1,0:T(4,128)(2,1)}, u32[]{:S(2)}) copy-start(bf16[1,4,1024]{2,1,0:T(4,128)(2,1)} %geo_ref.3) | copy-start | bytes 24580
  17.3 3.1 %copy-start.7 = (f32[2,128]{1,0:T(2,128)S(1)}, f32[2,128]{1,0:T(2,128)}, u32[]{:S(2)}) copy-start(f32[2,128]{1,0:T(2,128)} %bias_e.1) | copy-start | bytes 3076
  17.3 3.1 %copy-start.8 = (f32[2,128]{1,0:T(2,128)S(1)}, f32[2,128]{1,0:T(2,128)}, u32[]{:S(2)}) copy-start(f32[2,128]{1,0:T(2,128)} %bias_n.1) | copy-start | bytes 3076
  17.3 3.1 %copy-start.9 = (f32[2,128]{1,0:T(2,128)S(1)}, f32[2,128]{1,0:T(2,128)}, u32[]{:S(2)}) copy-start(f32[2,128]{1,0:T(2,128)} %gain.1) | copy-start | bytes 3076
  17.4 4.2 %copy-start.2 = (bf16[2,256,128]{2,1,0:T(8,128)(2,1)S(1)}, bf16[2,256,128]{2,1,0:T(8,128)(2,1)}, u32[]{:S(2)}) copy-start(bf16[2,256,128]{2,1,0:T(8,128)(2,1)} %refs_12_.1) | copy-start | bytes 393220
  17.4 4.1 %collective-permute-start.1 = (bf16[272,128]{1,0:T(8,128)(2,1)}, bf16[272,128]{1,0:T(8,128)(2,1)S(1)}, u32[]{:S(2)}, u32[]{:S(2)}) collective-permute-start(bf16[272,128]{1,0:T(8,128)(2,1)} %get-tuple-element.37), channel_id=1, source_target_pairs={{0,4},{8,12},{16,20},{24,28},{32,36},{40,44},{48,52},{56,60},{64,6... | collective-permute-start | bytes 208904 | tf_op jit(solution)/shard_map/ppermute | solution.py:604
  19.4 2.1 %copy-start = (bf16[1,256,128]{2,1,0:T(8,128)(2,1)S(1)}, bf16[1,256,128]{2,1,0:T(8,128)(2,1)}, u32[]{:S(2)}) copy-start(bf16[1,256,128]{2,1,0:T(8,128)(2,1)} %refs_0_.1) | copy-start | bytes 196612
  19.4 2.1 %copy-start.1 = (bf16[1,256,128]{2,1,0:T(8,128)(2,1)S(1)}, bf16[1,256,128]{2,1,0:T(8,128)(2,1)}, u32[]{:S(2)}) copy-start(bf16[1,256,128]{2,1,0:T(8,128)(2,1)} %refs_1_.1) | copy-start | bytes 196612
  48.5 3.1 %collective-permute-start.2 = (bf16[56,128]{1,0:T(8,128)(2,1)S(1)}, bf16[56,128]{1,0:T(8,128)(2,1)S(1)}, u32[]{:S(2)}, u32[]{:S(2)}) collective-permute-start(bf16[56,128]{1,0:T(8,128)(2,1)S(1)} %fold.3), channel_id=1, source_target_pairs={{0,4},{4,0},{1,5},{5,1},{2,6},{6,2},{3,7},{7,3},{8,12},{12,8},{9,1... | collective-permute-start | bytes 43016 | tf_op jit(solution)/shard_map/ppermute | solution.py:660

commit v6 on v5

--- a/solution.py
+++ b/solution.py
@@ -206,7 +206,7 @@
     own_row,
     b_ref,
     a_ref,
-    edge_in_ref,
+    edge_in_rows,
     edge_bias_ref,
     edge_out_ref,
     node_in_ref,
@@ -235,6 +235,8 @@
     final_v,
     arr_v,
     grad_v,
+    edge_in_wide,
+    edge_in_ref,
     sems,
 ):
     first = lax.axis_index("c") == 0
@@ -264,9 +266,6 @@
     upp_rows = upp_ref[D_AT:X_AT, :].astype(F32)
     for k in range(NB_BLOCKS):
         nb_rows[k] = jnp.concatenate([low_rows[8 * k : 8 * k + 8], upp_rows[8 * k : 8 * k + 8]], axis=1)
-    for k in range(SURE[3]):
-        set_block(BLK * k, nb_rows[k], lanes, subs, *nb_refs)
-
     def further(last, body):
         def step(k, carry):
             body(pl.multiple_of(BLK * k, BLK))
@@ -274,7 +273,9 @@
 
         lax.fori_loop(SURE[last], reach[last], step, 0)
 
-    further(3, lambda at: set_block(at, nb_rows[at // BLK], lanes, subs, *nb_refs))
+    edge_in_wide[...] = edge_in_rows[...].astype(F32)
+    for layer in range(2):
+        edge_in_ref[layer] = edge_in_wide[pl.ds(layer, edge_in_wide.shape[0] // 2, stride=2), :].astype(BF16)
 
     def around(source_low, source_upp, width, height):
         parts = []
@@ -304,7 +305,8 @@
             by_i[pl.ds(to, size), :L] = dot(refs[0][0, pl.ds(at, size), :], source).astype(by_i.dtype)
             work_p[pl.ds(to, size), :] = dot(refs[0][1, pl.ds(at, size), :], both)
 
-    def forward_rows(layer, parts, sources, both, weights, geo_weights, bias):
+    def forward_pre(parts, sources, constants):
+        both, weights, geo_weights, _ = constants
         gather(parts, sources, both, work_x)
         for hi, here in pieces(parts):
             is_hi = hi[...] > 0.5
@@ -312,6 +314,9 @@
         for refs, at, size, to in parts:
             rows = pl.ds(to, size)
             work_p[rows, :] = dot(work_x[rows, :], weights) + dot(refs[3][pl.ds(at, size), :], geo_weights)
+
+    def forward_act(layer, parts, constants):
+        bias = constants[3]
         for hi, here in pieces(parts):
             pre = work_p[here, :] + bias
             sig = 0.5 * jnp.tanh(0.5 * pre) + 0.5
@@ -324,7 +329,7 @@
             work_e[here, :L] = jnp.where(is_hi, none, diff).astype(BF16)
             work_e[here, L:] = jnp.where(is_hi, diff, none).astype(BF16)
 
-    def edge_forward(layer, h_lo, h_hi, last):
+    def edge_constants(layer, h_lo, h_hi):
         straight, crossed = edge_weights(layer)
         weights = jnp.concatenate([straight, crossed], axis=0)
         geo_top = edge_in_ref[layer, 2 * L : 2 * L + 4, :].astype(F32)
@@ -333,7 +338,9 @@
         ).astype(BF16)
         bias_row = edge_bias_ref[layer : layer + 1, :]
         bias = jnp.concatenate([bias_row, bias_row], axis=1)
-        both = jnp.concatenate([h_lo, h_hi], axis=1)
+        return jnp.concatenate([h_lo, h_hi], axis=1), weights, geo_weights, bias
+
+    def edge_forward(layer, h_lo, h_hi, last, constants, begun):
         t_nb[...] = jnp.zeros_like(t_nb)
 
         def collect(part):
@@ -344,14 +351,19 @@
 
         def more(at):
             part = nb_part(at, BLK)
-            forward_rows(layer, [part], [h_hi], both, weights, geo_weights, bias)
+            forward_pre([part], [h_hi], constants)
+            forward_act(layer, [part], constants)
             by_i, by_j = collect(part)
             t_nb[:, :L] += -by_j[:, :L]
             t_nb[:, L:] += by_i - by_j[:, L:]
 
         further(last, more)
         parts = [own_part, nb_part(0, BLK * SURE[last])]
-        forward_rows(layer, parts, [h_lo, h_hi], both, weights, geo_weights, bias)
+        if begun:
+            forward_pre(parts[1:], [h_hi], constants)
+        else:
+            forward_pre(parts, [h_lo, h_hi], constants)
+        forward_act(layer, parts, constants)
         by_i, by_j = collect(parts[0])
         nb_i, nb_j = collect(parts[1])
         own = (by_i - by_j[:, :L], -by_j[:, L:])
@@ -359,9 +371,11 @@
         return own, total
 
     def node_forward(layer, h, total):
-        agg = dot(total.astype(BF16), edge_out_ref[layer]).astype(BF16)
-        joined = jnp.concatenate([h, agg], axis=1)
-        pre = dot(joined, node_in_ref[layer]) + node_bias_ref[layer : layer + 1, :]
+        total = total.astype(BF16)
+        weights = jnp.concatenate([node_in_ref[layer, :L, :], through[layer]], axis=0)
+        pre = dot(jnp.concatenate([h, total], axis=1), weights) + node_bias_ref[layer : layer + 1, :]
+        agg = dot(total[:ROWS], edge_out_ref[layer]).astype(BF16)
+        joined = jnp.concatenate([h[:ROWS], agg], axis=1)
         sig = 0.5 * jnp.tanh(0.5 * pre) + 0.5
         act = pre * sig
         hidden = act.astype(BF16)
@@ -374,7 +388,8 @@
 
     def node_backward(layer, grad, kept):
         size = grad.shape[0]
-        joined, node_slope, hidden, normed, inv = (v[:size] for v in kept)
+        joined = kept[0]
+        node_slope, hidden, normed, inv = (v[:size] for v in kept[1:])
         gain_term = jnp.sum(grad[:ROWS] * normed[:ROWS], axis=0, keepdims=True)
         dnorm = grad * gain_ref[layer : layer + 1, :]
         mean_a = jnp.mean(dnorm, axis=1, keepdims=True)
@@ -382,10 +397,11 @@
         dout = ((dnorm - mean_a - normed * mean_b) * inv).astype(BF16)
         out_term = dot_tn(hidden[:ROWS], dout[:ROWS])
         dpre = (dot_nt(dout, node_out_ref[layer]) * node_slope).astype(BF16)
-        in_term = dot_tn(joined[:ROWS], dpre[:ROWS])
+        in_term = dot_tn(joined, dpre[:ROWS])
         bias_term = jnp.sum(dpre[:ROWS].astype(F32), axis=0, keepdims=True)
         dx = dot_nt(dpre, node_in_ref[layer])
-        return grad + dx[:, :L], dx[:, L:].astype(BF16), (in_term, bias_term, out_term, gain_term)
+        e = dot_nt(dpre, through[layer]).astype(BF16)
+        return grad + dx[:, :L], dx[:, L:].astype(BF16), e, (in_term, bias_term, out_term, gain_term)
 
     def backward_rows(layer, parts, sources, both):
         gather(parts, sources, both, work_s)
@@ -438,10 +454,18 @@
 
     h0_lo = lat_ref[0]
     h0_hi = around(low_ref[0:LAT_HALO, :], upp_ref[0:LAT_HALO, :], LAT_HALO, ROWS)
-    own0, total0 = (jnp.concatenate(t, axis=0) for t in edge_forward(0, h0_lo, h0_hi, 3))
+    constants0 = edge_constants(0, h0_lo, h0_hi)
+    forward_pre([own_part], [h0_lo], constants0)
+    for k in range(SURE[3]):
+        set_block(BLK * k, nb_rows[k], lanes, subs, *nb_refs)
+    through = [dot(edge_out_ref[s], node_in_ref[s, L:, :]).astype(BF16) for s in range(2)]
+    further(3, lambda at: set_block(at, nb_rows[at // BLK], lanes, subs, *nb_refs))
+    own0, total0 = (jnp.concatenate(t, axis=0) for t in edge_forward(0, h0_lo, h0_hi, 3, constants0, True))
     h0 = jnp.concatenate([h0_lo, h0_hi], axis=0)
     h1, kept0 = node_forward(0, h0, total0)
-    own1, total1 = (jnp.concatenate(t, axis=0) for t in edge_forward(1, h1[:ROWS], h1[ROWS:], 2))
+    h1_lo, h1_hi = h1[:ROWS], h1[ROWS:]
+    constants1 = edge_constants(1, h1_lo, h1_hi)
+    own1, total1 = (jnp.concatenate(t, axis=0) for t in edge_forward(1, h1_lo, h1_hi, 2, constants1, False))
     near = ROWS + 2 * COT_HALO
     h2, kept1 = node_forward(1, h1[:near], total1[:near])
     final_v[...] = h2[:ROWS]
@@ -462,9 +486,9 @@
         return jnp.concatenate([value, jnp.zeros((2 * ROWS - value.shape[0],) + value.shape[1:], value.dtype)], axis=0)
 
     def layer_back(layer, grad, kept, own_total, h, last, keep_rows):
-        part, dagg, node_terms = node_backward(layer, grad, kept)
+        part, dagg, e, node_terms = node_backward(layer, grad, kept)
         spread = with_zeros(dagg)
-        e = with_zeros(dot_nt(dagg, edge_out_ref[layer]).astype(BF16))
+        e = with_zeros(e)
         q_own, q_all, geo = edge_backward(layer, e[:ROWS], e[ROWS:], last)
         out_term = dot_tn(own_total.astype(BF16), spread)
         in_term = dot_tn(h, q_own.astype(BF16))
@@ -558,6 +582,10 @@
         edge_bias[layer : layer + 1, :] = small[4]
         node_bias[layer : layer + 1, :] = small[5]
         gain[layer : layer + 1, :] = small[6]
+
+
+def rows_of(array):
+    return jnp.transpose(array, (1, 0, 2)).reshape(-1, array.shape[2])
 
 
 def vmem(count):
@@ -615,7 +643,7 @@
             in_specs=vmem(6),
             out_specs=tuple(vmem(8)),
             compiler_params=pltpu.CompilerParams(vmem_limit_bytes=16 * 1024 * 1024),
-            cost_estimate=pl.CostEstimate(flops=2000000, bytes_accessed=8000000, transcendentals=0),
+            cost_estimate=pl.CostEstimate(flops=4000000000, bytes_accessed=40000000, transcendentals=0),
             name="own",
         )(pair_count, pairs, geometry, weights[1], weights[4], weights[6])
         final, grad, arrivals, packed = pl.pallas_call(
@@ -647,13 +675,15 @@
                 pltpu.VMEM((ROWS, L), BF16),
                 pltpu.VMEM((2, MIG, L), BF16),
                 pltpu.VMEM((ROWS, L), F32),
+                pltpu.VMEM((2 * weights[0].shape[1], L), F32),
+                pltpu.VMEM(weights[0].shape, BF16),
                 pltpu.SemaphoreType.DMA((3,)),
             ],
             compiler_params=params,
             name="steps",
         )(
             latents, cotangent, *own[:5], from_b, from_a,
-            weights[0], own[5], weights[2], weights[3], own[6], weights[5], own[7],
+            rows_of(weights[0]), own[5], weights[2], weights[3], own[6], weights[5], own[7],
         )
 
         got = fold(None, lax.all_to_all(packed, group, 0, 0, tiled=True))

time: 89.7 us -> 88.8 us (0.990)
  local copies, waits for them, and re-layouts: 1.02 us -> 0.07 us
    unnamed x21 -> x22, local copies, waits for them, and re-layouts: 1.02 us -> 0.07 us
  transfers between devices with their start and end apart: 3 -> 3, of which waited for: 1 -> 2; matrix products, arithmetic and copies ran while one was open for 1% -> 0% of each run, Pallas kernels for 1% -> 1%
where the time goes in v6:
time: 88.8 us; the launch traced here: 88.4 us
  blocking collectives  52 us (59%)
  starting transfers between devices  17.4 us (20%)
  Pallas kernels  15.9 us (18%)
  waiting for transfers between devices  1.5 us (2%)
  between operations  1.5 us (2%)
    all_to_all x1, blocking collectives, on_device(): got = lax.all_to_all(got, 'zh', 0, 0, tiled=True)  22.7 us
    all_to_all x1, blocking collectives, on_device(): got = fold(None, lax.all_to_all(packed, group, 0, 0, tiled=True))  15 us
    all_to_all x1, blocking collectives, on_device(): got = lax.all_to_all(fold(chunks, got), group, 0, 0, tiled=True)  14.3 us
    ppermute x1, starting transfers between devices, on_device(): from_b = lax.ppermute(to_b, space, cross + [(j, i) for i, j in cross])  13.4 us
    pallas_call x1, Pallas kernels, on_device(): pl.pallas_call(lambda *refs: main_kernel(chunks, *refs), out_shape=(jax.S...  11.2 us
    pallas_call x1, Pallas kernels, on_device(): pl.pallas_call(pack_kernel, out_shape=(sent, sent), in_specs=[pl.BlockSpe...  2.69 us
    ppermute x1, starting transfers between devices, on_device(): from_a = lax.ppermute(to_a, space, near + [(j, i) for i, j in near])  2.05 us
    ppermute x1, starting transfers between devices, on_device(): got = fold(n_h, got[None], lax.ppermute(got, 'c', [(0, 1), (1, 0)]))  1.92 us
  transfers between devices with their start and end apart: 3, of which 2 were waited for; matrix products, arithmetic and copies ran while one was open for 0% of the time, Pallas kernels for 1%

profile of v6, /device:TPU:2, one launch (start us, length us, event | category | flops | bytes accessed | tf_op | source)
XLA Modules:
  0.0 88.4 jit_solution(15210419690812111218)
XLA Ops:
  1.3 0.0 copy-start.6
  1.3 0.0 copy-start.7
  1.3 2.7 %pack.1 = (bf16[272,128]{1,0:T(8,128)(2,1)}, bf16[272,128]{1,0:T(8,128)(2,1)}) custom-call(s32[1,1]{1,0:T(1,128)S(6)} %copy.23.count_ref, bf16[1,256,128]{2,1,0:T(8,128)(2,1)} %refs_0_.1, bf16[1,256,128]{2,1,0:T(8,128)(2,1)} %refs_1_.1, s32[1,2,1024]{2,1,0:T(2,128)} %pairs_ref.3, bf16[1,4,1024]{2,1,0:T(4,128)(2,1)} %geo_ref.3, s32[1,2,16]{2,1,0:T(2,128)} %leav_ref.1), custom_call_target="tpu_custom_call" | custom-call | tf_op jit(solution)/shard_map/pack/pallas_call | solution.py:613
  4.0 0.0 copy-start.9
  4.0 0.0 copy-start.10
  4.0 0.0 copy-start.8
  4.0 13.4 %collective-permute-start = (bf16[272,128]{1,0:T(8,128)(2,1)}, bf16[272,128]{1,0:T(8,128)(2,1)S(1)}, u32[]{:S(2)}, u32[]{:S(2)}) collective-permute-start(bf16[272,128]{1,0:T(8,128)(2,1)} %get-tuple-element.36), channel_id=1, source_target_pairs={{4,8},{12,16},{20,24},{28,32},{36,40},{44,48},{52,56},{60,64},{68,... | collective-permute-start | bytes 208904 | tf_op jit(solution)/shard_map/ppermute | solution.py:631
  17.5 0.0 copy-start
  17.5 0.0 copy-start.1
  17.5 0.0 copy-start.2
  17.5 0.0 copy-start.3
  17.5 0.0 copy-start.4
  17.5 0.0 copy-start.5
  17.5 2.1 %collective-permute-start.1 = (bf16[272,128]{1,0:T(8,128)(2,1)}, bf16[272,128]{1,0:T(8,128)(2,1)S(1)}, u32[]{:S(2)}, u32[]{:S(2)}) collective-permute-start(bf16[272,128]{1,0:T(8,128)(2,1)} %get-tuple-element.37), channel_id=1, source_target_pairs={{0,4},{8,12},{16,20},{24,28},{32,36},{40,44},{48,52},{56,60},{64,6... | collective-permute-start | bytes 208904 | tf_op jit(solution)/shard_map/ppermute | solution.py:632
  19.6 0.0 copy-done.6
  19.6 0.0 copy-done.7
  19.6 0.0 copy-done.9
  19.6 0.0 copy-done.10
  19.6 0.0 copy-done.8
  19.7 1.0 %own.1 = (bf16[2,1024,256]{2,1,0:T(8,128)(2,1)S(1)}, bf16[2,256,1024]{2,1,0:T(8,128)(2,1)S(1)}, f32[1024,128]{1,0:T(8,128)S(1)}, bf16[1024,8]{1,0:T(8,128)(2,1)S...) custom-call(s32[1,1]{1,0:T(1,128)S(6)} %copy.23.count_ref, ...), custom_call_target="tpu_custom_call" | custom-call | flops 4000000000 | bytes 40000000 | tf_op jit(solution)/shard_map/own/pallas_call | solution.py:633
  20.7 0.0 collective-permute-done.refs_7_
  20.7 0.4 collective-permute-done.1.refs_8_
  21.0 0.0 copy-done
  21.0 0.0 copy-done.1
  21.0 0.0 copy-done.2
  21.1 0.0 copy-done.3
  21.1 0.0 copy-done.4
  21.1 0.0 copy-done.5
  21.1 11.2 %steps.1 = (bf16[1,256,128]{2,1,0:T(8,128)(2,1)}, f32[1,256,128]{2,1,0:T(8,128)}, bf16[1,2,16,128]{3,2,1,0:T(8,128)(2,1)}, bf16[32,56,128]{2,1,0:T(8,128)(2,1)S(1)}) custom-call(bf16[1,256,128]{2,1,0:T(8,128)(2,1)S(1)} %copy-done, bf16[1,256,128]{2,1,0:T(8,128)(2,1)S(1)} %copy-done.1, bf16[2,1024,256]{2,1,0:T(8,128)(2,1)S(1)} %get-tuple-element.31.refs_2_, ...), custom_call_target="tpu_custom_call" | custom-call | tf_op jit(solution)/shard_map/steps/pallas_call | solution.py:649
  32.3 15.0 %all_to_all.15.refs_0_ = bf16[32,56,128]{2,1,0:T(8,128)(2,1)S(1)} all-to-all(bf16[32,56,128]{2,1,0:T(8,128)(2,1)S(1)} %get-tuple-element.44), channel_id=1, replica_groups=mesh['y'=4,'zh'=8,'zl'=2,'c'=2,'x'=4] {'zl','y','x'}, dimensions={0} | all-to-all | bytes 917504 | tf_op jit(solution)/shard_map/all_to_all | solution.py:689
  47.3 0.1 fold.3
  47.4 1.9 %collective-permute-start.2 = (bf16[56,128]{1,0:T(8,128)(2,1)S(1)}, bf16[56,128]{1,0:T(8,128)(2,1)S(1)}, u32[]{:S(2)}, u32[]{:S(2)}) collective-permute-start(bf16[56,128]{1,0:T(8,128)(2,1)S(1)} %fold.3), channel_id=1, source_target_pairs={{0,4},{4,0},{1,5},{5,1},{2,6},{6,2},{3,7},{7,3},{8,12},{12,8},{9,1... | collective-permute-start | bytes 43016 | tf_op jit(solution)/shard_map/ppermute | solution.py:690
  49.3 1.1 %collective-permute-done.2.refs_1_ = bf16[56,128]{1,0:T(8,128)(2,1)S(1)} collective-permute-done((bf16[56,128]{1,0:T(8,128)(2,1)S(1)}, bf16[56,128]{1,0:T(8,128)(2,1)S(1)}, u32[]{:S(2)}, u32[]{:S(2)}) %collective-permute-start.2) | collective-permute-done | bytes 14368 | tf_op jit(solution)/shard_map/ppermute | solution.py:690
  50.4 22.7 %all_to_all.16.refs_0_ = bf16[8,56,128]{2,1,0:T(8,128)(2,1)S(1)} all-to-all(bf16[8,56,128]{2,1,0:T(8,128)(2,1)S(1)} %fold.4), channel_id=1, replica_groups=mesh['y'=4,'zh'=8,'zl'=2,'c'=2,'x'=4] {'zh'}, dimensions={0} | all-to-all | bytes 229376 | tf_op jit(solution)/shard_map/all_to_all | solution.py:691
  73.2 14.3 %all_to_all.17.refs_0_ = bf16[32,56,128]{2,1,0:T(8,128)(2,1)S(1)} all-to-all(bf16[32,56,128]{2,1,0:T(8,128)(2,1)S(1)} %fold.5), channel_id=1, replica_groups=mesh['y'=4,'zh'=8,'zl'=2,'c'=2,'x'=4] {'zl','y','x'}, dimensions={0} | all-to-all | bytes 917504 | tf_op jit(solution)/shard_map/all_to_all | solution.py:692
  87.5 0.9 %unpack.1 = (f32[520,128]{1,0:T(8,128)}, f32[2,128]{1,0:T(2,128)}, f32[2,128,128]{2,1,0:T(8,128)}, f32[2,256,128]{2,1,0:T(8,128)}, f32[2,128]{1,0:T(2,128)}, /*index=5*/f32[2,128,128]{2,1,0:T(8,128)}, f32[2,128]{1,0:T(2,128)}) custom-call(bf16[32,56,128]{2,1,0:T(8,128)(2,1)S(1)} %all_to_all.17.refs_0_), custom_call_target="tpu_custom_call" | custom-call | tf_op jit(solution)/shard_map/unpack/pallas_call | solution.py:694
  (2 shorter events, 0.1 us)
Async XLA Ops:
  1.3 18.3 %copy-start.6 = (s32[1,2,1024]{2,1,0:T(2,128)S(1)}, s32[1,2,1024]{2,1,0:T(2,128)}, u32[]{:S(2)}) copy-start(s32[1,2,1024]{2,1,0:T(2,128)} %pairs_ref.3) | copy-start | bytes 24580
  1.3 18.3 %copy-start.7 = (bf16[1,4,1024]{2,1,0:T(4,128)(2,1)S(1)}, bf16[1,4,1024]{2,1,0:T(4,128)(2,1)}, u32[]{:S(2)}) copy-start(bf16[1,4,1024]{2,1,0:T(4,128)(2,1)} %geo_ref.3) | copy-start | bytes 24580
  4.0 15.6 %copy-start.9 = (f32[2,128]{1,0:T(2,128)S(1)}, f32[2,128]{1,0:T(2,128)}, u32[]{:S(2)}) copy-start(f32[2,128]{1,0:T(2,128)} %bias_n.1) | copy-start | bytes 3076
  4.0 15.6 %copy-start.10 = (f32[2,128]{1,0:T(2,128)S(1)}, f32[2,128]{1,0:T(2,128)}, u32[]{:S(2)}) copy-start(f32[2,128]{1,0:T(2,128)} %gain.1) | copy-start | bytes 3076
  4.0 15.6 %copy-start.8 = (f32[2,128]{1,0:T(2,128)S(1)}, f32[2,128]{1,0:T(2,128)}, u32[]{:S(2)}) copy-start(f32[2,128]{1,0:T(2,128)} %bias_e.1) | copy-start | bytes 3076
  4.0 16.6 %collective-permute-start = (bf16[272,128]{1,0:T(8,128)(2,1)}, bf16[272,128]{1,0:T(8,128)(2,1)S(1)}, u32[]{:S(2)}, u32[]{:S(2)}) collective-permute-start(bf16[272,128]{1,0:T(8,128)(2,1)} %get-tuple-element.36), channel_id=1, source_target_pairs={{4,8},{12,16},{20,24},{28,32},{36,40},{44,48},{52,56},{60,64},{68,... | collective-permute-start | bytes 208904 | tf_op jit(solution)/shard_map/ppermute | solution.py:631
  17.5 3.6 %copy-start = (bf16[1,256,128]{2,1,0:T(8,128)(2,1)S(1)}, bf16[1,256,128]{2,1,0:T(8,128)(2,1)}, u32[]{:S(2)}) copy-start(bf16[1,256,128]{2,1,0:T(8,128)(2,1)} %refs_0_.1) | copy-start | bytes 196612
  17.5 3.6 %copy-start.1 = (bf16[1,256,128]{2,1,0:T(8,128)(2,1)S(1)}, bf16[1,256,128]{2,1,0:T(8,128)(2,1)}, u32[]{:S(2)}) copy-start(bf16[1,256,128]{2,1,0:T(8,128)(2,1)} %refs_1_.1) | copy-start | bytes 196612
  17.5 3.6 %copy-start.2 = (bf16[2,260,128]{2,0,1:T(2,128)(2,1)S(1)}, bf16[2,260,128]{2,0,1:T(2,128)(2,1)}, u32[]{:S(2)}) copy-start(bf16[2,260,128]{2,0,1:T(2,128)(2,1)} %param.19) | copy-start | bytes 399364
  17.5 3.5 %copy-start.3 = (bf16[2,256,128]{2,1,0:T(8,128)(2,1)S(1)}, bf16[2,256,128]{2,1,0:T(8,128)(2,1)}, u32[]{:S(2)}) copy-start(bf16[2,256,128]{2,1,0:T(8,128)(2,1)} %refs_12_.1) | copy-start | bytes 393220
  17.5 3.5 %copy-start.4 = (bf16[2,128,128]{2,1,0:T(8,128)(2,1)S(1)}, bf16[2,128,128]{2,1,0:T(8,128)(2,1)}, u32[]{:S(2)}) copy-start(bf16[2,128,128]{2,1,0:T(8,128)(2,1)} %refs_11_.1) | copy-start | bytes 196612
  17.5 3.5 %copy-start.5 = (bf16[2,128,128]{2,1,0:T(8,128)(2,1)S(1)}, bf16[2,128,128]{2,1,0:T(8,128)(2,1)}, u32[]{:S(2)}) copy-start(bf16[2,128,128]{2,1,0:T(8,128)(2,1)} %refs_14_.1) | copy-start | bytes 196612
  17.5 3.5 %collective-permute-start.1 = (bf16[272,128]{1,0:T(8,128)(2,1)}, bf16[272,128]{1,0:T(8,128)(2,1)S(1)}, u32[]{:S(2)}, u32[]{:S(2)}) collective-permute-start(bf16[272,128]{1,0:T(8,128)(2,1)} %get-tuple-element.37), channel_id=1, source_target_pairs={{0,4},{8,12},{16,20},{24,28},{32,36},{40,44},{48,52},{56,60},{64,6... | collective-permute-start | bytes 208904 | tf_op jit(solution)/shard_map/ppermute | solution.py:632
  47.4 3.1 %collective-permute-start.2 = (bf16[56,128]{1,0:T(8,128)(2,1)S(1)}, bf16[56,128]{1,0:T(8,128)(2,1)S(1)}, u32[]{:S(2)}, u32[]{:S(2)}) collective-permute-start(bf16[56,128]{1,0:T(8,128)(2,1)S(1)} %fold.3), channel_id=1, source_target_pairs={{0,4},{4,0},{1,5},{5,1},{2,6},{6,2},{3,7},{7,3},{8,12},{12,8},{9,1... | collective-permute-start | bytes 43016 | tf_op jit(solution)/shard_map/ppermute | solution.py:690

commit v7 on v6

--- a/solution.py
+++ b/solution.py
@@ -114,18 +114,17 @@
     before = dot(masked(jnp.logical_and(same, col_b < row_b)), sums.astype(BF16))
     at = inside + before
     lane = lax.broadcasted_iota(jnp.int32, (1, 128), 1)
-    col_w = lax.broadcasted_iota(jnp.int32, (128, BLK), 1).astype(F32)
+    slots = lax.broadcasted_iota(jnp.int32, (BLK, EMAX), 0).astype(F32)
     places = []
     for k in range(2):
         rank = jnp.full((8, 128), -1.0, F32)
         for c in range(4):
             here = 32 * k + 8 * c
             rank = jnp.where(kinds[k] == c, at[here : here + 8, :], rank)
-        places.append(jnp.transpose(rank))
+        places.append(jnp.concatenate([rank[q : q + 1, :] for q in range(8)], axis=1))
 
     def move(k, t, shift):
-        picks = [masked(places[k][:, q : q + 1] == col_w + shift) for q in range(8)]
-        moved = dot(rows[k], jnp.concatenate(picks, axis=0))
+        moved = jnp.transpose(dot_nt(masked(places[k] - shift == slots), rows[k]))
         ref = (a_ref, b_ref)[k]
         spot = D_AT + 16 * t
         if not isinstance(t, int):
@@ -230,6 +229,7 @@
     work_d,
     work_e,
     work_s,
+    from_geo,
     t_nb,
     q_nb,
     final_v,
@@ -306,19 +306,21 @@
             work_p[pl.ds(to, size), :] = dot(refs[0][1, pl.ds(at, size), :], both)
 
     def forward_pre(parts, sources, constants):
-        both, weights, geo_weights, _ = constants
+        both, weights, _ = constants
         gather(parts, sources, both, work_x)
         for hi, here in pieces(parts):
             is_hi = hi[...] > 0.5
             work_x[here, L:] = jnp.where(is_hi, work_p[here, L:], work_p[here, :L]).astype(BF16)
-        for refs, at, size, to in parts:
-            rows = pl.ds(to, size)
-            work_p[rows, :] = dot(work_x[rows, :], weights) + dot(refs[3][pl.ds(at, size), :], geo_weights)
+        for _, _, size, to in parts:
+            work_p[pl.ds(to, size), :] = dot(work_x[pl.ds(to, size), :], weights)
 
     def forward_act(layer, parts, constants):
-        bias = constants[3]
+        bias = constants[2]
         for hi, here in pieces(parts):
-            pre = work_p[here, :] + bias
+            by_pair = from_geo[here, L * layer : L * layer + L]
+            fwd = work_p[here, :L] + (bias + by_pair)
+            rev = work_p[here, L:] + (bias - by_pair)
+            pre = jnp.concatenate([fwd, rev], axis=1)
             sig = 0.5 * jnp.tanh(0.5 * pre) + 0.5
             act = pre * sig
             slope[layer, here, :] = sig + act * (1.0 - sig)
@@ -332,13 +334,7 @@
     def edge_constants(layer, h_lo, h_hi):
         straight, crossed = edge_weights(layer)
         weights = jnp.concatenate([straight, crossed], axis=0)
-        geo_top = edge_in_ref[layer, 2 * L : 2 * L + 4, :].astype(F32)
-        geo_weights = jnp.concatenate(
-            [jnp.zeros((4, 2 * L), F32), jnp.concatenate([geo_top, -geo_top], axis=1)], axis=0
-        ).astype(BF16)
-        bias_row = edge_bias_ref[layer : layer + 1, :]
-        bias = jnp.concatenate([bias_row, bias_row], axis=1)
-        return jnp.concatenate([h_lo, h_hi], axis=1), weights, geo_weights, bias
+        return jnp.concatenate([h_lo, h_hi], axis=1), weights, edge_bias_ref[layer : layer + 1, :]
 
     def edge_forward(layer, h_lo, h_hi, last, constants, begun):
         t_nb[...] = jnp.zeros_like(t_nb)
@@ -455,11 +451,24 @@
     h0_lo = lat_ref[0]
     h0_hi = around(low_ref[0:LAT_HALO, :], upp_ref[0:LAT_HALO, :], LAT_HALO, ROWS)
     constants0 = edge_constants(0, h0_lo, h0_hi)
+    geo_weights = jnp.concatenate([edge_in_ref[s, 2 * L : 2 * L + 4, :].astype(F32) for s in range(2)], axis=1)
+    geo_weights = jnp.concatenate([jnp.zeros((4, 2 * L), F32), geo_weights], axis=0).astype(BF16)
+
+    def set_geo(part):
+        refs, at, size, to = part
+        from_geo[pl.ds(to, size), :] = dot(refs[3][pl.ds(at, size), :], geo_weights)
+
+    def set_further(at):
+        set_block(at, nb_rows[at // BLK], lanes, subs, *nb_refs)
+        set_geo(nb_part(at, BLK))
+
     forward_pre([own_part], [h0_lo], constants0)
+    set_geo(own_part)
     for k in range(SURE[3]):
         set_block(BLK * k, nb_rows[k], lanes, subs, *nb_refs)
     through = [dot(edge_out_ref[s], node_in_ref[s, L:, :]).astype(BF16) for s in range(2)]
-    further(3, lambda at: set_block(at, nb_rows[at // BLK], lanes, subs, *nb_refs))
+    set_geo(nb_part(0, BLK * SURE[3]))
+    further(3, set_further)
     own0, total0 = (jnp.concatenate(t, axis=0) for t in edge_forward(0, h0_lo, h0_hi, 3, constants0, True))
     h0 = jnp.concatenate([h0_lo, h0_hi], axis=0)
     h1, kept0 = node_forward(0, h0, total0)
@@ -600,8 +609,9 @@
     n_y = n_space // (n_c * n_z)
     n_l = 2 if n_z > 4 else 1
     n_h = n_z // n_l
-    fine = Mesh(mesh.devices.reshape(n_y, n_h, n_l, n_c, n_x), ("y", "zh", "zl", "c", "x"))
-    space = ("y", "zh", "zl", "c")
+    n_b = 2 if n_h > 4 else 1
+    fine = Mesh(mesh.devices.reshape(n_y, n_h // n_b, n_b, n_l, n_c, n_x), ("y", "za", "zb", "zl", "c", "x"))
+    space = ("y", "za", "zb", "zl", "c")
     group = ("zl", "y", "x")
     chunks = n_y * n_l * n_x
     size = MAIN // chunks
@@ -670,6 +680,7 @@
                 pltpu.VMEM((ALL_PAIRS, 2 * L), BF16),
                 pltpu.VMEM((ALL_PAIRS, 2 * L), BF16),
                 pltpu.VMEM((ALL_PAIRS, L), F32),
+                pltpu.VMEM((ALL_PAIRS, 2 * L), F32),
                 pltpu.VMEM((ROWS, 2 * L), F32),
                 pltpu.VMEM((2 * ROWS, 2 * L), F32),
                 pltpu.VMEM((ROWS, L), BF16),
@@ -688,7 +699,7 @@
 
         got = fold(None, lax.all_to_all(packed, group, 0, 0, tiled=True))
         got = fold(n_h, got[None], lax.ppermute(got, "c", [(0, 1), (1, 0)]))
-        got = lax.all_to_all(got, "zh", 0, 0, tiled=True)
+        got = lax.all_to_all(got, ("zb", "za"), 0, 0, tiled=True)
         got = lax.all_to_all(fold(chunks, got), group, 0, 0, tiled=True)
 
         grads = pl.pallas_call(

time: 88.8 us -> 87.4 us (0.984)
  the two profiles are of different devices: /device:TPU:2 before, /device:TPU:64 now
where the time goes in v7:
time: 87.4 us; the launch traced here: 87.1 us
  blocking collectives  60.6 us (69%)
  Pallas kernels  15.7 us (18%)
  starting transfers between devices  8.02 us (9%)
  between operations  1.52 us (2%)
  waiting for transfers between devices  1.16 us (1%)
    all_to_all x1, blocking collectives, on_device(): got = lax.all_to_all(got, ('zb', 'za'), 0, 0, tiled=True)  24.9 us
    all_to_all x1, blocking collectives, on_device(): got = fold(None, lax.all_to_all(packed, group, 0, 0, tiled=True))  21.1 us
    all_to_all x1, blocking collectives, on_device(): got = lax.all_to_all(fold(chunks, got), group, 0, 0, tiled=True)  14.6 us
    pallas_call x1, Pallas kernels, on_device(): pl.pallas_call(lambda *refs: main_kernel(chunks, *refs), out_shape=(jax.S...  11 us
    ppermute x1, starting transfers between devices, on_device(): from_a = lax.ppermute(to_a, space, near + [(j, i) for i, j in near])  4.06 us
    pallas_call x1, Pallas kernels, on_device(): pl.pallas_call(pack_kernel, out_shape=(sent, sent), in_specs=[pl.BlockSpe...  2.63 us
    ppermute x1, starting transfers between devices, on_device(): from_b = lax.ppermute(to_b, space, cross + [(j, i) for i, j in cross])  2.05 us
    ppermute x1, starting transfers between devices, on_device(): got = fold(n_h, got[None], lax.ppermute(got, 'c', [(0, 1), (1, 0)]))  1.92 us
  transfers between devices with their start and end apart: 3, of which 1 were waited for; matrix products, arithmetic and copies ran while one was open for 0% of the time, Pallas kernels for 1%

profile of v7, /device:TPU:64, one launch (start us, length us, event | category | flops | bytes accessed | tf_op | source)
XLA Modules:
  0.0 87.1 jit_solution(2519944028260725259)
XLA Ops:
  1.3 0.0 copy-start.6
  1.3 0.0 copy-start.7
  1.3 2.6 %pack.1 = (bf16[272,128]{1,0:T(8,128)(2,1)}, bf16[272,128]{1,0:T(8,128)(2,1)}) custom-call(s32[1,1]{1,0:T(1,128)S(6)} %copy.23.count_ref, bf16[1,256,128]{2,1,0:T(8,128)(2,1)} %refs_0_.1, bf16[1,256,128]{2,1,0:T(8,128)(2,1)} %refs_1_.1, s32[1,2,1024]{2,1,0:T(2,128)} %pairs_ref.3, bf16[1,4,1024]{2,1,0:T(4,128)(2,1)} %geo_ref.3, s32[1,2,16]{2,1,0:T(2,128)} %leav_ref.1), custom_call_target="tpu_custom_call" | custom-call | tf_op jit(solution)/shard_map/pack/pallas_call | solution.py:623
  3.9 0.0 copy-start.9
  4.0 0.0 copy-start.10
  4.0 0.0 copy-start.8
  4.0 2.1 %collective-permute-start = (bf16[272,128]{1,0:T(8,128)(2,1)}, bf16[272,128]{1,0:T(8,128)(2,1)S(1)}, u32[]{:S(2)}, u32[]{:S(2)}) collective-permute-start(bf16[272,128]{1,0:T(8,128)(2,1)} %get-tuple-element.36), channel_id=1, source_target_pairs={{4,8},{12,16},{20,24},{28,32},{36,40},{44,48},{52,56},{60,64},{68,... | collective-permute-start | bytes 208904 | tf_op jit(solution)/shard_map/ppermute | solution.py:641
  6.0 0.0 copy-start
  6.1 0.0 copy-start.1
  6.1 0.0 copy-start.2
  6.1 0.0 copy-start.3
  6.1 0.0 copy-start.4
  6.1 0.0 copy-start.5
  6.1 4.1 %collective-permute-start.1 = (bf16[272,128]{1,0:T(8,128)(2,1)}, bf16[272,128]{1,0:T(8,128)(2,1)S(1)}, u32[]{:S(2)}, u32[]{:S(2)}) collective-permute-start(bf16[272,128]{1,0:T(8,128)(2,1)} %get-tuple-element.37), channel_id=1, source_target_pairs={{0,4},{8,12},{16,20},{24,28},{32,36},{40,44},{48,52},{56,60},{64,6... | collective-permute-start | bytes 208904 | tf_op jit(solution)/shard_map/ppermute | solution.py:642
  10.2 0.0 copy-done.6
  10.2 0.0 copy-done.7
  10.2 0.0 copy-done.9
  10.2 0.0 copy-done.10
  10.2 0.0 copy-done.8
  10.2 1.0 %own.1 = (bf16[2,1024,256]{2,1,0:T(8,128)(2,1)S(1)}, bf16[2,256,1024]{2,1,0:T(8,128)(2,1)S(1)}, f32[1024,128]{1,0:T(8,128)S(1)}, bf16[1024,8]{1,0:T(8,128)(2,1)S...) custom-call(s32[1,1]{1,0:T(1,128)S(6)} %copy.23.count_ref, ...), custom_call_target="tpu_custom_call" | custom-call | flops 4000000000 | bytes 40000000 | tf_op jit(solution)/shard_map/own/pallas_call | solution.py:643
  11.3 0.0 collective-permute-done.refs_7_
  11.3 0.0 collective-permute-done.1.refs_8_
  11.3 0.0 copy-done
  11.3 0.0 copy-done.1
  11.3 0.0 copy-done.2
  11.3 0.0 copy-done.3
  11.3 0.0 copy-done.4
  11.3 0.0 copy-done.5
  11.3 11.0 %steps.1 = (bf16[1,256,128]{2,1,0:T(8,128)(2,1)}, f32[1,256,128]{2,1,0:T(8,128)}, bf16[1,2,16,128]{3,2,1,0:T(8,128)(2,1)}, bf16[32,56,128]{2,1,0:T(8,128)(2,1)S(1)}) custom-call(bf16[1,256,128]{2,1,0:T(8,128)(2,1)S(1)} %copy-done, bf16[1,256,128]{2,1,0:T(8,128)(2,1)S(1)} %copy-done.1, bf16[2,1024,256]{2,1,0:T(8,128)(2,1)S(1)} %get-tuple-element.31.refs_2_, ...), custom_call_target="tpu_custom_call" | custom-call | tf_op jit(solution)/shard_map/steps/pallas_call | solution.py:659
  22.3 21.1 %all_to_all.15.refs_0_ = bf16[32,56,128]{2,1,0:T(8,128)(2,1)S(1)} all-to-all(bf16[32,56,128]{2,1,0:T(8,128)(2,1)S(1)} %get-tuple-element.44), channel_id=1, replica_groups=mesh['y'=4,'za'=4,'zb'=2,'zl'=2,'c'=2,'x'=4] {'zl','y','x'}, dimensions={0} | all-to-all | bytes 917504 | tf_op jit(solution)/shard_map/all_to_all | solution.py:700
  43.4 0.1 fold.3
  43.5 1.9 %collective-permute-start.2 = (bf16[56,128]{1,0:T(8,128)(2,1)S(1)}, bf16[56,128]{1,0:T(8,128)(2,1)S(1)}, u32[]{:S(2)}, u32[]{:S(2)}) collective-permute-start(bf16[56,128]{1,0:T(8,128)(2,1)S(1)} %fold.3), channel_id=1, source_target_pairs={{0,4},{4,0},{1,5},{5,1},{2,6},{6,2},{3,7},{7,3},{8,12},{12,8},{9,1... | collective-permute-start | bytes 43016 | tf_op jit(solution)/shard_map/ppermute | solution.py:701
  45.4 1.1 %collective-permute-done.2.refs_1_ = bf16[56,128]{1,0:T(8,128)(2,1)S(1)} collective-permute-done((bf16[56,128]{1,0:T(8,128)(2,1)S(1)}, bf16[56,128]{1,0:T(8,128)(2,1)S(1)}, u32[]{:S(2)}, u32[]{:S(2)}) %collective-permute-start.2) | collective-permute-done | bytes 14368 | tf_op jit(solution)/shard_map/ppermute | solution.py:701
  46.6 24.9 %all_to_all.16.refs_0_ = bf16[8,56,128]{2,1,0:T(8,128)(2,1)S(1)} all-to-all(bf16[8,56,128]{2,1,0:T(8,128)(2,1)S(1)} %fold.4), channel_id=1, replica_groups=mesh['y'=4,'za'=4,'zb'=2,'zl'=2,'c'=2,'x'=4] {'zb','za'}, dimensions={0} | all-to-all | bytes 229376 | tf_op jit(solution)/shard_map/all_to_all | solution.py:702
  71.6 14.6 %all_to_all.17.refs_0_ = bf16[32,56,128]{2,1,0:T(8,128)(2,1)S(1)} all-to-all(bf16[32,56,128]{2,1,0:T(8,128)(2,1)S(1)} %fold.5), channel_id=1, replica_groups=mesh['y'=4,'za'=4,'zb'=2,'zl'=2,'c'=2,'x'=4] {'zl','y','x'}, dimensions={0} | all-to-all | bytes 917504 | tf_op jit(solution)/shard_map/all_to_all | solution.py:703
  86.1 0.9 %unpack.1 = (f32[520,128]{1,0:T(8,128)}, f32[2,128]{1,0:T(2,128)}, f32[2,128,128]{2,1,0:T(8,128)}, f32[2,256,128]{2,1,0:T(8,128)}, f32[2,128]{1,0:T(2,128)}, /*index=5*/f32[2,128,128]{2,1,0:T(8,128)}, f32[2,128]{1,0:T(2,128)}) custom-call(bf16[32,56,128]{2,1,0:T(8,128)(2,1)S(1)} %all_to_all.17.refs_0_), custom_call_target="tpu_custom_call" | custom-call | tf_op jit(solution)/shard_map/unpack/pallas_call | solution.py:705
  (2 shorter events, 0.1 us)
Async XLA Ops:
  1.3 8.9 %copy-start.6 = (s32[1,2,1024]{2,1,0:T(2,128)S(1)}, s32[1,2,1024]{2,1,0:T(2,128)}, u32[]{:S(2)}) copy-start(s32[1,2,1024]{2,1,0:T(2,128)} %pairs_ref.3) | copy-start | bytes 24580
  1.3 8.9 %copy-start.7 = (bf16[1,4,1024]{2,1,0:T(4,128)(2,1)S(1)}, bf16[1,4,1024]{2,1,0:T(4,128)(2,1)}, u32[]{:S(2)}) copy-start(bf16[1,4,1024]{2,1,0:T(4,128)(2,1)} %geo_ref.3) | copy-start | bytes 24580
  3.9 6.3 %copy-start.9 = (f32[2,128]{1,0:T(2,128)S(1)}, f32[2,128]{1,0:T(2,128)}, u32[]{:S(2)}) copy-start(f32[2,128]{1,0:T(2,128)} %bias_n.1) | copy-start | bytes 3076
  4.0 6.3 %copy-start.10 = (f32[2,128]{1,0:T(2,128)S(1)}, f32[2,128]{1,0:T(2,128)}, u32[]{:S(2)}) copy-start(f32[2,128]{1,0:T(2,128)} %gain.1) | copy-start | bytes 3076
  4.0 6.2 %copy-start.8 = (f32[2,128]{1,0:T(2,128)S(1)}, f32[2,128]{1,0:T(2,128)}, u32[]{:S(2)}) copy-start(f32[2,128]{1,0:T(2,128)} %bias_e.1) | copy-start | bytes 3076
  4.0 7.3 %collective-permute-start = (bf16[272,128]{1,0:T(8,128)(2,1)}, bf16[272,128]{1,0:T(8,128)(2,1)S(1)}, u32[]{:S(2)}, u32[]{:S(2)}) collective-permute-start(bf16[272,128]{1,0:T(8,128)(2,1)} %get-tuple-element.36), channel_id=1, source_target_pairs={{4,8},{12,16},{20,24},{28,32},{36,40},{44,48},{52,56},{60,64},{68,... | collective-permute-start | bytes 208904 | tf_op jit(solution)/shard_map/ppermute | solution.py:641
  6.0 5.2 %copy-start = (bf16[1,256,128]{2,1,0:T(8,128)(2,1)S(1)}, bf16[1,256,128]{2,1,0:T(8,128)(2,1)}, u32[]{:S(2)}) copy-start(bf16[1,256,128]{2,1,0:T(8,128)(2,1)} %refs_0_.1) | copy-start | bytes 196612
  6.1 5.2 %copy-start.1 = (bf16[1,256,128]{2,1,0:T(8,128)(2,1)S(1)}, bf16[1,256,128]{2,1,0:T(8,128)(2,1)}, u32[]{:S(2)}) copy-start(bf16[1,256,128]{2,1,0:T(8,128)(2,1)} %refs_1_.1) | copy-start | bytes 196612
  6.1 5.2 %copy-start.2 = (bf16[2,260,128]{2,0,1:T(2,128)(2,1)S(1)}, bf16[2,260,128]{2,0,1:T(2,128)(2,1)}, u32[]{:S(2)}) copy-start(bf16[2,260,128]{2,0,1:T(2,128)(2,1)} %param.19) | copy-start | bytes 399364
  6.1 5.2 %copy-start.3 = (bf16[2,256,128]{2,1,0:T(8,128)(2,1)S(1)}, bf16[2,256,128]{2,1,0:T(8,128)(2,1)}, u32[]{:S(2)}) copy-start(bf16[2,256,128]{2,1,0:T(8,128)(2,1)} %refs_12_.1) | copy-start | bytes 393220
  6.1 5.2 %copy-start.4 = (bf16[2,128,128]{2,1,0:T(8,128)(2,1)S(1)}, bf16[2,128,128]{2,1,0:T(8,128)(2,1)}, u32[]{:S(2)}) copy-start(bf16[2,128,128]{2,1,0:T(8,128)(2,1)} %refs_11_.1) | copy-start | bytes 196612
  6.1 5.2 %copy-start.5 = (bf16[2,128,128]{2,1,0:T(8,128)(2,1)S(1)}, bf16[2,128,128]{2,1,0:T(8,128)(2,1)}, u32[]{:S(2)}) copy-start(bf16[2,128,128]{2,1,0:T(8,128)(2,1)} %refs_14_.1) | copy-start | bytes 196612
  6.1 5.2 %collective-permute-start.1 = (bf16[272,128]{1,0:T(8,128)(2,1)}, bf16[272,128]{1,0:T(8,128)(2,1)S(1)}, u32[]{:S(2)}, u32[]{:S(2)}) collective-permute-start(bf16[272,128]{1,0:T(8,128)(2,1)} %get-tuple-element.37), channel_id=1, source_target_pairs={{0,4},{8,12},{16,20},{24,28},{32,36},{40,44},{48,52},{56,60},{64,6... | collective-permute-start | bytes 208904 | tf_op jit(solution)/shard_map/ppermute | solution.py:642
  43.5 3.1 %collective-permute-start.2 = (bf16[56,128]{1,0:T(8,128)(2,1)S(1)}, bf16[56,128]{1,0:T(8,128)(2,1)S(1)}, u32[]{:S(2)}, u32[]{:S(2)}) collective-permute-start(bf16[56,128]{1,0:T(8,128)(2,1)S(1)} %fold.3), channel_id=1, source_target_pairs={{0,4},{4,0},{1,5},{5,1},{2,6},{6,2},{3,7},{7,3},{8,12},{12,8},{9,1... | collective-permute-start | bytes 43016 | tf_op jit(solution)/shard_map/ppermute | solution.py:701

commit v8 on v7

--- a/solution.py
+++ b/solution.py
@@ -17,7 +17,7 @@
 NB_BLOCKS = EMAX // SIDE
 ALL_PAIRS = EMAX + 2 * EMAX
 SURE = (1, 2, 3, 4)
-CHUNK = 64
+CHUNK = 32
 LAT_HALO = 128
 COT_HALO = 64
 SENT = LAT_HALO + COT_HALO + 64 + 16
@@ -496,11 +496,11 @@
 
     def layer_back(layer, grad, kept, own_total, h, last, keep_rows):
         part, dagg, e, node_terms = node_backward(layer, grad, kept)
-        spread = with_zeros(dagg)
+        reached = ROWS + 64
         e = with_zeros(e)
         q_own, q_all, geo = edge_backward(layer, e[:ROWS], e[ROWS:], last)
-        out_term = dot_tn(own_total.astype(BF16), spread)
-        in_term = dot_tn(h, q_own.astype(BF16))
+        out_term = dot_tn(own_total[:reached].astype(BF16), dagg[:reached])
+        in_term = dot_tn(h[:reached], q_own[:reached].astype(BF16))
         straight, _ = edge_weights(layer)
         new = part[:keep_rows] + dot_nt(q_all[:keep_rows].astype(BF16), straight)
         return new, (in_term, geo, out_term) + node_terms
@@ -508,18 +508,13 @@
     cot = jnp.concatenate(
         [cot_ref[0], around(low_ref[LAT_HALO:D_AT, :], upp_ref[LAT_HALO:D_AT, :], COT_HALO, 2 * COT_HALO)], axis=0
     ).astype(F32)
-    grad1, terms1 = layer_back(1, cot, kept1, own1, h1, 1, ROWS + 64)
-    grad0, terms0 = layer_back(0, grad1, kept0, own0, h0, 0, ROWS)
-    grad_v[...] = grad0
-    copies[2].start()
-
     size = MAIN // chunks
     per = -(-EXTRA // chunks)
     packed_ref[:, size:, :] = jnp.zeros((chunks, packed_ref.shape[1] - size, L), BF16)
-    at = 0
-    extra = 0
-    for terms in (terms0, terms1):
+
+    def put(layer, terms):
         in_term, geo, out_term, node_in_term, node_bias_term, node_out_term, gain_term = terms
+        at = layer * (MAIN // 2)
         for value in (in_term[:, :L], in_term[:, L:], out_term, node_in_term, node_out_term):
             value = value.astype(BF16)
             while value.shape[0]:
@@ -529,10 +524,16 @@
                 at += take
         small = [geo[4 + g : 5 + g, :L] - geo[4 + g : 5 + g, L:] for g in range(4)]
         small += [geo[3:4, :L] + geo[3:4, L:], node_bias_term, gain_term]
-        for value in small:
+        for extra, value in enumerate(small, layer * (EXTRA // 2)):
             spot = size + extra % per
             packed_ref[extra // per, spot : spot + 1, :] = value.astype(BF16)
-            extra += 1
+
+    grad1, terms1 = layer_back(1, cot, kept1, own1, h1, 1, ROWS + 64)
+    put(1, terms1)
+    grad0, terms0 = layer_back(0, grad1, kept0, own0, h0, 0, ROWS)
+    grad_v[...] = grad0
+    copies[2].start()
+    put(0, terms0)
 
     for copy in copies:
         copy.wait()
@@ -697,10 +698,10 @@
             rows_of(weights[0]), own[5], weights[2], weights[3], own[6], weights[5], own[7],
         )
 
-        got = fold(None, lax.all_to_all(packed, group, 0, 0, tiled=True))
-        got = fold(n_h, got[None], lax.ppermute(got, "c", [(0, 1), (1, 0)]))
-        got = lax.all_to_all(got, ("zb", "za"), 0, 0, tiled=True)
-        got = lax.all_to_all(fold(chunks, got), group, 0, 0, tiled=True)
+        got = lax.all_to_all(packed, group, 0, 0, tiled=True)
+        got = fold(None, lax.all_to_all(fold(n_h, got), ("zb", "za"), 0, 0, tiled=True))
+        got = fold(chunks, got[None], lax.ppermute(got, "c", [(0, 1), (1, 0)]))
+        got = lax.all_to_all(got, group, 0, 0, tiled=True)
 
         grads = pl.pallas_call(
             lambda *refs: unpack_kernel(chunks, *refs),

time: 87.4 us -> 88 us (level)
  the two profiles are of different devices: /device:TPU:64 before, /device:TPU:1 now
where the time goes in v8:
time: 88 us; the launch traced here: 87.7 us
  blocking collectives  46.6 us (53%)
  starting transfers between devices  22.9 us (26%)
  Pallas kernels  15.7 us (18%)
  between operations  1.52 us (2%)
    all_to_all x1, blocking collectives, on_device(): lax.all_to_all(fold(n_h, got), ('zb', 'za'), 0, 0, tiled=True)  18.4 us
    all_to_all x1, blocking collectives, on_device(): got = lax.all_to_all(packed, group, 0, 0, tiled=True)  14.3 us
    all_to_all x1, blocking collectives, on_device(): got = lax.all_to_all(got, group, 0, 0, tiled=True)  13.9 us
    ppermute x1, starting transfers between devices, on_device(): from_a = lax.ppermute(to_a, space, near + [(j, i) for i, j in near])  11.9 us
    pallas_call x1, Pallas kernels, on_device(): pl.pallas_call(lambda *refs: main_kernel(chunks, *refs), out_shape=(jax.S...  11 us
    ppermute x1, starting transfers between devices, on_device(): got = fold(chunks, got[None], lax.ppermute(got, 'c', [(0, 1), (1, 0)]))  5.97 us
    ppermute x1, starting transfers between devices, on_device(): from_b = lax.ppermute(to_b, space, cross + [(j, i) for i, j in cross])  5.07 us
    pallas_call x1, Pallas kernels, on_device(): pl.pallas_call(pack_kernel, out_shape=(sent, sent), in_specs=[pl.BlockSpe...  2.62 us
  transfers between devices with their start and end apart: 3, of which 1 were waited for; matrix products, arithmetic and copies ran while one was open for 0% of the time, Pallas kernels for 1%

profile of v8, /device:TPU:1, one launch (start us, length us, event | category | flops | bytes accessed | tf_op | source)
XLA Modules:
  0.0 87.7 jit_solution(7556291705779690669)
XLA Ops:
  1.3 0.0 copy-start.6
  1.3 0.0 copy-start.7
  1.3 2.6 %pack.1 = (bf16[272,128]{1,0:T(8,128)(2,1)}, bf16[272,128]{1,0:T(8,128)(2,1)}) custom-call(s32[1,1]{1,0:T(1,128)S(6)} %copy.23.count_ref, bf16[1,256,128]{2,1,0:T(8,128)(2,1)} %refs_0_.1, bf16[1,256,128]{2,1,0:T(8,128)(2,1)} %refs_1_.1, s32[1,2,1024]{2,1,0:T(2,128)} %pairs_ref.3, bf16[1,4,1024]{2,1,0:T(4,128)(2,1)} %geo_ref.3, s32[1,2,16]{2,1,0:T(2,128)} %leav_ref.1), custom_call_target="tpu_custom_call" | custom-call | tf_op jit(solution)/shard_map/pack/pallas_call | solution.py:624
  3.9 0.0 copy-start.9
  4.0 0.0 copy-start.10
  4.0 0.0 copy-start.8
  4.0 5.1 %collective-permute-start = (bf16[272,128]{1,0:T(8,128)(2,1)}, bf16[272,128]{1,0:T(8,128)(2,1)S(1)}, u32[]{:S(2)}, u32[]{:S(2)}) collective-permute-start(bf16[272,128]{1,0:T(8,128)(2,1)} %get-tuple-element.36), channel_id=1, source_target_pairs={{4,8},{12,16},{20,24},{28,32},{36,40},{44,48},{52,56},{60,64},{68,... | collective-permute-start | bytes 208904 | tf_op jit(solution)/shard_map/ppermute | solution.py:642
  9.1 0.0 copy-start
  9.1 0.0 copy-start.1
  9.1 0.0 copy-start.2
  9.1 0.0 copy-start.3
  9.1 0.0 copy-start.4
  9.1 0.0 copy-start.5
  9.1 11.9 %collective-permute-start.1 = (bf16[272,128]{1,0:T(8,128)(2,1)}, bf16[272,128]{1,0:T(8,128)(2,1)S(1)}, u32[]{:S(2)}, u32[]{:S(2)}) collective-permute-start(bf16[272,128]{1,0:T(8,128)(2,1)} %get-tuple-element.37), channel_id=1, source_target_pairs={{0,4},{8,12},{16,20},{24,28},{32,36},{40,44},{48,52},{56,60},{64,6... | collective-permute-start | bytes 208904 | tf_op jit(solution)/shard_map/ppermute | solution.py:643
  21.0 0.0 copy-done.6
  21.0 0.0 copy-done.7
  21.1 0.0 copy-done.9
  21.1 0.0 copy-done.10
  21.1 0.0 copy-done.8
  21.1 1.0 %own.1 = (bf16[2,1024,256]{2,1,0:T(8,128)(2,1)S(1)}, bf16[2,256,1024]{2,1,0:T(8,128)(2,1)S(1)}, f32[1024,128]{1,0:T(8,128)S(1)}, bf16[1024,8]{1,0:T(8,128)(2,1)S...) custom-call(s32[1,1]{1,0:T(1,128)S(6)} %copy.23.count_ref, ...), custom_call_target="tpu_custom_call" | custom-call | flops 4000000000 | bytes 40000000 | tf_op jit(solution)/shard_map/own/pallas_call | solution.py:644
  22.1 0.0 collective-permute-done.refs_7_
  22.1 0.0 collective-permute-done.1.refs_8_
  22.1 0.0 copy-done
  22.1 0.0 copy-done.1
  22.2 0.0 copy-done.2
  22.2 0.0 copy-done.3
  22.2 0.0 copy-done.4
  22.2 0.0 copy-done.5
  22.2 11.0 %steps.1 = (bf16[1,256,128]{2,1,0:T(8,128)(2,1)}, f32[1,256,128]{2,1,0:T(8,128)}, bf16[1,2,16,128]{3,2,1,0:T(8,128)(2,1)}, bf16[32,56,128]{2,1,0:T(8,128)(2,1)S(1)}) custom-call(bf16[1,256,128]{2,1,0:T(8,128)(2,1)S(1)} %copy-done, bf16[1,256,128]{2,1,0:T(8,128)(2,1)S(1)} %copy-done.1, bf16[2,1024,256]{2,1,0:T(8,128)(2,1)S(1)} %get-tuple-element.31.refs_2_, ...), custom_call_target="tpu_custom_call" | custom-call | tf_op jit(solution)/shard_map/steps/pallas_call | solution.py:660
  33.2 14.3 %all_to_all.15.refs_0_ = bf16[32,56,128]{2,1,0:T(8,128)(2,1)S(1)} all-to-all(bf16[32,56,128]{2,1,0:T(8,128)(2,1)S(1)} %get-tuple-element.44), channel_id=1, replica_groups=mesh['y'=4,'za'=4,'zb'=2,'zl'=2,'c'=2,'x'=4] {'zl','y','x'}, dimensions={0} | all-to-all | bytes 917504 | tf_op jit(solution)/shard_map/all_to_all | solution.py:701
  47.5 0.1 fold.3
  47.6 18.4 %all_to_all.16.refs_0_ = bf16[8,56,128]{2,1,0:T(8,128)(2,1)S(1)} all-to-all(bf16[8,56,128]{2,1,0:T(8,128)(2,1)S(1)} %fold.3), channel_id=1, replica_groups=mesh['y'=4,'za'=4,'zb'=2,'zl'=2,'c'=2,'x'=4] {'zb','za'}, dimensions={0} | all-to-all | bytes 229376 | tf_op jit(solution)/shard_map/all_to_all | solution.py:702
  66.1 6.0 %collective-permute-start.2 = (bf16[56,128]{1,0:T(8,128)(2,1)S(1)}, bf16[56,128]{1,0:T(8,128)(2,1)S(1)}, u32[]{:S(2)}, u32[]{:S(2)}) collective-permute-start(bf16[56,128]{1,0:T(8,128)(2,1)S(1)} %fold.4), channel_id=1, source_target_pairs={{0,4},{4,0},{1,5},{5,1},{2,6},{6,2},{3,7},{7,3},{8,12},{12,8},{9,1... | collective-permute-start | bytes 43016 | tf_op jit(solution)/shard_map/ppermute | solution.py:703
  72.0 0.8 collective-permute-done.2.refs_1_
  72.9 13.9 %all_to_all.17.refs_0_ = bf16[32,56,128]{2,1,0:T(8,128)(2,1)S(1)} all-to-all(bf16[32,56,128]{2,1,0:T(8,128)(2,1)S(1)} %fold.5), channel_id=1, replica_groups=mesh['y'=4,'za'=4,'zb'=2,'zl'=2,'c'=2,'x'=4] {'zl','y','x'}, dimensions={0} | all-to-all | bytes 917504 | tf_op jit(solution)/shard_map/all_to_all | solution.py:704
  86.7 0.9 %unpack.1 = (f32[520,128]{1,0:T(8,128)}, f32[2,128]{1,0:T(2,128)}, f32[2,128,128]{2,1,0:T(8,128)}, f32[2,256,128]{2,1,0:T(8,128)}, f32[2,128]{1,0:T(2,128)}, /*index=5*/f32[2,128,128]{2,1,0:T(8,128)}, f32[2,128]{1,0:T(2,128)}) custom-call(bf16[32,56,128]{2,1,0:T(8,128)(2,1)S(1)} %all_to_all.17.refs_0_), custom_call_target="tpu_custom_call" | custom-call | tf_op jit(solution)/shard_map/unpack/pallas_call | solution.py:706
  (2 shorter events, 0.1 us)
Async XLA Ops:
  1.3 19.7 %copy-start.6 = (s32[1,2,1024]{2,1,0:T(2,128)S(1)}, s32[1,2,1024]{2,1,0:T(2,128)}, u32[]{:S(2)}) copy-start(s32[1,2,1024]{2,1,0:T(2,128)} %pairs_ref.3) | copy-start | bytes 24580
  1.3 19.7 %copy-start.7 = (bf16[1,4,1024]{2,1,0:T(4,128)(2,1)S(1)}, bf16[1,4,1024]{2,1,0:T(4,128)(2,1)}, u32[]{:S(2)}) copy-start(bf16[1,4,1024]{2,1,0:T(4,128)(2,1)} %geo_ref.3) | copy-start | bytes 24580
  3.9 17.1 %copy-start.9 = (f32[2,128]{1,0:T(2,128)S(1)}, f32[2,128]{1,0:T(2,128)}, u32[]{:S(2)}) copy-start(f32[2,128]{1,0:T(2,128)} %bias_n.1) | copy-start | bytes 3076
  4.0 17.1 %copy-start.10 = (f32[2,128]{1,0:T(2,128)S(1)}, f32[2,128]{1,0:T(2,128)}, u32[]{:S(2)}) copy-start(f32[2,128]{1,0:T(2,128)} %gain.1) | copy-start | bytes 3076
  4.0 17.1 %copy-start.8 = (f32[2,128]{1,0:T(2,128)S(1)}, f32[2,128]{1,0:T(2,128)}, u32[]{:S(2)}) copy-start(f32[2,128]{1,0:T(2,128)} %bias_e.1) | copy-start | bytes 3076
  4.0 18.1 %collective-permute-start = (bf16[272,128]{1,0:T(8,128)(2,1)}, bf16[272,128]{1,0:T(8,128)(2,1)S(1)}, u32[]{:S(2)}, u32[]{:S(2)}) collective-permute-start(bf16[272,128]{1,0:T(8,128)(2,1)} %get-tuple-element.36), channel_id=1, source_target_pairs={{4,8},{12,16},{20,24},{28,32},{36,40},{44,48},{52,56},{60,64},{68,... | collective-permute-start | bytes 208904 | tf_op jit(solution)/shard_map/ppermute | solution.py:642
  9.1 13.1 %copy-start = (bf16[1,256,128]{2,1,0:T(8,128)(2,1)S(1)}, bf16[1,256,128]{2,1,0:T(8,128)(2,1)}, u32[]{:S(2)}) copy-start(bf16[1,256,128]{2,1,0:T(8,128)(2,1)} %refs_0_.1) | copy-start | bytes 196612
  9.1 13.1 %copy-start.1 = (bf16[1,256,128]{2,1,0:T(8,128)(2,1)S(1)}, bf16[1,256,128]{2,1,0:T(8,128)(2,1)}, u32[]{:S(2)}) copy-start(bf16[1,256,128]{2,1,0:T(8,128)(2,1)} %refs_1_.1) | copy-start | bytes 196612
  9.1 13.1 %copy-start.2 = (bf16[2,260,128]{2,0,1:T(2,128)(2,1)S(1)}, bf16[2,260,128]{2,0,1:T(2,128)(2,1)}, u32[]{:S(2)}) copy-start(bf16[2,260,128]{2,0,1:T(2,128)(2,1)} %param.19) | copy-start | bytes 399364
  9.1 13.1 %copy-start.3 = (bf16[2,256,128]{2,1,0:T(8,128)(2,1)S(1)}, bf16[2,256,128]{2,1,0:T(8,128)(2,1)}, u32[]{:S(2)}) copy-start(bf16[2,256,128]{2,1,0:T(8,128)(2,1)} %refs_12_.1) | copy-start | bytes 393220
  9.1 13.1 %copy-start.4 = (bf16[2,128,128]{2,1,0:T(8,128)(2,1)S(1)}, bf16[2,128,128]{2,1,0:T(8,128)(2,1)}, u32[]{:S(2)}) copy-start(bf16[2,128,128]{2,1,0:T(8,128)(2,1)} %refs_11_.1) | copy-start | bytes 196612
  9.1 13.1 %copy-start.5 = (bf16[2,128,128]{2,1,0:T(8,128)(2,1)S(1)}, bf16[2,128,128]{2,1,0:T(8,128)(2,1)}, u32[]{:S(2)}) copy-start(bf16[2,128,128]{2,1,0:T(8,128)(2,1)} %refs_14_.1) | copy-start | bytes 196612
  9.1 13.0 %collective-permute-start.1 = (bf16[272,128]{1,0:T(8,128)(2,1)}, bf16[272,128]{1,0:T(8,128)(2,1)S(1)}, u32[]{:S(2)}, u32[]{:S(2)}) collective-permute-start(bf16[272,128]{1,0:T(8,128)(2,1)} %get-tuple-element.37), channel_id=1, source_target_pairs={{0,4},{8,12},{16,20},{24,28},{32,36},{40,44},{48,52},{56,60},{64,6... | collective-permute-start | bytes 208904 | tf_op jit(solution)/shard_map/ppermute | solution.py:643
  66.1 6.8 %collective-permute-start.2 = (bf16[56,128]{1,0:T(8,128)(2,1)S(1)}, bf16[56,128]{1,0:T(8,128)(2,1)S(1)}, u32[]{:S(2)}, u32[]{:S(2)}) collective-permute-start(bf16[56,128]{1,0:T(8,128)(2,1)S(1)} %fold.4), channel_id=1, source_target_pairs={{0,4},{4,0},{1,5},{5,1},{2,6},{6,2},{3,7},{7,3},{8,12},{12,8},{9,1... | collective-permute-start | bytes 43016 | tf_op jit(solution)/shard_map/ppermute | solution.py:703
